TPU v7x, 32 devices: a whole 2x2x4 slice. The times are simulated.
32 devices in a mesh: wide: 8 (over y, x, core), narrow: 4 (over z).
Axes of the slice: x: 2, y: 2, z: 4, core: 2. Of those that a mesh axis runs over, the one named last changes fastest.
Arguments:
- layer_input: bfloat16 [4, 1024, 2048], P('narrow', 'wide'), may hold values from -6 to 6
- output_grad: bfloat16 [4, 1024, 2048], P('narrow', 'wide'), may hold values from -6 to 6
- doc_ids: int32 [4, 1024], P('narrow'), may hold values from 0 to 2, as said below
- keep_mask: int32 [4, 1024], P('narrow'), may hold values from 0 to 1, as said below
- attention_gain: bfloat16 [2048], P(('wide', 'narrow')), may hold values from 0.099609375 to 1.8984375
- query_weight: bfloat16 [2048, 2048], P(('wide', 'narrow')), may hold values from -0.125 to 0.125
- key_weight: bfloat16 [2048, 512], P(('wide', 'narrow')), may hold values from -0.125 to 0.125
- value_weight: bfloat16 [2048, 512], P(('wide', 'narrow')), may hold values from -0.125 to 0.125
- out_weight: bfloat16 [2048, 2048], P(('wide', 'narrow')), may hold values from -2 to 2
- feedforward_gain: bfloat16 [2048], P(('wide', 'narrow')), may hold values from 0.099609375 to 1.8984375
- gate_weight: bfloat16 [2048, 8192], P(('wide', 'narrow')), may hold values from -0.125 to 0.125
- up_weight: bfloat16 [2048, 8192], P(('wide', 'narrow')), may hold values from -0.125 to 0.125
- down_weight: bfloat16 [8192, 2048], P(('wide', 'narrow')), may hold values from -0.0625 to 0.0625
Outputs:
- layer_output: bfloat16 [4, 1024, 2048], P('narrow', 'wide')
- input_grad: bfloat16 [4, 1024, 2048], P('narrow', 'wide')
- attention_gain_grad: float32 [2048], P(('wide', 'narrow'))
- query_grad: float32 [2048, 2048], P(('wide', 'narrow'))
- key_grad: float32 [2048, 512], P(('wide', 'narrow'))
- value_grad: float32 [2048, 512], P(('wide', 'narrow'))
- out_grad: float32 [2048, 2048], P(('wide', 'narrow'))
- feedforward_gain_grad: float32 [2048], P(('wide', 'narrow'))
- gate_grad: float32 [2048, 8192], P(('wide', 'narrow'))
- up_grad: float32 [2048, 8192], P(('wide', 'narrow'))
- down_grad: float32 [8192, 2048], P(('wide', 'narrow'))
Inputs may be any that keep to these rules, and one draw needn't show every extreme that they name: `doc_ids`: in every stream document numbers never fall; document 0 ends within the first 128 tokens, document 2 begins within the last 128 tokens, and every document has a token. `keep_mask`: in every stream the zeros are one run at its end, inside document 2, after at least one token of it that is 1.
All inputs are finite; a program needn't handle non-finite values.
Results may differ from a plain program's by a relative error of at most 0.015.
Values may be sent and summed in bfloat16 or wider, within the bound.
No kernel may reach another device: no remote copies, remote signals or barrier semaphores. Data moves between devices by JAX's collectives and lax.ppermute only.
A program may use at most 640 MiB of HBM per device.

v0:
```python
import jax
import jax.numpy as jnp
import numpy as np
from jax import lax
from jax.sharding import PartitionSpec as P

HEADS = 32
HEAD = 64
DOCS = 3


EPSILON = 1e-05
MASKED = -1e30


def inverse_rates(head_width):
    plain = 500000.0 ** (-(np.arange(0, head_width, 2) * 1.0) / head_width)
    wavelength = 2.0 * np.pi / plain
    smooth = (8192.0 / wavelength - 1.0) / 3.0
    blended = (1.0 - smooth) * plain / 32.0 + smooth * plain
    scaled = np.where(
        wavelength > 8192.0, plain / 32.0, np.where(wavelength < 2048.0, plain, blended)
    )
    return scaled.astype(np.float32)


def turn_tables(positions):
    rates = jnp.asarray(inverse_rates(HEAD))
    angles = positions.astype(jnp.float32)[..., None] * rates
    angles = jnp.concatenate([angles, angles], axis=-1)
    return (jnp.cos(angles), jnp.sin(angles))


def rotate(values, cosine, sine_table):
    half_width = values.shape[-1] // 2
    turned = jnp.concatenate([-values[..., half_width:], values[..., :half_width]], axis=-1)
    return values * cosine[..., None, :] + turned * sine_table[..., None, :]


def rotate_back(gradient, cosine, sine_table):
    half_width = gradient.shape[-1] // 2
    scaled = gradient * sine_table[..., None, :]
    back_part = jnp.concatenate([scaled[..., half_width:], -scaled[..., :half_width]], axis=-1)
    return gradient * cosine[..., None, :] + back_part


def stream_positions(documents):
    numbers = jnp.arange(DOCS, dtype=jnp.int32)
    starts = jnp.sum((documents[None, :] < numbers[:, None]).astype(jnp.int32), axis=1)
    own_start = jnp.sum(
        jnp.where(documents[:, None] == numbers[None, :], starts[None, :], 0), axis=1
    )
    return jnp.arange(documents.shape[0], dtype=jnp.int32) - own_start


def normalize(values):
    factor = lax.rsqrt(jnp.mean(values * values, axis=-1, keepdims=True) + EPSILON)
    return (values * factor, factor)


def contract_rows(left_side, right_side):
    return lax.dot_general(
        left_side, right_side, (((0,), (0,)), ((), ())), preferred_element_type=jnp.float32
    )


def contract_cols(left_side, right_side):
    return lax.dot_general(
        left_side, right_side, (((1,), (1,)), ((), ())), preferred_element_type=jnp.float32
    )


def per_device(
    layer_input,
    output_grad,
    doc_ids,
    keep_mask,
    attention_gain,
    query_weight,
    key_weight,
    value_weight,
    out_weight,
    feedforward_gain,
    gate_weight,
    up_weight,
    down_weight,
):
    token_count = layer_input.shape[1]
    model_width = layer_input.shape[2]
    key_width = key_weight.shape[1]
    key_heads = key_width // HEAD
    group_size = HEADS // key_heads
    score_scale = HEAD ** (-0.5)
    documents = doc_ids[0]
    keep_flags = keep_mask[0]
    length = documents.shape[0]
    block_size = min(512, length)
    first_row = lax.axis_index("wide") * token_count
    cosine, sine_table = turn_tables(
        lax.dynamic_slice_in_dim(stream_positions(documents), first_row, token_count)
    )
    own_docs = lax.dynamic_slice_in_dim(documents, first_row, token_count)
    own_places = first_row + jnp.arange(token_count, dtype=jnp.int32)
    blocks_needed = (first_row + token_count + block_size - 1) // block_size
    residual = layer_input[0].astype(jnp.float32)
    attention_full = (
        lax.all_gather(query_weight, ("wide", "narrow"), axis=0, tiled=True),
        lax.all_gather(key_weight, ("wide", "narrow"), axis=0, tiled=True),
        lax.all_gather(value_weight, ("wide", "narrow"), axis=0, tiled=True),
        lax.all_gather(out_weight, ("wide", "narrow"), axis=0, tiled=True),
        lax.all_gather(attention_gain, ("wide", "narrow"), axis=0, tiled=True),
        lax.all_gather(feedforward_gain, ("wide", "narrow"), axis=0, tiled=True),
    )
    query_full, key_full, value_full, out_full, gain_one, gain_two = attention_full
    scaled_one, factor_one = normalize(residual)
    normed_one = (scaled_one * gain_one.astype(jnp.float32)).astype(jnp.bfloat16)
    query_lin = jnp.dot(normed_one, query_full, preferred_element_type=jnp.float32).reshape(
        token_count, HEADS, HEAD
    )
    key_lin = jnp.dot(normed_one, key_full, preferred_element_type=jnp.float32).reshape(
        token_count, key_heads, HEAD
    )
    value_lin = jnp.dot(normed_one, value_full, preferred_element_type=jnp.float32)
    queries = (
        rotate(query_lin, cosine, sine_table)
        .astype(jnp.bfloat16)
        .reshape(token_count, key_heads, group_size, HEAD)
    )
    own_keys = (
        rotate(key_lin, cosine, sine_table).astype(jnp.bfloat16).reshape(token_count, key_width)
    )
    own_values = value_lin.astype(jnp.bfloat16)
    all_keys, all_values = (
        lax.all_gather(own_keys, "wide", axis=0, tiled=True),
        lax.all_gather(own_values, "wide", axis=0, tiled=True),
    )

    def block_scores(block_index):
        key_start = block_index * block_size
        key_block = lax.dynamic_slice_in_dim(all_keys, key_start, block_size, 0).reshape(
            block_size, key_heads, HEAD
        )
        raw_scores = (
            jnp.einsum("tkgd,skd->kgts", queries, key_block, preferred_element_type=jnp.float32)
            * score_scale
        )
        key_docs = lax.dynamic_slice_in_dim(documents, key_start, block_size)
        key_keep = lax.dynamic_slice_in_dim(keep_flags, key_start, block_size)
        key_places = key_start + jnp.arange(block_size, dtype=jnp.int32)
        allowed = (
            (own_docs[:, None] == key_docs[None, :])
            & (key_places[None, :] <= own_places[:, None])
            & (key_keep[None, :] > 0)
        )
        return (jnp.where(allowed, raw_scores, MASKED), allowed, key_block)

    def value_block(block_index):
        return lax.dynamic_slice_in_dim(
            all_values, block_index * block_size, block_size, 0
        ).reshape(block_size, key_heads, HEAD)

    def gather_stats(block_index, state_pair):
        row_top, row_total = state_pair
        scores, allowed, key_block = block_scores(block_index)
        new_top = jnp.maximum(row_top, jnp.max(scores, axis=-1))
        kept_terms = jnp.where(allowed, jnp.exp(scores - new_top[..., None]), 0.0)
        return (new_top, row_total * jnp.exp(row_top - new_top) + jnp.sum(kept_terms, axis=-1))

    stat_shape = (key_heads, group_size, token_count)
    row_top, row_total = lax.fori_loop(
        0,
        blocks_needed,
        gather_stats,
        (jnp.full(stat_shape, MASKED, jnp.float32), jnp.zeros(stat_shape, jnp.float32)),
    )

    def softmax_block(block_index):
        scores, allowed, key_block = block_scores(block_index)
        return (jnp.exp(scores - row_top[..., None]) / row_total[..., None], key_block)

    def mix_block(block_index, summed):
        weights, key_block = softmax_block(block_index)
        return summed + jnp.einsum(
            "kgts,skd->tkgd",
            weights.astype(jnp.bfloat16),
            value_block(block_index),
            preferred_element_type=jnp.float32,
        )

    attended = lax.fori_loop(
        0,
        blocks_needed,
        mix_block,
        jnp.zeros((token_count, key_heads, group_size, HEAD), jnp.float32),
    )
    mixed = attended.reshape(token_count, model_width).astype(jnp.bfloat16)
    after_attention = residual + jnp.dot(mixed, out_full, preferred_element_type=jnp.float32)
    scaled_two, factor_two = normalize(after_attention)
    normed_two = (scaled_two * gain_two.astype(jnp.float32)).astype(jnp.bfloat16)
    grad_rows = output_grad[0].astype(jnp.float32)
    grad_branch = output_grad[0]
    hidden_units = gate_weight.shape[1]
    gate_full, upward_full, down_full = (
        lax.all_gather(gate_weight, ("wide", "narrow"), axis=0, tiled=True),
        lax.all_gather(up_weight, ("wide", "narrow"), axis=0, tiled=True),
        lax.all_gather(down_weight, ("wide", "narrow"), axis=0, tiled=True),
    )
    gate_lin = jnp.dot(normed_two, gate_full, preferred_element_type=jnp.float32)
    upward = jnp.dot(normed_two, upward_full, preferred_element_type=jnp.float32)
    sigmoid_gate = jax.nn.sigmoid(gate_lin)
    activated = gate_lin * sigmoid_gate
    hidden = (activated * upward).astype(jnp.bfloat16)
    layer_output = after_attention + jnp.dot(hidden, down_full, preferred_element_type=jnp.float32)
    grad_hidden = contract_cols(grad_branch, down_full)
    slope = sigmoid_gate * (1.0 + gate_lin * (1.0 - sigmoid_gate))
    grad_gate = (grad_hidden * upward * slope).astype(jnp.bfloat16)
    grad_upward = (grad_hidden * activated).astype(jnp.bfloat16)
    paired = jnp.concatenate([grad_gate, grad_upward], axis=1)
    projection_sums = lax.psum_scatter(
        contract_rows(normed_two, paired), ("wide", "narrow"), scatter_dimension=0, tiled=True
    )
    gate_grad = projection_sums[:, :hidden_units]
    up_grad = projection_sums[:, hidden_units:]
    down_grad = lax.psum_scatter(
        contract_rows(hidden, grad_branch), ("wide", "narrow"), scatter_dimension=0, tiled=True
    )
    grad_two = contract_cols(grad_gate, gate_full) + contract_cols(grad_upward, upward_full)
    forward_gain_term = jnp.sum(grad_two * scaled_two, axis=0)
    grad_scaled_two = grad_two * gain_two.astype(jnp.float32)
    grad_middle = grad_rows + factor_two * (
        grad_scaled_two
        - scaled_two * jnp.mean(grad_scaled_two * scaled_two, axis=-1, keepdims=True)
    )
    grad_attention = grad_middle.astype(jnp.bfloat16)
    grad_mixed = contract_cols(grad_attention, out_full).astype(jnp.bfloat16)
    out_term = contract_rows(mixed, grad_attention)
    grad_grouped = grad_mixed.reshape(token_count, key_heads, group_size, HEAD)
    row_delta = jnp.sum(grad_grouped.astype(jnp.float32) * attended, axis=-1).transpose(1, 2, 0)

    def back_block(block_index, state_triple):
        grad_queries, grad_keys, grad_values = state_triple
        weights, key_block = softmax_block(block_index)
        key_start = block_index * block_size
        weights_low = weights.astype(jnp.bfloat16)
        grad_value_block = jnp.einsum(
            "kgts,tkgd->skd", weights_low, grad_grouped, preferred_element_type=jnp.float32
        ).reshape(block_size, key_width)
        grad_weights = jnp.einsum(
            "tkgd,skd->kgts",
            grad_grouped,
            value_block(block_index),
            preferred_element_type=jnp.float32,
        )
        grad_scores = (weights * (grad_weights - row_delta[..., None])).astype(jnp.bfloat16)
        grad_queries = (
            grad_queries
            + jnp.einsum(
                "kgts,skd->tkgd", grad_scores, key_block, preferred_element_type=jnp.float32
            )
            * score_scale
        )
        grad_key_block = (
            jnp.einsum("kgts,tkgd->skd", grad_scores, queries, preferred_element_type=jnp.float32)
            * score_scale
        ).reshape(block_size, key_width)
        grad_keys = lax.dynamic_update_slice_in_dim(
            grad_keys,
            lax.dynamic_slice_in_dim(grad_keys, key_start, block_size, 0) + grad_key_block,
            key_start,
            0,
        )
        grad_values = lax.dynamic_update_slice_in_dim(
            grad_values,
            lax.dynamic_slice_in_dim(grad_values, key_start, block_size, 0) + grad_value_block,
            key_start,
            0,
        )
        return (grad_queries, grad_keys, grad_values)

    grad_queries, grad_keys, grad_values = lax.fori_loop(
        0,
        blocks_needed,
        back_block,
        (
            jnp.zeros((token_count, key_heads, group_size, HEAD), jnp.float32),
            jnp.zeros((length, key_width), jnp.float32),
            jnp.zeros((length, key_width), jnp.float32),
        ),
    )
    own_grad_keys, own_grad_values = (
        lax.psum_scatter(
            grad_keys.astype(jnp.bfloat16), "wide", scatter_dimension=0, tiled=True
        ).astype(jnp.float32),
        lax.psum_scatter(
            grad_values.astype(jnp.bfloat16), "wide", scatter_dimension=0, tiled=True
        ).astype(jnp.float32),
    )
    grad_query_lin = rotate_back(grad_queries.reshape(token_count, HEADS, HEAD), cosine, sine_table)
    grad_query_lin = grad_query_lin.reshape(token_count, model_width).astype(jnp.bfloat16)
    grad_key_lin = rotate_back(
        own_grad_keys.reshape(token_count, key_heads, HEAD), cosine, sine_table
    )
    grad_key_lin = grad_key_lin.reshape(token_count, key_width).astype(jnp.bfloat16)
    grad_value_lin = own_grad_values.astype(jnp.bfloat16)
    grad_one = (
        contract_cols(grad_query_lin, query_full)
        + contract_cols(grad_key_lin, key_full)
        + contract_cols(grad_value_lin, value_full)
    )
    attention_gain_term = jnp.sum(grad_one * scaled_one, axis=0)
    grad_scaled_one = grad_one * gain_one.astype(jnp.float32)
    input_grad = grad_middle + factor_one * (
        grad_scaled_one
        - scaled_one * jnp.mean(grad_scaled_one * scaled_one, axis=-1, keepdims=True)
    )
    reduced = (
        lax.psum_scatter(
            contract_rows(normed_one, grad_query_lin),
            ("wide", "narrow"),
            scatter_dimension=0,
            tiled=True,
        ),
        lax.psum_scatter(
            contract_rows(normed_one, grad_key_lin),
            ("wide", "narrow"),
            scatter_dimension=0,
            tiled=True,
        ),
        lax.psum_scatter(
            contract_rows(normed_one, grad_value_lin),
            ("wide", "narrow"),
            scatter_dimension=0,
            tiled=True,
        ),
        lax.psum_scatter(out_term, ("wide", "narrow"), scatter_dimension=0, tiled=True),
        lax.psum_scatter(attention_gain_term, ("wide", "narrow"), scatter_dimension=0, tiled=True),
        lax.psum_scatter(forward_gain_term, ("wide", "narrow"), scatter_dimension=0, tiled=True),
    )
    return (
        layer_output[None].astype(jnp.bfloat16),
        input_grad[None].astype(jnp.bfloat16),
        reduced[4],
        reduced[0],
        reduced[1],
        reduced[2],
        reduced[3],
        reduced[5],
        gate_grad,
        up_grad,
        down_grad,
    )


def solution(mesh):
    placed = (
        P("narrow", "wide", None),
        P("narrow", "wide", None),
        P("narrow", None),
        P("narrow", None),
        P(("wide", "narrow")),
        P(("wide", "narrow"), None),
        P(("wide", "narrow"), None),
        P(("wide", "narrow"), None),
        P(("wide", "narrow"), None),
        P(("wide", "narrow")),
        P(("wide", "narrow"), None),
        P(("wide", "narrow"), None),
        P(("wide", "narrow"), None),
    )
    return jax.shard_map(
        per_device,
        mesh=mesh,
        in_specs=placed,
        out_specs=(
            P("narrow", "wide", None),
            P("narrow", "wide", None),
            P(("wide", "narrow")),
            P(("wide", "narrow"), None),
            P(("wide", "narrow"), None),
            P(("wide", "narrow"), None),
            P(("wide", "narrow"), None),
            P(("wide", "narrow")),
            P(("wide", "narrow"), None),
            P(("wide", "narrow"), None),
            P(("wide", "narrow"), None),
        ),
        check_vma=False,
    )
```

profile of v0, /device:TPU:0, one launch (start us, length us, event | category | flops | bytes accessed | tf_op | source)
XLA Modules:
  0.0 5428.8 jit_solution(3475475778382927909)
XLA Ops:
  10.4 42.1 all-reduce.6
  52.5 1.2 fusion.53
  53.8 16.4 all-gather.10.cloned.1.call-done
  70.2 2.9 convolution_convert_fusion.1
  76.2 52.2 all-gather.14.cloned.1.call-done
  128.5 2.9 copy.58
  135.9 17.4 all-gather.12.cloned.1.call-done
  153.3 1.5 copy.60
  154.8 78.7 %all-gather.18.cloned.1.call-done = bf16[2048,2048]{1,0:T(8,128)(2,1)} async-done(((bf16[64,2048]{1,0:T(8,128)(2,1)}), bf16[2048,2048]{1,0:T(8,128)(2,1)}) %all-gather.18.cloned.1.call-update) | async-done | bytes 8388624 | tf_op jit(solution)/shard_map/all_gather | solution.py:107
  233.5 12.3 copy.59
  245.8 5.9 fusion.66
  252.0 6.0 all-gather.16.cloned.1.call-done
  258.0 5.1 while.39
  259.6 1.3 fusion.167
  260.9 2.1 select_reduce_fusion.3
  264.2 7.1 while.40
  266.2 5.1 fusion.172
  271.3 2.5 convert_element_type.135
  273.8 64.5 %all-gather.20.cloned.1.call-done = bf16[2048,2048]{1,0:T(8,128)(2,1)} async-done(((bf16[64,2048]{1,0:T(8,128)(2,1)}), bf16[2048,2048]{1,0:T(8,128)(2,1)}) %all-gather.20.cloned.1.call-update) | async-done | bytes 8388624 | tf_op jit(solution)/shard_map/all_gather | solution.py:110
  338.2 4.9 multiply_reduce_fusion.3
  343.4 191.2 %all-gather.22.cloned.1.call-done = bf16[2048,8192]{1,0:T(8,128)(2,1)} async-done(((bf16[64,8192]{1,0:T(8,128)(2,1)}), bf16[2048,8192]{1,0:T(8,128)(2,1)}) %all-gather.22.cloned.1.call-update) | async-done | bytes 33554448 | tf_op jit(solution)/shard_map/all_gather | solution.py:204
  534.6 17.8 fusion.92
  552.3 178.2 %all-gather.24.cloned.1.call-done = bf16[2048,8192]{1,0:T(8,128)(2,1)} async-done(((bf16[64,8192]{1,0:T(8,128)(2,1)}), bf16[2048,8192]{1,0:T(8,128)(2,1)}) %all-gather.24.cloned.1.call-update) | async-done | bytes 33554448 | tf_op jit(solution)/shard_map/all_gather | solution.py:205
  730.5 17.8 fusion.93
  748.3 178.1 %all-gather.26.cloned.1.call-done = bf16[8192,2048]{1,0:T(8,128)(2,1)} async-done(((bf16[256,2048]{1,0:T(8,128)(2,1)}), bf16[8192,2048]{1,0:T(8,128)(2,1)}) %all-gather.26.cloned.1.call-update) | async-done | bytes 33554448 | tf_op jit(solution)/shard_map/all_gather | solution.py:206
  926.4 21.0 multiply_convert_fusion
  947.4 16.3 fusion.94
  963.7 17.2 multiply_reduce_fusion
  981.2 7.4 convolution_convert_fusion
  988.7 1.4 copy.61
  990.1 1.4 multiply_reduce_fusion.1
  991.6 1.6 broadcast.172
  993.2 1.6 broadcast.172.clone
  994.8 11.9 while.41
  995.4 2.5 fusion.183
  997.9 1.4 fusion.184
  1000.1 1.4 fusion.186
  1001.5 1.4 fusion.187
  1004.4 1.4 copy-done.4
  1006.8 1.7 convert_element_type.149
  1008.5 1.3 copy.74
  1009.9 1.8 convert_element_type.152
  1011.7 1.3 copy.76
  1013.1 46.5 fusion.33
  1061.1 2.8 fusion.86
  1064.0 31.0 reduce-scatter.24.cloned.1.call-done
  1095.0 3.6 fusion.84
  1098.9 1.2 fusion.60
  1100.1 9.4 fusion.70
  1109.6 1.1 copy-done.12
  1110.9 8.3 fusion.75
  1120.2 25.8 fusion.62
  1146.1 1.4 fusion.58
  1147.5 6.8 fusion.95
  1154.3 15.9 fusion.39
  1172.8 41.3 all-reduce.5
  1215.3 1.2 fusion.61
  1216.4 1763.6 %all-reduce.9.cloned.1.call-done = f32[2048,16384]{1,0:T(8,128)} async-done(((f32[2048,16384]{1,0:T(8,128)}), f32[2048,16384]{1,0:T(8,128)}) %all-reduce.9.cloned.1.call-update) | async-done | bytes 134217744
  2980.1 4.9 fusion.89
  2985.0 145.4 %reduce-scatter.14.cloned.1.call-done = f32[64,512]{1,0:T(8,128)} async-done(((f32[2048,512]{1,0:T(8,128)}), f32[64,512]{1,0:T(8,128)}) %reduce-scatter.14.cloned.1.call-update) | async-done | bytes 131088 | tf_op jit(solution)/shard_map/reduce_scatter | solution.py:323
  3130.4 149.7 %reduce-scatter.16.cloned.1.call-done = f32[64,512]{1,0:T(8,128)} async-done(((f32[2048,512]{1,0:T(8,128)}), f32[64,512]{1,0:T(8,128)}) %reduce-scatter.16.cloned.1.call-update) | async-done | bytes 131088 | tf_op jit(solution)/shard_map/reduce_scatter | solution.py:329
  3280.1 365.7 %reduce-scatter.12.cloned.1.call-done = f32[64,2048]{1,0:T(8,128)} async-done(((f32[2048,2048]{1,0:T(8,128)}), f32[64,2048]{1,0:T(8,128)}) %reduce-scatter.12.cloned.1.call-update) | async-done | bytes 524304 | tf_op jit(solution)/shard_map/reduce_scatter | solution.py:317
  3645.8 364.9 %reduce-scatter.18.cloned.1.call-done = f32[64,2048]{1,0:T(8,128)} async-done(((f32[2048,2048]{1,0:T(8,128)}), f32[64,2048]{1,0:T(8,128)}) %reduce-scatter.18.cloned.1.call-update) | async-done | bytes 524304 | tf_op jit(solution)/shard_map/reduce_scatter | solution.py:335
  4010.7 1411.4 %reduce-scatter.20.cloned.1.call-done = f32[256,2048]{1,0:T(8,128)} async-done(((f32[8192,2048]{1,0:T(8,128)}), f32[256,2048]{1,0:T(8,128)}) %reduce-scatter.20.cloned.1.call-update) | async-done | bytes 2097168 | tf_op jit(solution)/shard_map/reduce_scatter | solution.py:224
  (162 shorter events, 26.0 us)
Async XLA Ops:
  7.2 124.2 %copy-start.1 = (bf16[1,128,2048]{2,1,0:T(8,128)(2,1)S(1)}, bf16[1,128,2048]{2,1,0:T(8,128)(2,1)}, u32[]{:S(2)}) copy-start(bf16[1,128,2048]{2,1,0:T(8,128)(2,1)} %param.20) | copy-start | bytes 1572868
  7.2 63.0 %all-gather.10.cloned.1.call-start = ((), (), s32[]{:S(2)}) async-start(), calls=%async_computation.7 | async-start | bytes 2162688 | tf_op jit(solution)/shard_map/all_gather | solution.py:109
  7.9 120.5 %all-gather.14.cloned.1.call-start = ((), (), s32[]{:S(2)}) async-start(), calls=%async_computation.9 | async-start | bytes 2162688 | tf_op jit(solution)/shard_map/all_gather | solution.py:108
  8.7 144.6 %all-gather.12.cloned.1.call-start = ((), (), s32[]{:S(2)}) async-start(), calls=%async_computation.8 | async-start | bytes 1179648 | tf_op jit(solution)/shard_map/all_gather | solution.py:135
  52.5 193.3 %copy-start.25 = (f32[2048]{0:T(1024)}, f32[2048]{0:T(1024)S(1)}, u32[]{:S(2)}) copy-start(f32[2048]{0:T(1024)S(1)} %convert_element_type.125) | copy-start | bytes 24580
  53.8 192.1 %copy-start.31 = (f32[128]{0:T(128)}, f32[128]{0:T(128)S(1)}, u32[]{:S(2)}) copy-start(f32[128]{0:T(128)S(1)} %add_rsqrt_fusion.1) | copy-start | bytes 1540
  73.1 160.4 %all-gather.18.cloned.1.call-start = ((), (), s32[]{:S(2)}) async-start(), calls=%async_computation.11 | async-start | bytes 8650752 | tf_op jit(solution)/shard_map/all_gather | solution.py:107
  73.7 184.3 %all-gather.16.cloned.1.call-start = ((), (), s32[]{:S(2)}) async-start(), calls=%async_computation.10 | async-start | bytes 1179648 | tf_op jit(solution)/shard_map/all_gather | solution.py:134
  76.2 175.6 %copy-start.21 = (f32[128,64]{0,1:T(8,128)}, f32[128,64]{0,1:T(8,128)S(1)}, u32[]{:S(2)}) copy-start(f32[128,64]{0,1:T(8,128)S(1)} %get-tuple-element.524) | copy-start | bytes 98308
  76.2 175.6 %copy-start.23 = (f32[128,64]{0,1:T(8,128)}, f32[128,64]{0,1:T(8,128)S(1)}, u32[]{:S(2)}) copy-start(f32[128,64]{0,1:T(8,128)S(1)} %get-tuple-element.525) | copy-start | bytes 98308
  131.4 4.4 copy-start.28
  133.0 205.3 %all-gather.20.cloned.1.call-start = ((), (), s32[]{:S(2)}) async-start(), calls=%async_computation.12 | async-start | bytes 8650752 | tf_op jit(solution)/shard_map/all_gather | solution.py:110
  133.5 401.0 %all-gather.22.cloned.1.call-start = ((), (), s32[]{:S(2)}) async-start(), calls=%async_computation.13 | async-start | bytes 34603008 | tf_op jit(solution)/shard_map/all_gather | solution.py:204
  134.3 596.2 %all-gather.24.cloned.1.call-start = ((), (), s32[]{:S(2)}) async-start(), calls=%async_computation.14 | async-start | bytes 34603008 | tf_op jit(solution)/shard_map/all_gather | solution.py:205
  135.0 791.4 %all-gather.26.cloned.1.call-start = ((), (), s32[]{:S(2)}) async-start(), calls=%async_computation.15 | async-start | bytes 34603008 | tf_op jit(solution)/shard_map/all_gather | solution.py:206
  135.8 924.0 %reduce-scatter.22.cloned.1.call-start = ((), (), s32[]{:S(2)}) async-start(), calls=%async_computation.21 | async-start | bytes 1179648
  251.7 6.3 copy-start.29
  271.3 71.9 %copy-start.7 = (bf16[1024,512]{0,1:T(8,128)(2,1)}, bf16[1024,512]{0,1:T(8,128)(2,1)S(1)}, u32[]{:S(2)}) copy-start(bf16[1024,512]{0,1:T(8,128)(2,1)S(1)} %get-tuple-element.956) | copy-start | bytes 3145732
  343.2 637.7 %copy-start.9 = (f32[128,2048]{1,0:T(8,128)}, f32[128,2048]{1,0:T(8,128)S(1)}, u32[]{:S(2)}) copy-start(f32[128,2048]{1,0:T(8,128)S(1)} %get-tuple-element.527) | copy-start | bytes 3145732
  343.4 387.1 %copy-start.14 = (bf16[128,2048]{1,0:T(8,128)(2,1)}, bf16[128,2048]{1,0:T(8,128)(2,1)S(1)}, u32[]{:S(2)}) copy-start(bf16[128,2048]{1,0:T(8,128)(2,1)S(1)} %multiply_convert_fusion.3) | copy-start | bytes 1572868
  552.3 374.1 %copy-start.18 = (bf16[1,128,2048]{2,1,0:T(8,128)(2,1)S(1)}, bf16[1,128,2048]{2,1,0:T(8,128)(2,1)}, u32[]{:S(2)}) copy-start(bf16[1,128,2048]{2,1,0:T(8,128)(2,1)} %param.21) | copy-start | bytes 1572868
  981.2 7.4 copy-start.11
  988.7 6.2 copy-start
  995.3 2.5 copy-start.8
  1001.5 1.6 copy-start.3
  1001.5 2.2 copy-start.5
  1004.4 1.4 copy-start.4
  1004.4 2.0 copy-start.6
  1009.8 3.3 copy-start.15
  1009.9 85.1 %reduce-scatter.24.cloned.1.call-start = ((), (), s32[]{:S(2)}) async-start(), calls=%async_computation.22 | async-start | bytes 1179648
  1013.1 1967.0 %all-reduce.9.cloned.1.call-start = ((), (), s32[]{:S(2)}) async-start(), calls=%async_computation.23 | async-start | bytes 268435456
  1059.7 1.2 copy-start.24
  1059.7 1.3 copy-start.22
  1059.7 1.4 copy-start.2
  1059.7 1.4 copy-start.26
  1059.7 1.4 copy-start.32
  1059.7 2070.7 %reduce-scatter.14.cloned.1.call-start = ((), (), s32[]{:S(2)}) async-start(), calls=%async_computation.17 | async-start | bytes 4325376 | tf_op jit(solution)/shard_map/reduce_scatter | solution.py:323
  1063.9 2216.2 %reduce-scatter.16.cloned.1.call-start = ((), (), s32[]{:S(2)}) async-start(), calls=%async_computation.18 | async-start | bytes 4325376 | tf_op jit(solution)/shard_map/reduce_scatter | solution.py:329
  1098.6 2547.2 %reduce-scatter.12.cloned.1.call-start = ((), (), s32[]{:S(2)}) async-start(), calls=%async_computation.16 | async-start | bytes 17301504 | tf_op jit(solution)/shard_map/reduce_scatter | solution.py:317
  1109.5 1.2 copy-start.12
  1109.5 1.4 copy-start.17
  1109.5 2901.2 %reduce-scatter.18.cloned.1.call-start = ((), (), s32[]{:S(2)}) async-start(), calls=%async_computation.19 | async-start | bytes 17301504 | tf_op jit(solution)/shard_map/reduce_scatter | solution.py:335
  1119.2 1.1 copy-start.19
  1119.2 4302.9 %reduce-scatter.20.cloned.1.call-start = ((), (), s32[]{:S(2)}) async-start(), calls=%async_computation.20 | async-start | bytes 69206016 | tf_op jit(solution)/shard_map/reduce_scatter | solution.py:224
  1147.5 6.8 copy-start.10
  1147.5 6.8 copy-start.13
  1154.3 15.9 copy-start.16
  1170.2 1.6 copy-start.20
  1170.2 1.6 copy-start.27
  1170.2 2.6 copy-start.30
Sparse Core Ops, SparseCore 0:
  11.0 59.1 all-gather.9
  73.1 55.3 all-gather.13
  130.9 22.3 all-gather.11
  156.1 77.3 all-gather.17
  235.8 22.1 all-gather.15
  260.8 77.4 all-gather.19
  341.2 193.3 all-gather.21
  537.5 192.9 all-gather.23
  733.4 192.9 all-gather.25
  1010.0 45.7 reduce-scatter.21
  1058.9 35.9 reduce-scatter.23
  1101.2 1878.7 all-reduce.8
  2982.9 147.4 reduce-scatter.13
  3133.1 146.9 reduce-scatter.15
  3282.8 362.9 reduce-scatter.11
  3648.6 362.1 reduce-scatter.17
  4013.5 1408.5 reduce-scatter.19
where the time goes:
time: 5440 us; the launch traced here: 5430 us
  waiting for transfers between devices  5020 us (92%)
  matrix products  247 us (5%)
  blocking collectives  83.4 us (2%)
    unnamed x20, waiting for transfers between devices  1800 us
    reduce_scatter x1, waiting for transfers between devices, per_device(): lax.psum_scatter(contract_rows(hidden, grad_branch), ('wide', 'narrow'),...  1410 us
    reduce_scatter x1, waiting for transfers between devices, per_device(): lax.psum_scatter(contract_rows(normed_one, grad_query_lin), ('wide', 'nar...  366 us
    reduce_scatter x1, waiting for transfers between devices, per_device(): lax.psum_scatter(out_term, ('wide', 'narrow'), scatter_dimension=0, tiled...  365 us
    all_gather x1, waiting for transfers between devices, per_device(): lax.all_gather(gate_weight, ('wide', 'narrow'), axis=0, tiled=True)  191 us
    all_gather x1, waiting for transfers between devices, per_device(): lax.all_gather(up_weight, ('wide', 'narrow'), axis=0, tiled=True)  178 us
    all_gather x1, waiting for transfers between devices, per_device(): lax.all_gather(down_weight, ('wide', 'narrow'), axis=0, tiled=True)  178 us
    reduce_scatter x1, waiting for transfers between devices, per_device(): lax.psum_scatter(contract_rows(normed_one, grad_value_lin), ('wide', 'nar...  150 us
  transfers between devices with their start and end apart: 17, of which 16 were waited for; matrix products, arithmetic and copies ran while one was open for 4% of the time, Pallas kernels for 0%

commit v1 on v0

v1 whole, which is shorter than its diff:
```python
import functools

import jax
import jax.numpy as jnp
import numpy as np
from jax import lax
from jax.experimental import pallas as pl
from jax.experimental.pallas import tpu as pltpu
from jax.sharding import PartitionSpec as P

HEADS = 32
HEAD = 64
DOCS = 3
EPSILON = 1e-05
MASKED = -1e30
INNER = 2
F32 = jnp.float32
BF16 = jnp.bfloat16


def inverse_rates(head_width):
    plain = 500000.0 ** (-(np.arange(0, head_width, 2) * 1.0) / head_width)
    wavelength = 2.0 * np.pi / plain
    smooth = (8192.0 / wavelength - 1.0) / 3.0
    blended = (1.0 - smooth) * plain / 32.0 + smooth * plain
    scaled = np.where(
        wavelength > 8192.0, plain / 32.0, np.where(wavelength < 2048.0, plain, blended)
    )
    return scaled.astype(np.float32)


def stream_positions(documents):
    numbers = jnp.arange(DOCS, dtype=jnp.int32)
    starts = jnp.sum((documents[None, :] < numbers[:, None]).astype(jnp.int32), axis=1)
    own_start = jnp.sum(
        jnp.where(documents[:, None] == numbers[None, :], starts[None, :], 0), axis=1
    )
    return jnp.arange(documents.shape[0], dtype=jnp.int32) - own_start


def normalize(values):
    factor = lax.rsqrt(jnp.mean(values * values, axis=-1, keepdims=True) + EPSILON)
    return values * factor, factor


def mm(left, right, dims):
    return lax.dot_general(left, right, (dims, ((), ())), preferred_element_type=F32)


def block_offset(place, block, outer, tokens):
    peer = place ^ block
    return pl.multiple_of(((peer % INNER) * outer + peer // INNER) * tokens, tokens)


def fill_bias(bias_ref, keydoc_ref, doc_ref, start, width, length):
    shape = (length, width)
    key_index = lax.broadcasted_iota(jnp.int32, shape, 0)
    query_index = lax.broadcasted_iota(jnp.int32, shape, 1) + start
    allowed = (keydoc_ref[0:length, :] == doc_ref[:, start : start + width]) & (
        key_index <= query_index
    )
    bias_ref[0:length, :] = jnp.where(allowed, 0.0, MASKED)


def attend_kernel(
    heads, tokens, outer, width,
    place_ref, lin_ref, cos_ref, sin_ref, keydoc_ref, doc_ref,
    mixed_ref, query_ref, key_ref, value_ref, lse_ref,
    key_rows, bias_ref,
):
    length = doc_ref.shape[1]
    key_heads = key_ref.shape[0]
    group = heads // key_heads
    half = HEAD // 2
    place = place_ref[0]
    for block in range(length // tokens):
        source = pl.ds(block_offset(place, block, outer, tokens), tokens)
        lanes = slice(block * tokens, (block + 1) * tokens)
        cosine, sine = cos_ref[:, lanes], sin_ref[:, lanes]
        for head in range(heads + key_heads):
            first = lin_ref[head, 0:half, source]
            second = lin_ref[head, half:HEAD, source]
            one = (first * cosine - second * sine).astype(BF16)
            two = (second * cosine + first * sine).astype(BF16)
            if head < heads:
                scale = jnp.asarray(HEAD ** (-0.5), BF16)
                query_ref[head, 0:half, lanes] = one * scale
                query_ref[head, half:HEAD, lanes] = two * scale
            else:
                key_ref[head - heads, 0:half, lanes] = one
                key_ref[head - heads, half:HEAD, lanes] = two
        for head in range(key_heads):
            value_ref[head, :, lanes] = lin_ref[heads + key_heads + head, :, source].astype(BF16)
    for kv in range(key_heads):
        key_rows[kv] = key_ref[kv].astype(F32).T.astype(BF16)
    for step in range(length // width):
        start = step * width
        reach = start + width
        fill_bias(bias_ref, keydoc_ref, doc_ref, start, width, reach)
        for kv in range(key_heads):

            def one_head(index, carry, kv=kv, start=start, reach=reach):
                head = kv * group + index
                query = query_ref[head, :, start:reach]
                scores = mm(key_rows[kv, 0:reach, :], query, ((1,), (0,))) + bias_ref[0:reach, :]
                top = jnp.max(scores, axis=0, keepdims=True)
                terms = jnp.exp(scores - top)
                total = jnp.sum(terms, axis=0, keepdims=True)
                probs = (terms * (1.0 / total)).astype(BF16)
                mixed = mm(value_ref[kv, :, 0:reach], probs, ((1,), (0,))).astype(BF16)
                for block in range(start // tokens, reach // tokens):
                    target = pl.ds(block_offset(place, block, outer, tokens), tokens)
                    lanes = slice(block * tokens - start, (block + 1) * tokens - start)
                    mixed_ref[head, :, target] = mixed[:, lanes]
                lse_ref[head, :, start:reach] = top + jnp.log(total)
                return carry

            lax.fori_loop(0, group, one_head, 0)


def attend_back_kernel(
    heads, tokens, outer, width,
    place_ref, grad_ref, query_ref, key_ref, value_ref, lse_ref, cos_ref, sin_ref,
    keydoc_ref, doc_ref,
    out_ref,
    key_rows, value_rows, key_grad, value_grad, grad_abs, bias_ref,
):
    length = doc_ref.shape[1]
    key_heads = key_ref.shape[0]
    group = heads // key_heads
    half = HEAD // 2
    scale = HEAD ** (-0.5)
    place = place_ref[0]

    def put_back(head, block, gradient):
        target = pl.ds(block_offset(place, block, outer, tokens), tokens)
        lanes = slice(block * tokens, (block + 1) * tokens)
        cosine, sine = cos_ref[:, lanes], sin_ref[:, lanes]
        one, two = gradient[0:half], gradient[half:HEAD]
        out_ref[head, 0:half, target] = (one * cosine + two * sine).astype(BF16)
        out_ref[head, half:HEAD, target] = (two * cosine - one * sine).astype(BF16)

    for block in range(length // tokens):
        source = pl.ds(block_offset(place, block, outer, tokens), tokens)
        lanes = slice(block * tokens, (block + 1) * tokens)
        for head in range(heads):
            grad_abs[head, :, lanes] = grad_ref[head, :, source]
    for kv in range(key_heads):
        key_rows[kv] = key_ref[kv].astype(F32).T.astype(BF16)
        value_rows[kv] = value_ref[kv].astype(F32).T.astype(BF16)
    key_grad[...] = jnp.zeros_like(key_grad)
    value_grad[...] = jnp.zeros_like(value_grad)
    for step in range(length // width):
        start = step * width
        reach = start + width
        fill_bias(bias_ref, keydoc_ref, doc_ref, start, width, reach)
        for kv in range(key_heads):

            def one_head(index, carry, kv=kv, start=start, reach=reach):
                head = kv * group + index
                query = query_ref[head, :, start:reach]
                grad = grad_abs[head, :, start:reach]
                query_rows = query.astype(F32).T.astype(BF16)
                grad_rows = grad.astype(F32).T.astype(BF16)
                scores = mm(key_rows[kv, 0:reach, :], query, ((1,), (0,))) + bias_ref[0:reach, :]
                probs = jnp.exp(scores - lse_ref[head, :, start:reach])
                grad_probs = mm(value_rows[kv, 0:reach, :], grad, ((1,), (0,)))
                delta = jnp.sum(probs * grad_probs, axis=0, keepdims=True)
                grad_scores = (probs * (grad_probs - delta)).astype(BF16)
                value_grad[kv, 0:reach, :] += mm(probs.astype(BF16), grad_rows, ((1,), (0,)))
                key_grad[kv, 0:reach, :] += mm(grad_scores, query_rows, ((1,), (0,)))
                grad_query = mm(key_ref[kv, :, 0:reach], grad_scores, ((1,), (0,))) * scale
                for block in range(start // tokens, reach // tokens):
                    lanes = slice(block * tokens - start, (block + 1) * tokens - start)
                    put_back(head, block, grad_query[:, lanes])
                return carry

            lax.fori_loop(0, group, one_head, 0)
    for block in range(length // tokens):
        lanes = slice(block * tokens, (block + 1) * tokens)
        target = pl.ds(block_offset(place, block, outer, tokens), tokens)
        for kv in range(key_heads):
            put_back(heads + kv, block, key_grad[kv, lanes, :].T)
            out_ref[heads + key_heads + kv, :, target] = value_grad[kv, lanes, :].T.astype(BF16)


def vmem_spec():
    return pl.BlockSpec(memory_space=pltpu.VMEM)


def attend(place, lin, cosine, sine, keydoc, doc, heads, tokens, outer):
    total, _, length = lin.shape
    key_heads = (total - heads) // 2
    width = min(256, length)
    shape = jax.ShapeDtypeStruct
    return pl.pallas_call(
        functools.partial(attend_kernel, heads, tokens, outer, width),
        out_shape=(
            shape((heads, HEAD, length), BF16),
            shape((heads, HEAD, length), BF16),
            shape((key_heads, HEAD, length), BF16),
            shape((key_heads, HEAD, length), BF16),
            shape((heads, 1, length), F32),
        ),
        in_specs=[pl.BlockSpec(memory_space=pltpu.SMEM)] + [vmem_spec()] * 5,
        out_specs=(vmem_spec(),) * 5,
        scratch_shapes=[
            pltpu.VMEM((key_heads, length, HEAD), BF16),
            pltpu.VMEM((length, width), F32),
        ],
        compiler_params=pltpu.CompilerParams(vmem_limit_bytes=40 * 2**20),
        cost_estimate=pl.CostEstimate(
            flops=4 * heads * length * length * HEAD,
            bytes_accessed=8 * total * HEAD * length,
            transcendentals=heads * length * length,
        ),
    )(place, lin, cosine, sine, keydoc, doc)


def attend_back(place, grad, query, key, value, lse, cosine, sine, keydoc, doc, tokens, outer):
    heads, _, length = query.shape
    key_heads = key.shape[0]
    width = min(256, length)
    total = heads + 2 * key_heads
    return pl.pallas_call(
        functools.partial(attend_back_kernel, heads, tokens, outer, width),
        out_shape=jax.ShapeDtypeStruct((total, HEAD, length), BF16),
        in_specs=[pl.BlockSpec(memory_space=pltpu.SMEM)] + [vmem_spec()] * 9,
        out_specs=vmem_spec(),
        scratch_shapes=[
            pltpu.VMEM((key_heads, length, HEAD), BF16),
            pltpu.VMEM((key_heads, length, HEAD), BF16),
            pltpu.VMEM((key_heads, length, HEAD), F32),
            pltpu.VMEM((key_heads, length, HEAD), F32),
            pltpu.VMEM((heads, HEAD, length), BF16),
            pltpu.VMEM((length, width), F32),
        ],
        compiler_params=pltpu.CompilerParams(vmem_limit_bytes=40 * 2**20),
        cost_estimate=pl.CostEstimate(
            flops=10 * heads * length * length * HEAD,
            bytes_accessed=8 * total * HEAD * length,
            transcendentals=heads * length * length,
        ),
    )(place, grad, query, key, value, lse, cosine, sine, keydoc, doc)


def exchange(value, axis, size, step):
    return lax.ppermute(value, axis, [(i, i ^ step) for i in range(size)])


def put(buffer, piece, index):
    return lax.dynamic_update_slice(
        buffer, piece, tuple(jnp.asarray(i, jnp.int32) for i in index)
    )


def pick(value, index, axis=0):
    return lax.dynamic_index_in_dim(value, index, axis, keepdims=False)


def make_program(wide, narrow):
    outer = wide // INNER

    def core_swap(value):
        return exchange(value, "wide", wide, 1)

    def outer_swap(value, step):
        return exchange(value, "wide", wide, INNER * step)

    def narrow_swap(value, step):
        return exchange(value, "narrow", narrow, step)

    def fan_out(value, swap, size):
        return [value] + [swap(value, step) for step in range(1, size)]

    def sum_scatter(parts, swap, size):
        arrived = [swap(parts[step].astype(BF16), step) for step in range(1, size)]
        total = parts[0].astype(F32)
        for piece in arrived:
            total = total + piece.astype(F32)
        return total

    def gather_near(value, swap, size):
        first = jnp.stack(fan_out(value, swap, size))
        return jnp.concatenate([first, core_swap(first)], axis=0).reshape(-1, value.shape[-1])

    def scatter_near(total, swap, size):
        split = total.reshape(INNER, size, -1, total.shape[-1])
        arrived = core_swap(split[1].astype(BF16))
        both = [split[0, step].astype(F32) + arrived[step].astype(F32) for step in range(size)]
        return sum_scatter(both, swap, size)

    def per_device(
        layer_input, output_grad, doc_ids, keep_mask, attention_gain, query_weight, key_weight,
        value_weight, out_weight, feedforward_gain, gate_weight, up_weight, down_weight,
    ):
        tokens = layer_input.shape[1]
        model = layer_input.shape[2]
        rows = query_weight.shape[0]
        down_rows = down_weight.shape[0]
        kv_total = key_weight.shape[1] // HEAD
        heads = HEADS // wide
        group = HEADS // kv_total
        key_heads = max(1, heads // group)
        repeat = max(1, group // heads)
        place = lax.axis_index("wide")
        core = place % INNER
        chip = place // INNER
        layer = lax.axis_index("narrow")
        place_arg = place.reshape(1).astype(jnp.int32)
        documents = doc_ids[0]
        positions = stream_positions(documents)
        angles = jnp.asarray(inverse_rates(HEAD))[:, None] * positions.astype(F32)[None, :]
        cosine, sine = jnp.cos(angles), jnp.sin(angles)
        keydoc = jnp.where(keep_mask[0] > 0, documents, -1)[:, None]
        doc = documents[None, :]

        head_cols = heads * HEAD
        kv_cols = key_heads * HEAD

        def kv_split(weight):
            parts = weight.reshape(rows, -1, kv_cols)
            return jnp.repeat(parts, repeat, axis=1)

        packed = jnp.concatenate(
            [query_weight.reshape(rows, wide, head_cols), kv_split(key_weight), kv_split(value_weight)],
            axis=2,
        )
        cols = packed.shape[2]
        packed = packed.reshape(rows, outer, INNER, cols).transpose(2, 1, 0, 3)
        mine = pick(packed, core)
        other = core_swap(pick(packed, 1 - core))
        pair = jnp.stack([mine, other], axis=1)
        blocks = [pick(pair, chip)] + [
            outer_swap(pick(pair, chip ^ step), step) for step in range(1, outer)
        ]
        by_wide = jnp.zeros((wide, 1, rows, cols), BF16)
        for step in range(outer):
            for near in range(INNER):
                by_wide = put(
                    by_wide, blocks[step][near][None, None], (place ^ (INNER * step + near), 0, 0, 0)
                )
        by_wide = by_wide.reshape(wide, rows, cols)
        attention_weight = jnp.zeros((wide, narrow, rows, cols), BF16)
        for step, piece in enumerate(fan_out(by_wide, narrow_swap, narrow)):
            attention_weight = put(attention_weight, piece[:, None], (0, layer ^ step, 0, 0))
        attention_weight = attention_weight.reshape(model, cols)

        out_own = jnp.zeros((narrow, rows, model), BF16)
        for step, piece in enumerate(fan_out(out_weight, narrow_swap, narrow)):
            out_own = put(out_own, piece[None], (layer ^ step, 0, 0))
        out_own = out_own.reshape(narrow * rows, model)

        gains = jnp.stack([attention_gain, feedforward_gain]).astype(F32)
        gain_buffer = jnp.zeros((2, wide, narrow, rows), F32)
        near_gains = jnp.stack([gains, core_swap(gains)])
        wide_gains = [near_gains] + [outer_swap(near_gains, s) for s in range(1, outer)]
        wide_gains = jnp.stack(wide_gains)
        for far in range(narrow):
            piece = wide_gains if far == 0 else narrow_swap(wide_gains, far)
            for step in range(outer):
                for near in range(INNER):
                    gain_buffer = put(
                        gain_buffer,
                        piece[step, near][:, None, None, :],
                        (0, place ^ (INNER * step + near), layer ^ far, 0),
                    )
        gain_one, gain_two = gain_buffer[0].reshape(1, model), gain_buffer[1].reshape(1, model)

        own_input = layer_input[0]
        residual = own_input.astype(F32)
        all_input = gather_near(own_input, outer_swap, outer)
        normed_one = (normalize(all_input.astype(F32))[0] * gain_one).astype(BF16)
        lin = mm(attention_weight, normed_one, ((0,), (1,)))
        lin = lin.reshape(-1, HEAD, lin.shape[1])
        mixed, query, key, value, lse = attend(
            place_arg, lin, cosine, sine, keydoc, doc, heads, tokens, outer
        )
        mixed = mixed.reshape(head_cols, -1)
        attended = scatter_near(mm(mixed, out_own, ((0,), (0,))), outer_swap, outer)
        after_attention = residual + attended
        scaled_two, factor_two = normalize(after_attention)
        normed_own = (scaled_two * gain_two).astype(BF16)

        def for_group(weight):
            return weight.reshape(rows, outer, INNER, narrow, down_rows)

        pair_weight = jnp.stack([for_group(gate_weight), for_group(up_weight)])
        pair_weight = pair_weight.transpose(3, 4, 1, 0, 2, 5)
        pair_cols = 2 * outer * down_rows
        pair_weight = pair_weight.reshape(INNER, narrow, rows, pair_cols)
        mine = pick(pair_weight, core)
        other = core_swap(pick(pair_weight, 1 - core))
        near_pair = jnp.stack([mine, other])
        column = jnp.zeros((INNER, narrow, rows, pair_cols), BF16)
        for step in range(narrow):
            piece = pick(near_pair, layer ^ step, 1)
            if step:
                piece = narrow_swap(piece, step)
            for near in range(INNER):
                column = put(column, piece[near][None, None], (core ^ near, layer ^ step, 0, 0))
        gate_up = jnp.zeros((outer, INNER * narrow * rows, pair_cols), BF16)
        column = column.reshape(INNER * narrow * rows, pair_cols)
        for step, piece in enumerate(fan_out(column, outer_swap, outer)):
            gate_up = put(gate_up, piece[None], (chip ^ step, 0, 0))
        gate_up = gate_up.reshape(model, pair_cols)
        down = jnp.zeros((outer, down_rows, model), BF16)
        for step, piece in enumerate(fan_out(down_weight, outer_swap, outer)):
            down = put(down, piece[None], (chip ^ step, 0, 0))
        down = down.reshape(outer * down_rows, model)

        grad_out_own = output_grad[0]
        grad_out = gather_near(grad_out_own, narrow_swap, narrow)
        normed_two = gather_near(normed_own, narrow_swap, narrow)
        both = mm(normed_two, gate_up, ((1,), (0,)))
        units = pair_cols // 2
        gate, upward = both[:, :units], both[:, units:]
        sigmoid_gate = jax.nn.sigmoid(gate)
        activated = gate * sigmoid_gate
        hidden = (activated * upward).astype(BF16)
        grad_hidden = mm(grad_out, down, ((1,), (1,)))
        slope = sigmoid_gate * (1.0 + gate * (1.0 - sigmoid_gate))
        grad_gate = (grad_hidden * upward * slope).astype(BF16)
        grad_up = (grad_hidden * activated).astype(BF16)
        grad_pair = jnp.concatenate([grad_gate, grad_up], axis=1)
        grad_two = scatter_near(mm(grad_pair, gate_up, ((1,), (1,))), narrow_swap, narrow)

        grad_scaled_two = grad_two * gain_two
        grad_middle = grad_out_own.astype(F32) + factor_two * (
            grad_scaled_two
            - scaled_two * jnp.mean(grad_scaled_two * scaled_two, axis=-1, keepdims=True)
        )
        grad_attention = gather_near(grad_middle.astype(BF16), outer_swap, outer)
        grad_mixed = mm(out_own, grad_attention, ((1,), (1,))).astype(BF16)
        grad_lin = attend_back(
            place_arg, grad_mixed.reshape(heads, HEAD, -1), query, key, value, lse, cosine, sine,
            keydoc, doc, tokens, outer,
        ).reshape(cols, -1)
        grad_one = scatter_near(mm(grad_lin, attention_weight, ((0,), (1,))), outer_swap, outer)
        scaled_one, factor_one = normalize(residual)
        grad_scaled_one = grad_one * gain_one
        input_grad = grad_middle + factor_one * (
            grad_scaled_one
            - scaled_one * jnp.mean(grad_scaled_one * scaled_one, axis=-1, keepdims=True)
        )

        branch = scatter_near(mm(hidden, down, ((1,), (0,))), narrow_swap, narrow)
        layer_output = after_attention + branch

        down_term = mm(hidden, grad_out, ((0,), (0,))).reshape(outer, down_rows, model)
        down_grad = sum_scatter(
            [pick(down_term, chip ^ step) for step in range(outer)], outer_swap, outer
        )
        pair_term = mm(normed_two, grad_pair, ((0,), (0,))).reshape(outer, -1, pair_cols)
        pair_sum = sum_scatter(
            [pick(pair_term, chip ^ step) for step in range(outer)], outer_swap, outer
        )
        pair_sum = pair_sum.astype(BF16).reshape(INNER, narrow, rows, pair_cols)
        mine = pick(pair_sum, core)
        other = core_swap(pick(pair_sum, 1 - core))
        near_pair = jnp.stack([mine, other])
        pair_grad = jnp.zeros((2, rows, outer, INNER, narrow, down_rows), F32)
        for step in range(narrow):
            piece = pick(near_pair, layer ^ step, 1)
            if step:
                piece = narrow_swap(piece, step)
            piece = piece.astype(F32).reshape(INNER, rows, 2, outer, down_rows)
            piece = piece.transpose(0, 2, 1, 3, 4)
            for near in range(INNER):
                pair_grad = put(
                    pair_grad,
                    piece[near][:, :, :, None, None, :],
                    (0, 0, 0, core ^ near, layer ^ step, 0),
                )
        pair_grad = pair_grad.reshape(2, rows, -1)
        gate_grad, up_grad = pair_grad[0], pair_grad[1]
        gain_two_grad = (
            jnp.sum(gate_grad * gate_weight.astype(F32), axis=1)
            + jnp.sum(up_grad * up_weight.astype(F32), axis=1)
        ) / feedforward_gain.astype(F32)

        out_term = mm(mixed, grad_attention, ((1,), (0,))).reshape(narrow, rows, model)
        out_grad = sum_scatter(
            [pick(out_term, layer ^ step) for step in range(narrow)], narrow_swap, narrow
        )
        lin_term = mm(normed_one, grad_lin, ((0,), (1,))).reshape(wide, narrow, rows, cols)
        lin_sum = sum_scatter(
            [pick(lin_term, layer ^ step, 1) for step in range(narrow)], narrow_swap, narrow
        )
        lin_sum = lin_sum.astype(BF16).reshape(outer, INNER, rows, cols)
        mine = pick(lin_sum, core, 1)
        other = core_swap(pick(lin_sum, 1 - core, 1))
        pair = jnp.stack([mine, other], axis=1)
        lin_grad = jnp.zeros((wide, rows, cols), F32)
        for step in range(outer):
            piece = pick(pair, chip ^ step)
            if step:
                piece = outer_swap(piece, step)
            for near in range(INNER):
                lin_grad = put(
                    lin_grad, piece[near][None].astype(F32), (place ^ (INNER * step + near), 0, 0)
                )
        query_grad = lin_grad[:, :, :head_cols].transpose(1, 0, 2).reshape(rows, -1)

        def kv_join(part):
            joined = part.reshape(wide // repeat, repeat, rows, kv_cols).sum(axis=1)
            return joined.transpose(1, 0, 2).reshape(rows, -1)

        key_grad = kv_join(lin_grad[:, :, head_cols : head_cols + kv_cols])
        value_grad = kv_join(lin_grad[:, :, head_cols + kv_cols :])
        gain_one_grad = (
            jnp.sum(query_grad * query_weight.astype(F32), axis=1)
            + jnp.sum(key_grad * key_weight.astype(F32), axis=1)
            + jnp.sum(value_grad * value_weight.astype(F32), axis=1)
        ) / attention_gain.astype(F32)
        return (
            layer_output[None].astype(BF16),
            input_grad[None].astype(BF16),
            gain_one_grad,
            query_grad,
            key_grad,
            value_grad,
            out_grad,
            gain_two_grad,
            gate_grad,
            up_grad,
            down_grad,
        )

    return per_device


def solution(mesh):
    rows = P(("wide", "narrow"), None)
    line = P(("wide", "narrow"))
    stream = P("narrow", "wide", None)
    return jax.shard_map(
        make_program(mesh.shape["wide"], mesh.shape["narrow"]),
        mesh=mesh,
        in_specs=(
            stream, stream, P("narrow", None), P("narrow", None),
            line, rows, rows, rows, rows, line, rows, rows, rows,
        ),
        out_specs=(stream, stream, line, rows, rows, rows, rows, line, rows, rows, rows),
        check_vma=False,
    )
```

time: 5440 us -> 904 us (0.17)
  waiting for transfers between devices: 5020 us -> 334 us
  local copies, waits for them, and re-layouts: 42.5 us -> 241 us
  matrix products: 247 us -> 81.6 us
  starting transfers between devices: 0.85 us -> 135 us
  blocking collectives: 83.4 us -> 0 us
    reduce_scatter x5 -> x0, waiting for transfers between devices: 2440 us -> none  [the longest x1 1410 us: per_device(): lax.psum_scatter(contract_rows(hidden, grad_branch), ('wide', 'narrow'),...]
    unnamed x20 -> x0, waiting for transfers between devices: 1800 us -> none
    all_gather x9 -> x0, waiting for transfers between devices: 783 us -> none  [the longest x1 191 us: per_device(): lax.all_gather(gate_weight, ('wide', 'narrow'), axis=0, tiled=True)]
    ppermute x0 -> x79, waiting for transfers between devices: none -> 334 us  [exchange(): return lax.ppermute(value, axis, [(i, i ^ step) for i in range(size)])]
    dot_general x27 -> x12, matrix products: 247 us -> 81.6 us  [mm(): lax.dot_general(left, right, (dims, ((), ())), preferred_element_type=F32)]
    ppermute x0 -> x79, starting transfers between devices: none -> 135 us  [exchange(): return lax.ppermute(value, axis, [(i, i ^ step) for i in range(size)])]
    dynamic_update_slice x0 -> x79, local copies, waits for them, and re-layouts: none -> 106 us  [put(): lax.dynamic_update_slice(buffer, piece, tuple((jnp.asarray(i, jnp.int32)...]
    unnamed x2 -> x0, blocking collectives: 83.4 us -> none
  transfers between devices with their start and end apart: 17 -> 79, of which waited for: 16 -> 33; matrix products, arithmetic and copies ran while one was open for 4% -> 37% of each run, Pallas kernels for 0% -> 3%
where the time goes in v1:
time: 904 us; the launch traced here: 892 us
  waiting for transfers between devices  334 us (37%)
  local copies, waits for them, and re-layouts  241 us (27%)
  starting transfers between devices  135 us (15%)
  matrix products  81.6 us (9%)
  other arithmetic  73 us (8%)
  Pallas kernels  24.4 us (3%)
    ppermute x79, waiting for transfers between devices, exchange(): return lax.ppermute(value, axis, [(i, i ^ step) for i in range(size)])  334 us
    ppermute x79, starting transfers between devices, exchange(): return lax.ppermute(value, axis, [(i, i ^ step) for i in range(size)])  135 us
    dynamic_update_slice x79, local copies, waits for them, and re-layouts, put(): lax.dynamic_update_slice(buffer, piece, tuple((jnp.asarray(i, jnp.int32)...  106 us
    dot_general x12, matrix products, mm(): lax.dot_general(left, right, (dims, ((), ())), preferred_element_type=F32)  81.6 us
    unnamed x103, local copies, waits for them, and re-layouts  30.5 us
  transfers between devices with their start and end apart: 79, of which 33 were waited for; matrix products, arithmetic and copies ran while one was open for 37% of the time, Pallas kernels for 3%

profile of v1, /device:TPU:0, one launch (start us, length us, event | category | flops | bytes accessed | tf_op | source)
XLA Modules:
  0.0 891.9 jit_solution(11284435532639995217)
XLA Ops:
  40.3 4.5 collective-permute-done.15
  49.3 3.7 collective-permute-start.17
  61.4 16.4 %collective-permute-done.19 = bf16[64,2048]{1,0:T(8,128)(2,1)S(1)} collective-permute-done((bf16[64,2048]{1,0:T(8,128)(2,1)S(1)}, bf16[64,2048]{1,0:T(8,128)(2,1)S(1)}, u32[]{:S(2)}, u32[]{:S(2)}) %collective-permute-start.19) | collective-permute-done | bytes 262176 | tf_op jit(solution)/shard_map/ppermute | solution.py:248
  92.7 5.7 collective-permute-start.44
  110.5 21.0 %collective-permute-done.44 = bf16[128,2048]{1,0:T(8,128)(2,1)S(1)} collective-permute-done((bf16[128,2048]{1,0:T(8,128)(2,1)}, bf16[128,2048]{1,0:T(8,128)(2,1)S(1)}, u32[]{:S(2)}, u32[]{:S(2)}) %collective-permute-start.44) | collective-permute-done | bytes 524320 | tf_op jit(solution)/shard_map/ppermute | solution.py:248
  132.3 9.6 %collective-permute-start.5 = (bf16[8,64,384]{2,1,0:T(8,128)(2,1)S(1)}, bf16[8,64,384]{2,1,0:T(8,128)(2,1)S(1)}, u32[]{:S(2)}, u32[]{:S(2)}) collective-permute-start(bf16[8,64,384]{2,1,0:T(8,128)(2,1)S(1)} %bitcast.773), channel_id=1, source_target_pairs={{0,2},{1,3},{2,0},{3,1},{4,6},{5,7},{6,4},{7,5},{8,10},{9,11},{10,... | collective-permute-start | bytes 1179656 | tf_op jit(solution)/shard_map/ppermute | solution.py:248
  151.4 17.4 %collective-permute-done.5 = bf16[8,64,384]{2,1,0:T(8,128)(2,1)S(1)} collective-permute-done((bf16[8,64,384]{2,1,0:T(8,128)(2,1)S(1)}, bf16[8,64,384]{2,1,0:T(8,128)(2,1)S(1)}, u32[]{:S(2)}, u32[]{:S(2)}) %collective-permute-start.5) | collective-permute-done | bytes 393248 | tf_op jit(solution)/shard_map/ppermute | solution.py:248
  175.7 4.5 collective-permute-start.30
  186.6 4.8 collective-permute-done.38
  191.4 4.3 collective-permute-start.32
  212.6 11.5 %shard_map.221 = (bf16[4,64,1024]{2,1,0:T(8,128)(2,1)S(1)}, bf16[4,64,1024]{2,1,0:T(8,128)(2,1)S(1)}, bf16[1,64,1024]{2,1,0:T(8,128)(2,1)S(1)}, bf16[1,64,1024]{2,1,0:T(8,128)(2,1)S(1)}, f32[4,1,1024]{2,1,0:T(1,128)S(1)}) custom-call(s32[1]{0:T(128)} %bitcast.1.place_ref, f32[6,64,1024]{2,1,0:T(8,128)S(1)} %fusion.136.lin_ref, ...), custom_call_target="tpu_custom_call" | custom-call | flops 1073741824 | bytes 3145728 | tf_op jit(solution)/shard_map/pallas_call | solution.py:196
  234.9 4.4 broadcast_in_dim.112
  243.6 43.1 %collective-permute-done.24 = bf16[128,2048]{1,0:T(8,128)(2,1)S(1)} collective-permute-done((bf16[128,2048]{1,0:T(8,128)(2,1)}, bf16[128,2048]{1,0:T(8,128)(2,1)S(1)}, u32[]{:S(2)}, u32[]{:S(2)}) %collective-permute-start.24) | collective-permute-done | bytes 524320 | tf_op jit(solution)/shard_map/ppermute | solution.py:248
  289.0 8.3 collective-permute-done.22
  300.1 5.8 collective-permute-start.25
  310.2 12.3 %collective-permute-done.25 = bf16[128,2048]{1,0:T(8,128)(2,1)S(1)} collective-permute-done((bf16[128,2048]{1,0:T(8,128)(2,1)S(1)}, bf16[128,2048]{1,0:T(8,128)(2,1)S(1)}, u32[]{:S(2)}, u32[]{:S(2)}) %collective-permute-start.25) | collective-permute-done | bytes 524320 | tf_op jit(solution)/shard_map/ppermute | solution.py:248
  322.5 21.6 %collective-permute-done.26 = bf16[128,2048]{1,0:T(8,128)(2,1)S(1)} collective-permute-done((bf16[128,2048]{1,0:T(8,128)(2,1)S(1)}, bf16[128,2048]{1,0:T(8,128)(2,1)S(1)}, u32[]{:S(2)}, u32[]{:S(2)}) %collective-permute-start.26) | collective-permute-done | bytes 524320 | tf_op jit(solution)/shard_map/ppermute | solution.py:248
  344.5 4.3 collective-permute-done.34
  355.7 6.4 copy.179
  362.1 14.5 %fusion.138 = f32[1024,2048]{1,0:T(8,128)} fusion(bf16[1024,2048]{1,0:T(8,128)(2,1)} %bitcast.101, bf16[2048,2048]{1,0:T(8,128)(2,1)} %bitcast.119), kind=kOutput, calls=%fused_computation.413 | convolution fusion | flops 8589934592 | bytes 20971520 | tf_op jit(solution)/shard_map/dot_general | solution.py:47
  376.6 11.7 %multiply_convert_fusion.2 = (bf16[1024,1024]{1,0:T(8,128)(2,1)S(1)}, bf16[1024,1024]{1,0:T(8,128)(2,1)S(1)}, bf16[1024,1024]{1,0:T(8,128)(2,1)S(1)}) fusion(f32[1024,2048]{1,0:T(8,128)} %fusion.138, bf16[1024,2048]{1,0:T(8,128)(2,1)} %bitcast.140, bf16[1024,2048]{1,0:T(8,128)(2,1)} %bitcast.124), kind=kOutput, calls=%fused_computation.20 | convolution fusion | flops 4310695936 | bytes 23068672 | tf_op jit(solution)/shard_map/dot_general | solution.py:47
  388.4 13.5 %fusion.8 = f32[1024,2048]{1,0:T(8,128)S(1)} fusion(bf16[2048,2048]{1,0:T(8,128)(2,1)} %bitcast.119, bf16[1024,1024]{1,0:T(8,128)(2,1)S(1)} %get-tuple-element.37, bf16[1024,1024]{1,0:T(8,128)(2,1)S(1)} %get-tuple-element.36), kind=kOutput, calls=%fused_computation.40 | convolution fusion | flops 8598323200 | bytes 20971520 | tf_op jit(solution)/shard_map/dot_general | solution.py:47
  403.8 7.9 fusion.139
  416.6 3.9 copy.189
  420.6 7.2 fusion.143
  435.2 11.8 %fusion.5 = f32[4,512,2048]{2,1,0:T(8,128)} fusion(bf16[4,512,1024]{2,1,0:T(8,128)(2,1)S(1)} %bitcast.752, bf16[1024,1024]{1,0:T(8,128)(2,1)S(1)} %copy-done.43, bf16[1024,1024]{1,0:T(8,128)(2,1)S(1)} %copy-done.41), kind=kOutput, calls=%fused_computation.14 | convolution fusion | flops 8598323200 | bytes 25165824 | tf_op jit(solution)/shard_map/dot_general | solution.py:47
  447.0 7.7 fusion.9
  454.7 3.9 collective-permute-done.78
  459.1 20.9 %collective-permute-done.77 = bf16[256,2048]{1,0:T(8,128)(2,1)S(1)} collective-permute-done((bf16[256,2048]{1,0:T(8,128)(2,1)S(1)}, bf16[256,2048]{1,0:T(8,128)(2,1)S(1)}, u32[]{:S(2)}, u32[]{:S(2)}) %collective-permute-start.77) | collective-permute-done | bytes 1048608 | tf_op jit(solution)/shard_map/ppermute | solution.py:248
  482.1 5.2 fusion.1
  487.3 6.8 copy.170
  494.6 4.5 fusion.13
  503.0 3.9 collective-permute-start.49
  506.9 3.7 fusion.52
  510.6 15.5 %collective-permute-done.71 = bf16[512,2048]{1,0:T(8,128)(2,1)} collective-permute-done((bf16[512,2048]{1,0:T(8,128)(2,1)}, bf16[512,2048]{1,0:T(8,128)(2,1)}, u32[]{:S(2)}, u32[]{:S(2)}) %collective-permute-start.71) | collective-permute-done | bytes 2097184 | tf_op jit(solution)/shard_map/ppermute | solution.py:248
  528.8 41.8 %collective-permute-done.70 = bf16[512,2048]{1,0:T(8,128)(2,1)} collective-permute-done((bf16[512,2048]{1,0:T(8,128)(2,1)}, bf16[512,2048]{1,0:T(8,128)(2,1)}, u32[]{:S(2)}, u32[]{:S(2)}) %collective-permute-start.70) | collective-permute-done | bytes 2097184 | tf_op jit(solution)/shard_map/ppermute | solution.py:248
  571.8 5.7 fusion.4
  600.0 8.5 collective-permute-done.52
  623.6 6.9 copy.180
  631.1 5.3 collective-permute-done.74
  650.3 12.0 %dynamic_update_slice.315 = f32[2,64,4,2,4,256]{5,4,3,2,1,0:T(4,128)} dynamic-update-slice(f32[2,64,4,2,4,256]{5,4,3,2,1,0:T(4,128)} %copy.180, f32[2,64,4,1,1,256]{5,4,3,2,1,0:T(1,128)S(1)} %copy.181, s32[]{:T(128)} %constant.160.clone.1, s32[]{:T(128)} %constant.160.clone.1, s32[]{:T(128)} %constant.160.clone.1, s32[]{:T(128)S(6)} %select_n.136, s32[]{:T(128)S(6)} %select_n.130, s32[]{:T(128)} %constant.160.clone.1) | dynamic-update-slice | bytes 1048580 | tf_op jit(solution)/shard_map/dynamic_update_slice | solution.py:252
  662.3 12.1 %dynamic_update_slice.316 = f32[2,64,4,2,4,256]{5,4,3,2,1,0:T(4,128)} dynamic-update-slice(f32[2,64,4,2,4,256]{5,4,3,2,1,0:T(4,128)} %dynamic_update_slice.315, f32[2,64,4,1,1,256]{5,4,3,2,1,0:T(1,128)} %copy.182, s32[]{:T(128)} %constant.160.clone.1, s32[]{:T(128)} %constant.160.clone.1, s32[]{:T(128)} %constant.160.clone.1, s32[]{:T(128)S(6)} %select_n.112, s32[]{:T(128)S(6)} %select_n.131, ...) | dynamic-update-slice | bytes 1048580 | tf_op jit(solution)/shard_map/dynamic_update_slice | solution.py:252
  674.4 12.1 %dynamic_update_slice.317 = f32[2,64,4,2,4,256]{5,4,3,2,1,0:T(4,128)} dynamic-update-slice(f32[2,64,4,2,4,256]{5,4,3,2,1,0:T(4,128)} %dynamic_update_slice.316, f32[2,64,4,1,1,256]{5,4,3,2,1,0:T(1,128)} %copy.183, s32[]{:T(128)} %constant.160.clone.1, s32[]{:T(128)} %constant.160.clone.1, s32[]{:T(128)} %constant.160.clone.1, s32[]{:T(128)S(6)} %select_n.136, s32[]{:T(128)S(6)} %select_n.131, ...) | dynamic-update-slice | bytes 1048580 | tf_op jit(solution)/shard_map/dynamic_update_slice | solution.py:252
  686.4 12.1 %dynamic_update_slice.318 = f32[2,64,4,2,4,256]{5,4,3,2,1,0:T(4,128)} dynamic-update-slice(f32[2,64,4,2,4,256]{5,4,3,2,1,0:T(4,128)} %dynamic_update_slice.317, f32[2,64,4,1,1,256]{5,4,3,2,1,0:T(1,128)} %copy.184, s32[]{:T(128)} %constant.160.clone.1, s32[]{:T(128)} %constant.160.clone.1, s32[]{:T(128)} %constant.160.clone.1, s32[]{:T(128)S(6)} %select_n.112, s32[]{:T(128)S(6)} %select_n.132, ...) | dynamic-update-slice | bytes 1048580 | tf_op jit(solution)/shard_map/dynamic_update_slice | solution.py:252
  698.5 12.1 %dynamic_update_slice.319 = f32[2,64,4,2,4,256]{5,4,3,2,1,0:T(4,128)} dynamic-update-slice(f32[2,64,4,2,4,256]{5,4,3,2,1,0:T(4,128)} %dynamic_update_slice.318, f32[2,64,4,1,1,256]{5,4,3,2,1,0:T(1,128)} %copy.185, s32[]{:T(128)} %constant.160.clone.1, s32[]{:T(128)} %constant.160.clone.1, s32[]{:T(128)} %constant.160.clone.1, s32[]{:T(128)S(6)} %select_n.136, s32[]{:T(128)S(6)} %select_n.132, ...) | dynamic-update-slice | bytes 1048580 | tf_op jit(solution)/shard_map/dynamic_update_slice | solution.py:252
  710.6 5.8 fusion.135
  723.0 3.4 multiply_reduce_fusion.1
  730.1 3.6 convolution_convert_fusion
  733.7 12.8 %shard_map.222 = bf16[6,64,1024]{2,1,0:T(8,128)(2,1)S(1)} custom-call(s32[1]{0:T(128)} %bitcast.1.place_ref, bf16[4,64,1024]{2,1,0:T(8,128)(2,1)S(1)} %bitcast.726, bf16[4,64,1024]{2,1,0:T(8,128)(2,1)S(1)} %get-tuple-element.17.query_ref, bf16[1,64,1024]{2,1,0:T(8,128)(2,1)S(1)} %get-tuple-element.18.key_ref, ...), custom_call_target="tpu_custom_call" | custom-call | flops 2684354560 | bytes 3145728 | tf_op jit(solution)/shard_map/pallas_call | solution.py:225
  750.6 3.6 copy-done.15
  761.5 3.4 fusion.142
  765.0 5.6 collective-permute-done.61
  773.0 24.6 %collective-permute-done.60 = bf16[8,64,384]{2,1,0:T(8,128)(2,1)S(1)} collective-permute-done((bf16[8,64,384]{2,1,0:T(8,128)(2,1)S(1)}, bf16[8,64,384]{2,1,0:T(8,128)(2,1)S(1)}, u32[]{:S(2)}, u32[]{:S(2)}) %collective-permute-start.60) | collective-permute-done | bytes 393248 | tf_op jit(solution)/shard_map/ppermute | solution.py:248
  800.8 9.5 %collective-permute-start.41 = (bf16[128,2048]{1,0:T(8,128)(2,1)}, bf16[128,2048]{1,0:T(8,128)(2,1)}, u32[]{:S(2)}, u32[]{:S(2)}) collective-permute-start(bf16[128,2048]{1,0:T(8,128)(2,1)} %get-tuple-element.46), channel_id=1, source_target_pairs={{0,2},{1,3},{2,0},{3,1},{4,6},{5,7},{6,4},{7,5},{8,10},{9,11},{10,... | collective-permute-start | bytes 1572872 | tf_op jit(solution)/shard_map/ppermute | solution.py:248
  810.3 15.4 %collective-permute-done.67 = bf16[64,2048]{1,0:T(8,128)(2,1)S(1)} collective-permute-done((bf16[64,2048]{1,0:T(8,128)(2,1)S(1)}, bf16[64,2048]{1,0:T(8,128)(2,1)S(1)}, u32[]{:S(2)}, u32[]{:S(2)}) %collective-permute-start.67) | collective-permute-done | bytes 262176 | tf_op jit(solution)/shard_map/ppermute | solution.py:248
  837.8 3.6 dynamic_update_slice.307
  841.4 3.6 dynamic_update_slice.308
  845.0 3.6 dynamic_update_slice.309
  848.6 3.6 dynamic_update_slice.310
  852.2 3.8 dynamic_update_slice.311
  856.0 4.0 fusion.30
  870.5 5.6 collective-permute-done.58
  876.1 8.8 collective-permute-done.57
  887.4 4.0 fusion.73
  (409 shorter events, 280.3 us)
Async XLA Ops:
  0.7 98.1 %collective-permute-start.7 = (bf16[128,2048]{1,0:T(8,128)(2,1)}, bf16[128,2048]{1,0:T(8,128)(2,1)}, u32[]{:S(2)}, u32[]{:S(2)}) collective-permute-start(bf16[128,2048]{1,0:T(8,128)(2,1)} %bitcast.732), channel_id=1, source_target_pairs={{0,8},{4,12},{8,0},{12,4},{16,24},{20,28},{24,16},{28,20},{1,9},{5... | collective-permute-start | bytes 1572872 | tf_op jit(solution)/shard_map/ppermute | solution.py:248
  3.7 99.0 %collective-permute-start.8 = (bf16[128,2048]{1,0:T(8,128)(2,1)}, bf16[128,2048]{1,0:T(8,128)(2,1)}, u32[]{:S(2)}, u32[]{:S(2)}) collective-permute-start(bf16[128,2048]{1,0:T(8,128)(2,1)} %bitcast.733), channel_id=1, source_target_pairs={{0,16},{4,20},{8,24},{12,28},{16,0},{20,4},{24,8},{28,12},{1,17},{... | collective-permute-start | bytes 1572872 | tf_op jit(solution)/shard_map/ppermute | solution.py:248
  5.9 27.1 %collective-permute-start.11 = (f32[2,64]{1,0:T(2,128)S(1)}, f32[2,64]{1,0:T(2,128)S(1)}, u32[]{:S(2)}, u32[]{:S(2)}) collective-permute-start(f32[2,64]{1,0:T(2,128)S(1)} %maximum_convert_fusion.1), channel_id=1, source_target_pairs={{0,4},{4,0},{8,12},{12,8},{16,20},{20,16},{24,28},{28,24},{1,5},{5... | collective-permute-start | bytes 1544 | tf_op jit(solution)/shard_map/ppermute | solution.py:248
  36.7 69.5 %collective-permute-start.9 = (bf16[128,2048]{1,0:T(8,128)(2,1)S(1)}, bf16[128,2048]{1,0:T(8,128)(2,1)}, u32[]{:S(2)}, u32[]{:S(2)}) collective-permute-start(bf16[128,2048]{1,0:T(8,128)(2,1)S(1)} %bitcast.734), channel_id=1, source_target_pairs={{0,24},{4,28},{8,16},{12,20},{16,8},{20,12},{24,0},{28,4},{1,25},{... | collective-permute-start | bytes 1572872 | tf_op jit(solution)/shard_map/ppermute | solution.py:248
  37.2 21.3 %collective-permute-start.18 = (bf16[64,2048]{1,0:T(8,128)(2,1)S(1)}, bf16[64,2048]{1,0:T(8,128)(2,1)S(1)}, u32[]{:S(2)}, u32[]{:S(2)}) collective-permute-start(bf16[64,2048]{1,0:T(8,128)(2,1)S(1)} %copy-done.32), channel_id=1, source_target_pairs={{0,1},{1,0},{2,3},{3,2},{4,5},{5,4},{6,7},{7,6},{8,9},{9,8},{10,11... | collective-permute-start | bytes 786440 | tf_op jit(solution)/shard_map/ppermute | solution.py:248
  56.6 21.3 %collective-permute-start.19 = (bf16[64,2048]{1,0:T(8,128)(2,1)S(1)}, bf16[64,2048]{1,0:T(8,128)(2,1)S(1)}, u32[]{:S(2)}, u32[]{:S(2)}) collective-permute-start(bf16[64,2048]{1,0:T(8,128)(2,1)S(1)} %copy-done.32), channel_id=1, source_target_pairs={{0,2},{1,3},{2,0},{3,1},{4,6},{5,7},{6,4},{7,5},{8,10},{9,11},{10,... | collective-permute-start | bytes 786440 | tf_op jit(solution)/shard_map/ppermute | solution.py:248
  58.5 19.4 %collective-permute-start.20 = (bf16[64,2048]{1,0:T(8,128)(2,1)S(1)}, bf16[64,2048]{1,0:T(8,128)(2,1)S(1)}, u32[]{:S(2)}, u32[]{:S(2)}) collective-permute-start(bf16[64,2048]{1,0:T(8,128)(2,1)S(1)} %copy-done.32), channel_id=1, source_target_pairs={{0,3},{1,2},{2,1},{3,0},{4,7},{5,6},{6,5},{7,4},{8,11},{9,10},{10,... | collective-permute-start | bytes 786440 | tf_op jit(solution)/shard_map/ppermute | solution.py:248
  77.9 31.8 %collective-permute-start.43 = (bf16[128,2048]{1,0:T(8,128)(2,1)}, bf16[128,2048]{1,0:T(8,128)(2,1)S(1)}, u32[]{:S(2)}, u32[]{:S(2)}) collective-permute-start(bf16[128,2048]{1,0:T(8,128)(2,1)} %bitcast.136), channel_id=1, source_target_pairs={{0,1},{1,0},{2,3},{3,2},{4,5},{5,4},{6,7},{7,6},{8,9},{9,8},{10,11... | collective-permute-start | bytes 1572872 | tf_op jit(solution)/shard_map/ppermute | solution.py:248
  92.7 38.7 %collective-permute-start.44 = (bf16[128,2048]{1,0:T(8,128)(2,1)}, bf16[128,2048]{1,0:T(8,128)(2,1)S(1)}, u32[]{:S(2)}, u32[]{:S(2)}) collective-permute-start(bf16[128,2048]{1,0:T(8,128)(2,1)} %bitcast.136), channel_id=1, source_target_pairs={{0,2},{1,3},{2,0},{3,1},{4,6},{5,7},{6,4},{7,5},{8,10},{9,11},{10,... | collective-permute-start | bytes 1572872 | tf_op jit(solution)/shard_map/ppermute | solution.py:248
  98.8 33.5 %collective-permute-start.45 = (bf16[128,2048]{1,0:T(8,128)(2,1)}, bf16[128,2048]{1,0:T(8,128)(2,1)S(1)}, u32[]{:S(2)}, u32[]{:S(2)}) collective-permute-start(bf16[128,2048]{1,0:T(8,128)(2,1)} %bitcast.136), channel_id=1, source_target_pairs={{0,3},{1,2},{2,1},{3,0},{4,7},{5,6},{6,5},{7,4},{8,11},{9,10},{10,... | collective-permute-start | bytes 1572872 | tf_op jit(solution)/shard_map/ppermute | solution.py:248
  102.7 73.0 %collective-permute-start.36 = (bf16[256,2048]{1,0:T(8,128)(2,1)}, bf16[256,2048]{1,0:T(8,128)(2,1)}, u32[]{:S(2)}, u32[]{:S(2)}) collective-permute-start(bf16[256,2048]{1,0:T(8,128)(2,1)} %param.26), channel_id=1, source_target_pairs={{0,8},{4,12},{8,0},{12,4},{16,24},{20,28},{24,16},{28,20},{1,9},{5... | collective-permute-start | bytes 3145736 | tf_op jit(solution)/shard_map/ppermute | solution.py:248
  106.2 76.6 %collective-permute-start.37 = (bf16[256,2048]{1,0:T(8,128)(2,1)}, bf16[256,2048]{1,0:T(8,128)(2,1)}, u32[]{:S(2)}, u32[]{:S(2)}) collective-permute-start(bf16[256,2048]{1,0:T(8,128)(2,1)} %param.26), channel_id=1, source_target_pairs={{0,16},{4,20},{8,24},{12,28},{16,0},{20,4},{24,8},{28,12},{1,17},{... | collective-permute-start | bytes 3145736 | tf_op jit(solution)/shard_map/ppermute | solution.py:248
  109.6 63.8 %collective-permute-start.29 = (bf16[4,64,2048]{2,1,0:T(8,128)(2,1)}, bf16[4,64,2048]{2,1,0:T(8,128)(2,1)}, u32[]{:S(2)}, u32[]{:S(2)}) collective-permute-start(bf16[4,64,2048]{2,1,0:T(8,128)(2,1)} %get-tuple-element.72), channel_id=1, source_target_pairs={{0,4},{4,0},{8,12},{12,8},{16,20},{20,16},{24,28},{28,24},{1,5},{5... | collective-permute-start | bytes 3145736 | tf_op jit(solution)/shard_map/ppermute | solution.py:248
  131.5 16.9 %collective-permute-start.4 = (bf16[8,64,384]{2,1,0:T(8,128)(2,1)S(1)}, bf16[8,64,384]{2,1,0:T(8,128)(2,1)S(1)}, u32[]{:S(2)}, u32[]{:S(2)}) collective-permute-start(bf16[8,64,384]{2,1,0:T(8,128)(2,1)S(1)} %bitcast.772), channel_id=1, source_target_pairs={{0,1},{1,0},{2,3},{3,2},{4,5},{5,4},{6,7},{7,6},{8,9},{9,8},{10,11... | collective-permute-start | bytes 1179656 | tf_op jit(solution)/shard_map/ppermute | solution.py:248
  132.3 36.5 %collective-permute-start.5 = (bf16[8,64,384]{2,1,0:T(8,128)(2,1)S(1)}, bf16[8,64,384]{2,1,0:T(8,128)(2,1)S(1)}, u32[]{:S(2)}, u32[]{:S(2)}) collective-permute-start(bf16[8,64,384]{2,1,0:T(8,128)(2,1)S(1)} %bitcast.773), channel_id=1, source_target_pairs={{0,2},{1,3},{2,0},{3,1},{4,6},{5,7},{6,4},{7,5},{8,10},{9,11},{10,... | collective-permute-start | bytes 1179656 | tf_op jit(solution)/shard_map/ppermute | solution.py:248
  148.3 23.1 %collective-permute-start.6 = (bf16[8,64,384]{2,1,0:T(8,128)(2,1)S(1)}, bf16[8,64,384]{2,1,0:T(8,128)(2,1)S(1)}, u32[]{:S(2)}, u32[]{:S(2)}) collective-permute-start(bf16[8,64,384]{2,1,0:T(8,128)(2,1)S(1)} %bitcast.774), channel_id=1, source_target_pairs={{0,3},{1,2},{2,1},{3,0},{4,7},{5,6},{6,5},{7,4},{8,11},{9,10},{10,... | collective-permute-start | bytes 1179656 | tf_op jit(solution)/shard_map/ppermute | solution.py:248
  168.8 22.6 %collective-permute-start.38 = (bf16[256,2048]{1,0:T(8,128)(2,1)}, bf16[256,2048]{1,0:T(8,128)(2,1)}, u32[]{:S(2)}, u32[]{:S(2)}) collective-permute-start(bf16[256,2048]{1,0:T(8,128)(2,1)} %param.26), channel_id=1, source_target_pairs={{0,24},{4,28},{8,16},{12,20},{16,8},{20,12},{24,0},{28,4},{1,25},{... | collective-permute-start | bytes 3145736 | tf_op jit(solution)/shard_map/ppermute | solution.py:248
  171.4 29.8 %collective-permute-start.10 = (bf16[4,128,2048]{2,1,0:T(8,128)(2,1)}, bf16[4,128,2048]{2,1,0:T(8,128)(2,1)}, u32[]{:S(2)}, u32[]{:S(2)}) collective-permute-start(bf16[4,128,2048]{2,1,0:T(8,128)(2,1)} %pad_maximum_fusion.3), channel_id=1, source_target_pairs={{0,4},{4,0},{8,12},{12,8},{16,20},{20,16},{24,28},{28,24},{1,5},{5... | collective-permute-start | bytes 6291464 | tf_op jit(solution)/shard_map/ppermute | solution.py:248
  173.5 67.3 %collective-permute-start.46 = (bf16[4,128,2048]{2,1,0:T(8,128)(2,1)}, bf16[4,128,2048]{2,1,0:T(8,128)(2,1)S(1)}, u32[]{:S(2)}, u32[]{:S(2)}) collective-permute-start(bf16[4,128,2048]{2,1,0:T(8,128)(2,1)} %pad_maximum_fusion.5), channel_id=1, source_target_pairs={{0,4},{4,0},{8,12},{12,8},{16,20},{20,16},{24,28},{28,24},{1,5},{5... | collective-permute-start | bytes 6291464 | tf_op jit(solution)/shard_map/ppermute | solution.py:248
  175.7 25.4 %collective-permute-start.30 = (bf16[2,64,2048]{2,1,0:T(8,128)(2,1)S(1)}, bf16[2,64,2048]{2,1,0:T(8,128)(2,1)S(1)}, u32[]{:S(2)}, u32[]{:S(2)}) collective-permute-start(bf16[2,64,2048]{2,1,0:T(8,128)(2,1)S(1)} %get-tuple-element.70), channel_id=1, source_target_pairs={{0,1},{1,0},{2,3},{3,2},{4,5},{5,4},{6,7},{7,6},{8,9},{9,8},{10,11... | collective-permute-start | bytes 1572872 | tf_op jit(solution)/shard_map/ppermute | solution.py:248
  182.8 43.1 %collective-permute-start.31 = (bf16[2,64,2048]{2,1,0:T(8,128)(2,1)S(1)}, bf16[2,64,2048]{2,1,0:T(8,128)(2,1)S(1)}, u32[]{:S(2)}, u32[]{:S(2)}) collective-permute-start(bf16[2,64,2048]{2,1,0:T(8,128)(2,1)S(1)} %get-tuple-element.71), channel_id=1, source_target_pairs={{0,2},{1,3},{2,0},{3,1},{4,6},{5,7},{6,4},{7,5},{8,10},{9,11},{10,... | collective-permute-start | bytes 1572872 | tf_op jit(solution)/shard_map/ppermute | solution.py:248
  191.4 34.6 %collective-permute-start.32 = (bf16[2,64,2048]{2,1,0:T(8,128)(2,1)S(1)}, bf16[2,64,2048]{2,1,0:T(8,128)(2,1)S(1)}, u32[]{:S(2)}, u32[]{:S(2)}) collective-permute-start(bf16[2,64,2048]{2,1,0:T(8,128)(2,1)S(1)} %get-tuple-element.68), channel_id=1, source_target_pairs={{0,3},{1,2},{2,1},{3,0},{4,7},{5,6},{6,5},{7,4},{8,11},{9,10},{10,... | collective-permute-start | bytes 1572872 | tf_op jit(solution)/shard_map/ppermute | solution.py:248
  226.1 81.2 %collective-permute-start.33 = (bf16[512,2048]{1,0:T(8,128)(2,1)S(1)}, bf16[512,2048]{1,0:T(8,128)(2,1)S(1)}, u32[]{:S(2)}, u32[]{:S(2)}) collective-permute-start(bf16[512,2048]{1,0:T(8,128)(2,1)S(1)} %bitcast.736), channel_id=1, source_target_pairs={{0,8},{4,12},{8,0},{12,4},{16,24},{20,28},{24,16},{28,20},{1,9},{5... | collective-permute-start | bytes 6291464 | tf_op jit(solution)/shard_map/ppermute | solution.py:248
  231.4 55.3 %collective-permute-start.24 = (bf16[128,2048]{1,0:T(8,128)(2,1)}, bf16[128,2048]{1,0:T(8,128)(2,1)S(1)}, u32[]{:S(2)}, u32[]{:S(2)}) collective-permute-start(bf16[128,2048]{1,0:T(8,128)(2,1)} %get-tuple-element.48), channel_id=1, source_target_pairs={{0,24},{4,28},{8,16},{12,20},{16,8},{20,12},{24,0},{28,4},{1,25},{... | collective-permute-start | bytes 1572872 | tf_op jit(solution)/shard_map/ppermute | solution.py:248
  233.7 54.5 %collective-permute-start.23 = (bf16[128,2048]{1,0:T(8,128)(2,1)}, bf16[128,2048]{1,0:T(8,128)(2,1)S(1)}, u32[]{:S(2)}, u32[]{:S(2)}) collective-permute-start(bf16[128,2048]{1,0:T(8,128)(2,1)} %get-tuple-element.49), channel_id=1, source_target_pairs={{0,16},{4,20},{8,24},{12,28},{16,0},{20,4},{24,8},{28,12},{1,17},{... | collective-permute-start | bytes 1572872 | tf_op jit(solution)/shard_map/ppermute | solution.py:248
  234.3 63.0 %collective-permute-start.22 = (bf16[128,2048]{1,0:T(8,128)(2,1)}, bf16[128,2048]{1,0:T(8,128)(2,1)}, u32[]{:S(2)}, u32[]{:S(2)}) collective-permute-start(bf16[128,2048]{1,0:T(8,128)(2,1)} %get-tuple-element.47), channel_id=1, source_target_pairs={{0,8},{4,12},{8,0},{12,4},{16,24},{20,28},{24,16},{28,20},{1,9},{5... | collective-permute-start | bytes 1572872 | tf_op jit(solution)/shard_map/ppermute | solution.py:248
  240.8 108.0 %collective-permute-start.34 = (bf16[512,2048]{1,0:T(8,128)(2,1)S(1)}, bf16[512,2048]{1,0:T(8,128)(2,1)S(1)}, u32[]{:S(2)}, u32[]{:S(2)}) collective-permute-start(bf16[512,2048]{1,0:T(8,128)(2,1)S(1)} %bitcast.738), channel_id=1, source_target_pairs={{0,16},{4,20},{8,24},{12,28},{16,0},{20,4},{24,8},{28,12},{1,17},{... | collective-permute-start | bytes 6291464 | tf_op jit(solution)/shard_map/ppermute | solution.py:248
  286.7 63.5 %collective-permute-start.35 = (bf16[512,2048]{1,0:T(8,128)(2,1)S(1)}, bf16[512,2048]{1,0:T(8,128)(2,1)S(1)}, u32[]{:S(2)}, u32[]{:S(2)}) collective-permute-start(bf16[512,2048]{1,0:T(8,128)(2,1)S(1)} %bitcast.739), channel_id=1, source_target_pairs={{0,24},{4,28},{8,16},{12,20},{16,8},{20,12},{24,0},{28,4},{1,25},{... | collective-permute-start | bytes 6291464 | tf_op jit(solution)/shard_map/ppermute | solution.py:248
  300.1 22.4 %collective-permute-start.25 = (bf16[128,2048]{1,0:T(8,128)(2,1)S(1)}, bf16[128,2048]{1,0:T(8,128)(2,1)S(1)}, u32[]{:S(2)}, u32[]{:S(2)}) collective-permute-start(bf16[128,2048]{1,0:T(8,128)(2,1)S(1)} %get-tuple-element.30), channel_id=1, source_target_pairs={{0,1},{1,0},{2,3},{3,2},{4,5},{5,4},{6,7},{7,6},{8,9},{9,8},{10,11... | collective-permute-start | bytes 1572872 | tf_op jit(solution)/shard_map/ppermute | solution.py:248
  305.9 38.2 %collective-permute-start.26 = (bf16[128,2048]{1,0:T(8,128)(2,1)S(1)}, bf16[128,2048]{1,0:T(8,128)(2,1)S(1)}, u32[]{:S(2)}, u32[]{:S(2)}) collective-permute-start(bf16[128,2048]{1,0:T(8,128)(2,1)S(1)} %get-tuple-element.30), channel_id=1, source_target_pairs={{0,2},{1,3},{2,0},{3,1},{4,6},{5,7},{6,4},{7,5},{8,10},{9,11},{10,... | collective-permute-start | bytes 1572872 | tf_op jit(solution)/shard_map/ppermute | solution.py:248
  307.3 36.8 %collective-permute-start.27 = (bf16[128,2048]{1,0:T(8,128)(2,1)S(1)}, bf16[128,2048]{1,0:T(8,128)(2,1)S(1)}, u32[]{:S(2)}, u32[]{:S(2)}) collective-permute-start(bf16[128,2048]{1,0:T(8,128)(2,1)S(1)} %get-tuple-element.30), channel_id=1, source_target_pairs={{0,3},{1,2},{2,1},{3,0},{4,7},{5,6},{6,5},{7,4},{8,11},{9,10},{10,... | collective-permute-start | bytes 1572872 | tf_op jit(solution)/shard_map/ppermute | solution.py:248
  344.4 9.8 %collective-permute-start.28 = (bf16[4,128,2048]{2,1,0:T(8,128)(2,1)S(1)}, bf16[4,128,2048]{2,1,0:T(8,128)(2,1)S(1)}, u32[]{:S(2)}, u32[]{:S(2)}) collective-permute-start(bf16[4,128,2048]{2,1,0:T(8,128)(2,1)S(1)} %pad_maximum_fusion.4), channel_id=1, source_target_pairs={{0,4},{4,0},{8,12},{12,8},{16,20},{20,16},{24,28},{28,24},{1,5},{5... | collective-permute-start | bytes 6291464 | tf_op jit(solution)/shard_map/ppermute | solution.py:248
  403.8 95.4 %collective-permute-start.47 = (bf16[4,128,2048]{2,1,0:T(8,128)(2,1)}, bf16[4,128,2048]{2,1,0:T(8,128)(2,1)}, u32[]{:S(2)}, u32[]{:S(2)}) collective-permute-start(bf16[4,128,2048]{2,1,0:T(8,128)(2,1)} %bitcast.143), channel_id=1, source_target_pairs={{0,4},{4,0},{8,12},{12,8},{16,20},{20,16},{24,28},{28,24},{1,5},{5... | collective-permute-start | bytes 6291464 | tf_op jit(solution)/shard_map/ppermute | solution.py:248
  416.6 86.4 %collective-permute-start.39 = (bf16[4,128,2048]{2,1,0:T(8,128)(2,1)}, bf16[4,128,2048]{2,1,0:T(8,128)(2,1)}, u32[]{:S(2)}, u32[]{:S(2)}) collective-permute-start(bf16[4,128,2048]{2,1,0:T(8,128)(2,1)} %bitcast.127), channel_id=1, source_target_pairs={{0,4},{4,0},{8,12},{12,8},{16,20},{20,16},{24,28},{28,24},{1,5},{5... | collective-permute-start | bytes 6291464 | tf_op jit(solution)/shard_map/ppermute | solution.py:248
  431.6 27.0 %collective-permute-start.78 = (bf16[256,2048]{1,0:T(8,128)(2,1)S(1)}, bf16[256,2048]{1,0:T(8,128)(2,1)S(1)}, u32[]{:S(2)}, u32[]{:S(2)}) collective-permute-start(bf16[256,2048]{1,0:T(8,128)(2,1)S(1)} %get-tuple-element.51), channel_id=1, source_target_pairs={{0,24},{4,28},{8,16},{12,20},{16,8},{20,12},{24,0},{28,4},{1,25},{... | collective-permute-start | bytes 3145736 | tf_op jit(solution)/shard_map/ppermute | solution.py:248
  432.2 47.8 %collective-permute-start.77 = (bf16[256,2048]{1,0:T(8,128)(2,1)S(1)}, bf16[256,2048]{1,0:T(8,128)(2,1)S(1)}, u32[]{:S(2)}, u32[]{:S(2)}) collective-permute-start(bf16[256,2048]{1,0:T(8,128)(2,1)S(1)} %get-tuple-element.52), channel_id=1, source_target_pairs={{0,16},{4,20},{8,24},{12,28},{16,0},{20,4},{24,8},{28,12},{1,17},{... | collective-permute-start | bytes 3145736 | tf_op jit(solution)/shard_map/ppermute | solution.py:248
  433.7 47.8 %collective-permute-start.76 = (bf16[256,2048]{1,0:T(8,128)(2,1)S(1)}, bf16[256,2048]{1,0:T(8,128)(2,1)S(1)}, u32[]{:S(2)}, u32[]{:S(2)}) collective-permute-start(bf16[256,2048]{1,0:T(8,128)(2,1)S(1)} %get-tuple-element.50), channel_id=1, source_target_pairs={{0,8},{4,12},{8,0},{12,4},{16,24},{20,28},{24,16},{28,20},{1,9},{5... | collective-permute-start | bytes 3145736 | tf_op jit(solution)/shard_map/ppermute | solution.py:248
  458.6 67.6 %collective-permute-start.71 = (bf16[512,2048]{1,0:T(8,128)(2,1)}, bf16[512,2048]{1,0:T(8,128)(2,1)}, u32[]{:S(2)}, u32[]{:S(2)}) collective-permute-start(bf16[512,2048]{1,0:T(8,128)(2,1)} %get-tuple-element.34), channel_id=1, source_target_pairs={{0,24},{4,28},{8,16},{12,20},{16,8},{20,12},{24,0},{28,4},{1,25},{... | collective-permute-start | bytes 6291464 | tf_op jit(solution)/shard_map/ppermute | solution.py:248
  480.0 90.7 %collective-permute-start.70 = (bf16[512,2048]{1,0:T(8,128)(2,1)}, bf16[512,2048]{1,0:T(8,128)(2,1)}, u32[]{:S(2)}, u32[]{:S(2)}) collective-permute-start(bf16[512,2048]{1,0:T(8,128)(2,1)} %get-tuple-element.35), channel_id=1, source_target_pairs={{0,16},{4,20},{8,24},{12,28},{16,0},{20,4},{24,8},{28,12},{1,17},{... | collective-permute-start | bytes 6291464 | tf_op jit(solution)/shard_map/ppermute | solution.py:248
  481.4 90.3 %collective-permute-start.69 = (bf16[512,2048]{1,0:T(8,128)(2,1)}, bf16[512,2048]{1,0:T(8,128)(2,1)}, u32[]{:S(2)}, u32[]{:S(2)}) collective-permute-start(bf16[512,2048]{1,0:T(8,128)(2,1)} %get-tuple-element.33), channel_id=1, source_target_pairs={{0,8},{4,12},{8,0},{12,4},{16,24},{20,28},{24,16},{28,20},{1,9},{5... | collective-permute-start | bytes 6291464 | tf_op jit(solution)/shard_map/ppermute | solution.py:248
  502.0 75.7 %collective-permute-start.50 = (bf16[128,2048]{1,0:T(8,128)(2,1)S(1)}, bf16[128,2048]{1,0:T(8,128)(2,1)S(1)}, u32[]{:S(2)}, u32[]{:S(2)}) collective-permute-start(bf16[128,2048]{1,0:T(8,128)(2,1)S(1)} %get-tuple-element.42), channel_id=1, source_target_pairs={{0,3},{1,2},{2,1},{3,0},{4,7},{5,6},{6,5},{7,4},{8,11},{9,10},{10,... | collective-permute-start | bytes 1572872 | tf_op jit(solution)/shard_map/ppermute | solution.py:248
  503.0 74.7 %collective-permute-start.49 = (bf16[128,2048]{1,0:T(8,128)(2,1)S(1)}, bf16[128,2048]{1,0:T(8,128)(2,1)S(1)}, u32[]{:S(2)}, u32[]{:S(2)}) collective-permute-start(bf16[128,2048]{1,0:T(8,128)(2,1)S(1)} %get-tuple-element.43), channel_id=1, source_target_pairs={{0,2},{1,3},{2,0},{3,1},{4,6},{5,7},{6,4},{7,5},{8,10},{9,11},{10,... | collective-permute-start | bytes 1572872 | tf_op jit(solution)/shard_map/ppermute | solution.py:248
  526.1 51.6 %collective-permute-start.48 = (bf16[128,2048]{1,0:T(8,128)(2,1)S(1)}, bf16[128,2048]{1,0:T(8,128)(2,1)S(1)}, u32[]{:S(2)}, u32[]{:S(2)}) collective-permute-start(bf16[128,2048]{1,0:T(8,128)(2,1)S(1)} %get-tuple-element.41), channel_id=1, source_target_pairs={{0,1},{1,0},{2,3},{3,2},{4,5},{5,4},{6,7},{7,6},{8,9},{9,8},{10,11... | collective-permute-start | bytes 1572872 | tf_op jit(solution)/shard_map/ppermute | solution.py:248
  570.7 316.7 %collective-permute-start.42 = (bf16[128,2048]{1,0:T(8,128)(2,1)}, bf16[128,2048]{1,0:T(8,128)(2,1)}, u32[]{:S(2)}, u32[]{:S(2)}) collective-permute-start(bf16[128,2048]{1,0:T(8,128)(2,1)} %get-tuple-element.45), channel_id=1, source_target_pairs={{0,3},{1,2},{2,1},{3,0},{4,7},{5,6},{6,5},{7,4},{8,11},{9,10},{10,... | collective-permute-start | bytes 1572872 | tf_op jit(solution)/shard_map/ppermute | solution.py:248
  577.6 8.3 collective-permute-start.72
  582.4 15.5 %collective-permute-start.51 = (bf16[128,2048]{1,0:T(8,128)(2,1)}, bf16[128,2048]{1,0:T(8,128)(2,1)S(1)}, u32[]{:S(2)}, u32[]{:S(2)}) collective-permute-start(bf16[128,2048]{1,0:T(8,128)(2,1)} %get-tuple-element.26), channel_id=1, source_target_pairs={{0,8},{4,12},{8,0},{12,4},{16,24},{20,28},{24,16},{28,20},{1,9},{5... | collective-permute-start | bytes 1572872 | tf_op jit(solution)/shard_map/ppermute | solution.py:248
  582.9 25.6 %collective-permute-start.52 = (bf16[128,2048]{1,0:T(8,128)(2,1)}, bf16[128,2048]{1,0:T(8,128)(2,1)}, u32[]{:S(2)}, u32[]{:S(2)}) collective-permute-start(bf16[128,2048]{1,0:T(8,128)(2,1)} %get-tuple-element.26), channel_id=1, source_target_pairs={{0,16},{4,20},{8,24},{12,28},{16,0},{20,4},{24,8},{28,12},{1,17},{... | collective-permute-start | bytes 1572872 | tf_op jit(solution)/shard_map/ppermute | solution.py:248
  583.4 27.8 %collective-permute-start.53 = (bf16[128,2048]{1,0:T(8,128)(2,1)}, bf16[128,2048]{1,0:T(8,128)(2,1)}, u32[]{:S(2)}, u32[]{:S(2)}) collective-permute-start(bf16[128,2048]{1,0:T(8,128)(2,1)} %get-tuple-element.26), channel_id=1, source_target_pairs={{0,24},{4,28},{8,16},{12,20},{16,8},{20,12},{24,0},{28,4},{1,25},{... | collective-permute-start | bytes 1572872 | tf_op jit(solution)/shard_map/ppermute | solution.py:248
  590.4 28.5 %collective-permute-start.73 = (bf16[2,64,2048]{2,1,0:T(8,128)(2,1)}, bf16[2,64,2048]{2,1,0:T(8,128)(2,1)}, u32[]{:S(2)}, u32[]{:S(2)}) collective-permute-start(bf16[2,64,2048]{2,1,0:T(8,128)(2,1)} %get-tuple-element.61), channel_id=1, source_target_pairs={{0,1},{1,0},{2,3},{3,2},{4,5},{5,4},{6,7},{7,6},{8,9},{9,8},{10,11... | collective-permute-start | bytes 1572872 | tf_op jit(solution)/shard_map/ppermute | solution.py:248
  597.9 38.5 %collective-permute-start.74 = (bf16[2,64,2048]{2,1,0:T(8,128)(2,1)}, bf16[2,64,2048]{2,1,0:T(8,128)(2,1)}, u32[]{:S(2)}, u32[]{:S(2)}) collective-permute-start(bf16[2,64,2048]{2,1,0:T(8,128)(2,1)} %get-tuple-element.62), channel_id=1, source_target_pairs={{0,2},{1,3},{2,0},{3,1},{4,6},{5,7},{6,4},{7,5},{8,10},{9,11},{10,... | collective-permute-start | bytes 1572872 | tf_op jit(solution)/shard_map/ppermute | solution.py:248
  608.5 34.9 %collective-permute-start.75 = (bf16[2,64,2048]{2,1,0:T(8,128)(2,1)}, bf16[2,64,2048]{2,1,0:T(8,128)(2,1)}, u32[]{:S(2)}, u32[]{:S(2)}) collective-permute-start(bf16[2,64,2048]{2,1,0:T(8,128)(2,1)} %get-tuple-element.59), channel_id=1, source_target_pairs={{0,3},{1,2},{2,1},{3,0},{4,7},{5,6},{6,5},{7,4},{8,11},{9,10},{10,... | collective-permute-start | bytes 1572872 | tf_op jit(solution)/shard_map/ppermute | solution.py:248
  614.2 112.6 %collective-permute-start.54 = (bf16[4,128,2048]{2,1,0:T(8,128)(2,1)}, bf16[4,128,2048]{2,1,0:T(8,128)(2,1)}, u32[]{:S(2)}, u32[]{:S(2)}) collective-permute-start(bf16[4,128,2048]{2,1,0:T(8,128)(2,1)} %pad_maximum_fusion.6), channel_id=1, source_target_pairs={{0,4},{4,0},{8,12},{12,8},{16,20},{20,16},{24,28},{28,24},{1,5},{5... | collective-permute-start | bytes 6291464 | tf_op jit(solution)/shard_map/ppermute | solution.py:248
  750.6 105.4 %collective-permute-start.55 = (bf16[4,128,2048]{2,1,0:T(8,128)(2,1)}, bf16[4,128,2048]{2,1,0:T(8,128)(2,1)}, u32[]{:S(2)}, u32[]{:S(2)}) collective-permute-start(bf16[4,128,2048]{2,1,0:T(8,128)(2,1)} %bitcast.161), channel_id=1, source_target_pairs={{0,4},{4,0},{8,12},{12,8},{16,20},{20,16},{24,28},{28,24},{1,5},{5... | collective-permute-start | bytes 6291464 | tf_op jit(solution)/shard_map/ppermute | solution.py:248
  756.8 13.9 %collective-permute-start.61 = (bf16[8,64,384]{2,1,0:T(8,128)(2,1)S(1)}, bf16[8,64,384]{2,1,0:T(8,128)(2,1)S(1)}, u32[]{:S(2)}, u32[]{:S(2)}) collective-permute-start(bf16[8,64,384]{2,1,0:T(8,128)(2,1)S(1)} %get-tuple-element.57), channel_id=1, source_target_pairs={{0,3},{1,2},{2,1},{3,0},{4,7},{5,6},{6,5},{7,4},{8,11},{9,10},{10,... | collective-permute-start | bytes 1179656 | tf_op jit(solution)/shard_map/ppermute | solution.py:248
  759.0 38.5 %collective-permute-start.60 = (bf16[8,64,384]{2,1,0:T(8,128)(2,1)S(1)}, bf16[8,64,384]{2,1,0:T(8,128)(2,1)S(1)}, u32[]{:S(2)}, u32[]{:S(2)}) collective-permute-start(bf16[8,64,384]{2,1,0:T(8,128)(2,1)S(1)} %get-tuple-element.58), channel_id=1, source_target_pairs={{0,2},{1,3},{2,0},{3,1},{4,6},{5,7},{6,4},{7,5},{8,10},{9,11},{10,... | collective-permute-start | bytes 1179656 | tf_op jit(solution)/shard_map/ppermute | solution.py:248
  761.5 36.1 %collective-permute-start.59 = (bf16[8,64,384]{2,1,0:T(8,128)(2,1)S(1)}, bf16[8,64,384]{2,1,0:T(8,128)(2,1)S(1)}, u32[]{:S(2)}, u32[]{:S(2)}) collective-permute-start(bf16[8,64,384]{2,1,0:T(8,128)(2,1)S(1)} %get-tuple-element.56), channel_id=1, source_target_pairs={{0,1},{1,0},{2,3},{3,2},{4,5},{5,4},{6,7},{7,6},{8,9},{9,8},{10,11... | collective-permute-start | bytes 1179656 | tf_op jit(solution)/shard_map/ppermute | solution.py:248
  770.7 30.1 %collective-permute-start.68 = (bf16[64,2048]{1,0:T(8,128)(2,1)S(1)}, bf16[64,2048]{1,0:T(8,128)(2,1)S(1)}, u32[]{:S(2)}, u32[]{:S(2)}) collective-permute-start(bf16[64,2048]{1,0:T(8,128)(2,1)S(1)} %get-tuple-element.66), channel_id=1, source_target_pairs={{0,3},{1,2},{2,1},{3,0},{4,7},{5,6},{6,5},{7,4},{8,11},{9,10},{10,... | collective-permute-start | bytes 786440 | tf_op jit(solution)/shard_map/ppermute | solution.py:248
  797.6 28.1 %collective-permute-start.67 = (bf16[64,2048]{1,0:T(8,128)(2,1)S(1)}, bf16[64,2048]{1,0:T(8,128)(2,1)S(1)}, u32[]{:S(2)}, u32[]{:S(2)}) collective-permute-start(bf16[64,2048]{1,0:T(8,128)(2,1)S(1)} %get-tuple-element.67), channel_id=1, source_target_pairs={{0,2},{1,3},{2,0},{3,1},{4,6},{5,7},{6,4},{7,5},{8,10},{9,11},{10,... | collective-permute-start | bytes 786440 | tf_op jit(solution)/shard_map/ppermute | solution.py:248
  797.6 28.1 %collective-permute-start.66 = (bf16[64,2048]{1,0:T(8,128)(2,1)S(1)}, bf16[64,2048]{1,0:T(8,128)(2,1)S(1)}, u32[]{:S(2)}, u32[]{:S(2)}) collective-permute-start(bf16[64,2048]{1,0:T(8,128)(2,1)S(1)} %get-tuple-element.65), channel_id=1, source_target_pairs={{0,1},{1,0},{2,3},{3,2},{4,5},{5,4},{6,7},{7,6},{8,9},{9,8},{10,11... | collective-permute-start | bytes 786440 | tf_op jit(solution)/shard_map/ppermute | solution.py:248
  800.8 86.6 %collective-permute-start.41 = (bf16[128,2048]{1,0:T(8,128)(2,1)}, bf16[128,2048]{1,0:T(8,128)(2,1)}, u32[]{:S(2)}, u32[]{:S(2)}) collective-permute-start(bf16[128,2048]{1,0:T(8,128)(2,1)} %get-tuple-element.46), channel_id=1, source_target_pairs={{0,2},{1,3},{2,0},{3,1},{4,6},{5,7},{6,4},{7,5},{8,10},{9,11},{10,... | collective-permute-start | bytes 1572872 | tf_op jit(solution)/shard_map/ppermute | solution.py:248
  860.0 16.1 %collective-permute-start.58 = (bf16[128,2048]{1,0:T(8,128)(2,1)}, bf16[128,2048]{1,0:T(8,128)(2,1)}, u32[]{:S(2)}, u32[]{:S(2)}) collective-permute-start(bf16[128,2048]{1,0:T(8,128)(2,1)} %get-tuple-element.39), channel_id=1, source_target_pairs={{0,24},{4,28},{8,16},{12,20},{16,8},{20,12},{24,0},{28,4},{1,25},{... | collective-permute-start | bytes 1572872 | tf_op jit(solution)/shard_map/ppermute | solution.py:248
  862.3 22.7 %collective-permute-start.57 = (bf16[128,2048]{1,0:T(8,128)(2,1)}, bf16[128,2048]{1,0:T(8,128)(2,1)}, u32[]{:S(2)}, u32[]{:S(2)}) collective-permute-start(bf16[128,2048]{1,0:T(8,128)(2,1)} %get-tuple-element.40), channel_id=1, source_target_pairs={{0,16},{4,20},{8,24},{12,28},{16,0},{20,4},{24,8},{28,12},{1,17},{... | collective-permute-start | bytes 1572872 | tf_op jit(solution)/shard_map/ppermute | solution.py:248
  862.8 22.1 %collective-permute-start.56 = (bf16[128,2048]{1,0:T(8,128)(2,1)}, bf16[128,2048]{1,0:T(8,128)(2,1)}, u32[]{:S(2)}, u32[]{:S(2)}) collective-permute-start(bf16[128,2048]{1,0:T(8,128)(2,1)} %get-tuple-element.38), channel_id=1, source_target_pairs={{0,8},{4,12},{8,0},{12,4},{16,24},{20,28},{24,16},{28,20},{1,9},{5... | collective-permute-start | bytes 1572872 | tf_op jit(solution)/shard_map/ppermute | solution.py:248
  876.1 11.3 %collective-permute-start.40 = (bf16[128,2048]{1,0:T(8,128)(2,1)}, bf16[128,2048]{1,0:T(8,128)(2,1)S(1)}, u32[]{:S(2)}, u32[]{:S(2)}) collective-permute-start(bf16[128,2048]{1,0:T(8,128)(2,1)} %get-tuple-element.44), channel_id=1, source_target_pairs={{0,1},{1,0},{2,3},{3,2},{4,5},{5,4},{6,7},{7,6},{8,9},{9,8},{10,11... | collective-permute-start | bytes 1572872 | tf_op jit(solution)/shard_map/ppermute | solution.py:248
  (59 other events, 519.4 us)

commit v2 on v1

--- a/solution.py
+++ b/solution.py
@@ -244,6 +244,46 @@
     )(place, grad, query, key, value, lse, cosine, sine, keydoc, doc)
 
 
+def join_kernel(down_rows, gate_part, up_part, gate_weight, up_weight, gate_ref, up_ref, sum_ref):
+    @pl.when(pl.program_id(0) == 0)
+    def _():
+        sum_ref[...] = jnp.zeros_like(sum_ref)
+
+    for part, weight, out in ((gate_part, gate_weight, gate_ref), (up_part, up_weight, up_ref)):
+        for block in range(part.shape[0]):
+            lanes = slice(block * down_rows, (block + 1) * down_rows)
+            piece = part[block].astype(F32)
+            out[:, lanes] = piece
+            term = piece * weight[:, lanes].astype(F32)
+            sum_ref[...] += jnp.sum(term, axis=1, keepdims=True)
+
+
+def join_pair(pair_grad, gate_weight, up_weight, outer, down_rows):
+    blocks, rows, _ = pair_grad.shape
+    units = gate_weight.shape[1]
+    width = blocks * down_rows
+    shape = jax.ShapeDtypeStruct
+    wide_spec = pl.BlockSpec((rows, width), lambda i: (0, i))
+    return pl.pallas_call(
+        functools.partial(join_kernel, down_rows),
+        grid=(outer,),
+        out_shape=(
+            shape((rows, units), F32), shape((rows, units), F32), shape((rows, 128), F32),
+        ),
+        in_specs=[
+            pl.BlockSpec((blocks, rows, down_rows), lambda i: (0, 0, i)),
+            pl.BlockSpec((blocks, rows, down_rows), lambda i: (0, 0, i + outer)),
+            wide_spec,
+            wide_spec,
+        ],
+        out_specs=(wide_spec, wide_spec, pl.BlockSpec((rows, 128), lambda i: (0, 0))),
+        compiler_params=pltpu.CompilerParams(vmem_limit_bytes=32 * 2**20),
+        cost_estimate=pl.CostEstimate(
+            flops=4 * rows * units, bytes_accessed=16 * rows * units, transcendentals=0
+        ),
+    )(pair_grad, pair_grad, gate_weight, up_weight)
+
+
 def exchange(value, axis, size, step):
     return lax.ppermute(value, axis, [(i, i ^ step) for i in range(size)])
 
@@ -258,8 +298,16 @@
     return lax.dynamic_index_in_dim(value, index, axis, keepdims=False)
 
 
+def after(value, *marks):
+    return lax.optimization_barrier((value,) + marks)[0]
+
+
 def make_program(wide, narrow):
     outer = wide // INNER
+    near_size = INNER * narrow
+    near_groups = [[o * near_size + i for i in range(near_size)] for o in range(outer)]
+    chip_groups = [[c + INNER * o for o in range(outer)] for c in range(INNER)]
+    both = ("wide", "narrow")
 
     def core_swap(value):
         return exchange(value, "wide", wide, 1)
@@ -273,22 +321,34 @@
     def fan_out(value, swap, size):
         return [value] + [swap(value, step) for step in range(1, size)]
 
-    def sum_scatter(parts, swap, size):
-        arrived = [swap(parts[step].astype(BF16), step) for step in range(1, size)]
+    def narrow_gather(value):
+        spread = jnp.broadcast_to(value[None], (narrow,) + value.shape)
+        return lax.all_to_all(spread, "narrow", 0, 0, tiled=True)
+
+    def narrow_sum(total):
+        split = total.reshape(narrow, -1, total.shape[-1])
+        return lax.all_to_all(split, "narrow", 0, 0, tiled=True)
+
+    def with_sibling(first):
+        return jnp.concatenate([first, core_swap(first)], axis=0)
+
+    def join_near(parts):
+        first = jnp.concatenate(parts, axis=0)
+        return jnp.concatenate([first, core_swap(first)], axis=0)
+
+    def near_total(product):
+        arrived = core_swap(product(1).astype(BF16))
+        return (product(0) + arrived.astype(F32)).astype(BF16), arrived
+
+    def scatter(total, swap, size):
+        split = total.reshape(size, -1, total.shape[-1])
+        return [split[0]] + [swap(split[step], step) for step in range(1, size)]
+
+    def add_up(parts):
         total = parts[0].astype(F32)
-        for piece in arrived:
+        for piece in parts[1:]:
             total = total + piece.astype(F32)
         return total
-
-    def gather_near(value, swap, size):
-        first = jnp.stack(fan_out(value, swap, size))
-        return jnp.concatenate([first, core_swap(first)], axis=0).reshape(-1, value.shape[-1])
-
-    def scatter_near(total, swap, size):
-        split = total.reshape(INNER, size, -1, total.shape[-1])
-        arrived = core_swap(split[1].astype(BF16))
-        both = [split[0, step].astype(F32) + arrived[step].astype(F32) for step in range(size)]
-        return sum_scatter(both, swap, size)
 
     def per_device(
         layer_input, output_grad, doc_ids, keep_mask, attention_gain, query_weight, key_weight,
@@ -304,117 +364,109 @@
         key_heads = max(1, heads // group)
         repeat = max(1, group // heads)
         place = lax.axis_index("wide")
-        core = place % INNER
         chip = place // INNER
         layer = lax.axis_index("narrow")
+        core = place % INNER
         place_arg = place.reshape(1).astype(jnp.int32)
+
+        head_cols = heads * HEAD
+        kv_cols = key_heads * HEAD
+
+        def kv_split(weight):
+            parts = weight.reshape(rows, -1, kv_cols)
+            return jnp.repeat(parts, repeat, axis=1)
+
+        packed = jnp.concatenate(
+            [query_weight.reshape(rows, wide, head_cols), kv_split(key_weight), kv_split(value_weight)],
+            axis=2,
+        )
+        cols = packed.shape[2]
+        own_input = layer_input[0]
+        residual = own_input.astype(F32)
+        out_parts = fan_out(out_weight, narrow_swap, narrow)
+        packed = packed.transpose(1, 0, 2)
+        gain_rows = -(-2 * rows // cols) * 8
+        gains = jnp.concatenate([attention_gain, feedforward_gain])
+        gains = jnp.pad(gains, (0, gain_rows * cols - 2 * rows)).reshape(1, gain_rows, cols)
+        gains = jnp.broadcast_to(gains, (wide, gain_rows, cols))
+        packed = jnp.concatenate([packed, gains], axis=1)
+        by_wide = lax.all_to_all(packed, "wide", 0, 0, tiled=True)
+        input_parts = fan_out(after(own_input, by_wide), outer_swap, outer)
+
+        weight_parts = fan_out(after(by_wide, *out_parts), narrow_swap, narrow)
+
+        def for_group(weight):
+            return weight.reshape(rows, outer, near_size, down_rows).transpose(2, 0, 1, 3)
+
+        pair_cols = 2 * outer * down_rows
+        units = pair_cols // 2
+        pair_weight = jnp.stack([for_group(gate_weight), for_group(up_weight)], axis=2)
+        pair_weight = pair_weight.reshape(near_size, rows, pair_cols)
+        pair_weight = after(pair_weight, *weight_parts, *input_parts)
+        column = lax.all_to_all(
+            pair_weight, both, 0, 0, axis_index_groups=near_groups, tiled=True
+        )
+        down = lax.all_gather(
+            down_weight, "wide", axis=0, tiled=True, axis_index_groups=chip_groups
+        )
+
+        all_input = join_near(input_parts)
+        scaled_all, factor_all = normalize(all_input.astype(F32))
+        attention_weight = after(jnp.zeros((wide, narrow, rows, cols), BF16), factor_all)
+        for step, piece in enumerate(weight_parts):
+            attention_weight = put(
+                attention_weight, piece[:, None, :rows], (0, layer ^ step, 0, 0)
+            )
+        attention_weight = attention_weight.reshape(model, cols)
+        lines = jnp.stack([piece[:, rows, : 2 * rows] for piece in weight_parts], axis=1)
+        lines = jnp.stack([pick(lines, layer ^ step, 1) for step in range(narrow)], axis=1)
+        lines = lines.astype(F32)
+        gain_one = lines[:, :, :rows].reshape(1, model)
+        gain_two = lines[:, :, rows:].reshape(1, model)
+
+        out_own = jnp.zeros((narrow, rows, model), BF16)
+        for step, piece in enumerate(out_parts):
+            out_own = put(out_own, piece[None], (layer ^ step, 0, 0))
+        out_own = out_own.reshape(narrow * rows, model)
+
+        grad_out_own = output_grad[0]
+        grad_out_near = narrow_gather(after(grad_out_own, column)).reshape(-1, model)
+
+        own = all_input.shape[0] // INNER
+        half = near_size * tokens // INNER
         documents = doc_ids[0]
         positions = stream_positions(documents)
         angles = jnp.asarray(inverse_rates(HEAD))[:, None] * positions.astype(F32)[None, :]
         cosine, sine = jnp.cos(angles), jnp.sin(angles)
         keydoc = jnp.where(keep_mask[0] > 0, documents, -1)[:, None]
         doc = documents[None, :]
-
-        head_cols = heads * HEAD
-        kv_cols = key_heads * HEAD
-
-        def kv_split(weight):
-            parts = weight.reshape(rows, -1, kv_cols)
-            return jnp.repeat(parts, repeat, axis=1)
-
-        packed = jnp.concatenate(
-            [query_weight.reshape(rows, wide, head_cols), kv_split(key_weight), kv_split(value_weight)],
-            axis=2,
-        )
-        cols = packed.shape[2]
-        packed = packed.reshape(rows, outer, INNER, cols).transpose(2, 1, 0, 3)
-        mine = pick(packed, core)
-        other = core_swap(pick(packed, 1 - core))
-        pair = jnp.stack([mine, other], axis=1)
-        blocks = [pick(pair, chip)] + [
-            outer_swap(pick(pair, chip ^ step), step) for step in range(1, outer)
-        ]
-        by_wide = jnp.zeros((wide, 1, rows, cols), BF16)
-        for step in range(outer):
-            for near in range(INNER):
-                by_wide = put(
-                    by_wide, blocks[step][near][None, None], (place ^ (INNER * step + near), 0, 0, 0)
-                )
-        by_wide = by_wide.reshape(wide, rows, cols)
-        attention_weight = jnp.zeros((wide, narrow, rows, cols), BF16)
-        for step, piece in enumerate(fan_out(by_wide, narrow_swap, narrow)):
-            attention_weight = put(attention_weight, piece[:, None], (0, layer ^ step, 0, 0))
-        attention_weight = attention_weight.reshape(model, cols)
-
-        out_own = jnp.zeros((narrow, rows, model), BF16)
-        for step, piece in enumerate(fan_out(out_weight, narrow_swap, narrow)):
-            out_own = put(out_own, piece[None], (layer ^ step, 0, 0))
-        out_own = out_own.reshape(narrow * rows, model)
-
-        gains = jnp.stack([attention_gain, feedforward_gain]).astype(F32)
-        gain_buffer = jnp.zeros((2, wide, narrow, rows), F32)
-        near_gains = jnp.stack([gains, core_swap(gains)])
-        wide_gains = [near_gains] + [outer_swap(near_gains, s) for s in range(1, outer)]
-        wide_gains = jnp.stack(wide_gains)
-        for far in range(narrow):
-            piece = wide_gains if far == 0 else narrow_swap(wide_gains, far)
-            for step in range(outer):
-                for near in range(INNER):
-                    gain_buffer = put(
-                        gain_buffer,
-                        piece[step, near][:, None, None, :],
-                        (0, place ^ (INNER * step + near), layer ^ far, 0),
-                    )
-        gain_one, gain_two = gain_buffer[0].reshape(1, model), gain_buffer[1].reshape(1, model)
-
-        own_input = layer_input[0]
-        residual = own_input.astype(F32)
-        all_input = gather_near(own_input, outer_swap, outer)
-        normed_one = (normalize(all_input.astype(F32))[0] * gain_one).astype(BF16)
+        normed_one = (scaled_all * gain_one).astype(BF16)
         lin = mm(attention_weight, normed_one, ((0,), (1,)))
         lin = lin.reshape(-1, HEAD, lin.shape[1])
         mixed, query, key, value, lse = attend(
             place_arg, lin, cosine, sine, keydoc, doc, heads, tokens, outer
         )
         mixed = mixed.reshape(head_cols, -1)
-        attended = scatter_near(mm(mixed, out_own, ((0,), (0,))), outer_swap, outer)
-        after_attention = residual + attended
+
+        def out_product(near):
+            return mm(mixed[:, near * own : (near + 1) * own], out_own, ((0,), (0,)))
+
+        attended, _ = near_total(out_product)
+        gate_up = lax.all_gather(
+            after(column.reshape(near_size * rows, pair_cols), down, attended), "wide", axis=0, tiled=True,
+            axis_index_groups=chip_groups,
+        )
+        attended_parts = scatter(attended, outer_swap, outer)
+        attended_parts[0] = after(attended_parts[0], grad_out_near)
+        after_attention = residual + add_up(attended_parts)
         scaled_two, factor_two = normalize(after_attention)
         normed_own = (scaled_two * gain_two).astype(BF16)
 
-        def for_group(weight):
-            return weight.reshape(rows, outer, INNER, narrow, down_rows)
-
-        pair_weight = jnp.stack([for_group(gate_weight), for_group(up_weight)])
-        pair_weight = pair_weight.transpose(3, 4, 1, 0, 2, 5)
-        pair_cols = 2 * outer * down_rows
-        pair_weight = pair_weight.reshape(INNER, narrow, rows, pair_cols)
-        mine = pick(pair_weight, core)
-        other = core_swap(pick(pair_weight, 1 - core))
-        near_pair = jnp.stack([mine, other])
-        column = jnp.zeros((INNER, narrow, rows, pair_cols), BF16)
-        for step in range(narrow):
-            piece = pick(near_pair, layer ^ step, 1)
-            if step:
-                piece = narrow_swap(piece, step)
-            for near in range(INNER):
-                column = put(column, piece[near][None, None], (core ^ near, layer ^ step, 0, 0))
-        gate_up = jnp.zeros((outer, INNER * narrow * rows, pair_cols), BF16)
-        column = column.reshape(INNER * narrow * rows, pair_cols)
-        for step, piece in enumerate(fan_out(column, outer_swap, outer)):
-            gate_up = put(gate_up, piece[None], (chip ^ step, 0, 0))
-        gate_up = gate_up.reshape(model, pair_cols)
-        down = jnp.zeros((outer, down_rows, model), BF16)
-        for step, piece in enumerate(fan_out(down_weight, outer_swap, outer)):
-            down = put(down, piece[None], (chip ^ step, 0, 0))
-        down = down.reshape(outer * down_rows, model)
-
-        grad_out_own = output_grad[0]
-        grad_out = gather_near(grad_out_own, narrow_swap, narrow)
-        normed_two = gather_near(normed_own, narrow_swap, narrow)
-        both = mm(normed_two, gate_up, ((1,), (0,)))
-        units = pair_cols // 2
-        gate, upward = both[:, :units], both[:, units:]
+        normed_near = narrow_gather(normed_own).reshape(-1, model)
+        normed_two = with_sibling(normed_near)
+        grad_out = with_sibling(grad_out_near)
+        pair = mm(normed_two, gate_up, ((1,), (0,)))
+        gate, upward = pair[:, :units], pair[:, units:]
         sigmoid_gate = jax.nn.sigmoid(gate)
         activated = gate * sigmoid_gate
         hidden = (activated * upward).astype(BF16)
@@ -423,20 +475,52 @@
         grad_gate = (grad_hidden * upward * slope).astype(BF16)
         grad_up = (grad_hidden * activated).astype(BF16)
         grad_pair = jnp.concatenate([grad_gate, grad_up], axis=1)
-        grad_two = scatter_near(mm(grad_pair, gate_up, ((1,), (1,))), narrow_swap, narrow)
+
+        def two_product(near):
+            return mm(grad_pair[near * half : (near + 1) * half], gate_up, ((1,), (1,)))
+
+        two_total, _ = near_total(two_product)
+        two_parts = narrow_sum(two_total)
+
+        pair_term = mm(normed_two, after(grad_pair, two_total), ((0,), (0,))).astype(BF16)
+        pair_sum = lax.psum_scatter(
+            pair_term, "wide", scatter_dimension=0, tiled=True, axis_index_groups=chip_groups
+        )
+        late_hidden = after(hidden, pair_term)
+
+        def branch_product(near):
+            return mm(late_hidden[near * half : (near + 1) * half], down, ((1,), (0,)))
+
+        branch_total, _ = near_total(branch_product)
+        down_term = mm(late_hidden, grad_out, ((0,), (0,))).astype(BF16)
+        grad_two = jnp.sum(after(two_parts, branch_total).astype(F32), axis=0)
+        branch_parts = narrow_sum(after(branch_total, grad_two))
+        layer_output = after_attention + jnp.sum(branch_parts.astype(F32), axis=0)
+        down_grad = lax.psum_scatter(
+            after(down_term, pair_sum), "wide", scatter_dimension=0, tiled=True,
+            axis_index_groups=chip_groups,
+        ).astype(F32)
 
         grad_scaled_two = grad_two * gain_two
         grad_middle = grad_out_own.astype(F32) + factor_two * (
             grad_scaled_two
             - scaled_two * jnp.mean(grad_scaled_two * scaled_two, axis=-1, keepdims=True)
         )
-        grad_attention = gather_near(grad_middle.astype(BF16), outer_swap, outer)
-        grad_mixed = mm(out_own, grad_attention, ((1,), (1,))).astype(BF16)
+        middle_parts = fan_out(grad_middle.astype(BF16), outer_swap, outer)
+        middle_parts[0] = after(middle_parts[0], down_term)
+        grad_attention = join_near(middle_parts)
+        grad_mixed = mm(out_own, grad_attention, ((1,), (1,)))
+        grad_mixed = grad_mixed.astype(BF16)
         grad_lin = attend_back(
             place_arg, grad_mixed.reshape(heads, HEAD, -1), query, key, value, lse, cosine, sine,
             keydoc, doc, tokens, outer,
         ).reshape(cols, -1)
-        grad_one = scatter_near(mm(grad_lin, attention_weight, ((0,), (1,))), outer_swap, outer)
+
+        def one_product(near):
+            return mm(grad_lin[:, near * own : (near + 1) * own], attention_weight, ((0,), (1,)))
+
+        one_total, one_swapped = near_total(one_product)
+        grad_one = add_up(scatter(one_total, outer_swap, outer))
         scaled_one, factor_one = normalize(residual)
         grad_scaled_one = grad_one * gain_one
         input_grad = grad_middle + factor_one * (
@@ -444,62 +528,32 @@
             - scaled_one * jnp.mean(grad_scaled_one * scaled_one, axis=-1, keepdims=True)
         )
 
-        branch = scatter_near(mm(hidden, down, ((1,), (0,))), narrow_swap, narrow)
-        layer_output = after_attention + branch
-
-        down_term = mm(hidden, grad_out, ((0,), (0,))).reshape(outer, down_rows, model)
-        down_grad = sum_scatter(
-            [pick(down_term, chip ^ step) for step in range(outer)], outer_swap, outer
-        )
-        pair_term = mm(normed_two, grad_pair, ((0,), (0,))).reshape(outer, -1, pair_cols)
-        pair_sum = sum_scatter(
-            [pick(pair_term, chip ^ step) for step in range(outer)], outer_swap, outer
-        )
-        pair_sum = pair_sum.astype(BF16).reshape(INNER, narrow, rows, pair_cols)
-        mine = pick(pair_sum, core)
-        other = core_swap(pick(pair_sum, 1 - core))
-        near_pair = jnp.stack([mine, other])
-        pair_grad = jnp.zeros((2, rows, outer, INNER, narrow, down_rows), F32)
-        for step in range(narrow):
-            piece = pick(near_pair, layer ^ step, 1)
-            if step:
-                piece = narrow_swap(piece, step)
-            piece = piece.astype(F32).reshape(INNER, rows, 2, outer, down_rows)
-            piece = piece.transpose(0, 2, 1, 3, 4)
-            for near in range(INNER):
-                pair_grad = put(
-                    pair_grad,
-                    piece[near][:, :, :, None, None, :],
-                    (0, 0, 0, core ^ near, layer ^ step, 0),
-                )
-        pair_grad = pair_grad.reshape(2, rows, -1)
-        gate_grad, up_grad = pair_grad[0], pair_grad[1]
-        gain_two_grad = (
-            jnp.sum(gate_grad * gate_weight.astype(F32), axis=1)
-            + jnp.sum(up_grad * up_weight.astype(F32), axis=1)
-        ) / feedforward_gain.astype(F32)
-
-        out_term = mm(mixed, grad_attention, ((1,), (0,))).reshape(narrow, rows, model)
-        out_grad = sum_scatter(
-            [pick(out_term, layer ^ step) for step in range(narrow)], narrow_swap, narrow
-        )
-        lin_term = mm(normed_one, grad_lin, ((0,), (1,))).reshape(wide, narrow, rows, cols)
-        lin_sum = sum_scatter(
-            [pick(lin_term, layer ^ step, 1) for step in range(narrow)], narrow_swap, narrow
-        )
-        lin_sum = lin_sum.astype(BF16).reshape(outer, INNER, rows, cols)
-        mine = pick(lin_sum, core, 1)
-        other = core_swap(pick(lin_sum, 1 - core, 1))
-        pair = jnp.stack([mine, other], axis=1)
-        lin_grad = jnp.zeros((wide, rows, cols), F32)
-        for step in range(outer):
-            piece = pick(pair, chip ^ step)
-            if step:
-                piece = outer_swap(piece, step)
-            for near in range(INNER):
-                lin_grad = put(
-                    lin_grad, piece[near][None].astype(F32), (place ^ (INNER * step + near), 0, 0)
-                )
+        pair_sum = after(pair_sum, branch_parts).reshape(near_size, rows, pair_cols)
+        pair_grad = lax.all_to_all(pair_sum, both, 0, 0, axis_index_groups=near_groups, tiled=True)
+        if down_rows % 128 == 0:
+            gate_grad, up_grad, gain_sum = join_pair(
+                pair_grad, gate_weight, up_weight, outer, down_rows
+            )
+            gain_sum = gain_sum[:, 0]
+        else:
+            pair_grad = pair_grad.reshape(near_size, rows, 2, outer, down_rows)
+            pair_grad = pair_grad.transpose(2, 1, 3, 0, 4).reshape(2, rows, -1).astype(F32)
+            gate_grad, up_grad = pair_grad[0], pair_grad[1]
+            gain_sum = jnp.sum(gate_grad * gate_weight.astype(F32), axis=1) + jnp.sum(
+                up_grad * up_weight.astype(F32), axis=1
+            )
+        gain_two_grad = gain_sum / feedforward_gain.astype(F32)
+
+        late_lin = after(grad_lin, one_swapped)
+        lin_term = mm(normed_one, late_lin, ((0,), (1,))).astype(BF16)
+        lin_term = lin_term.reshape(wide, narrow, rows, cols).transpose(1, 0, 2, 3)
+        lin_term = after(lin_term, pair_grad)
+        lin_sum = jnp.sum(lax.all_to_all(lin_term, "narrow", 0, 0, tiled=True).astype(F32), axis=0)
+        lin_grad = lax.all_to_all(lin_sum.astype(BF16), "wide", 0, 0, tiled=True).astype(F32)
+        out_term = mm(mixed, after(grad_attention, late_lin), ((1,), (0,))).astype(BF16)
+        out_term = out_term.reshape(narrow, rows, model)
+        out_grad = jnp.sum(lax.all_to_all(out_term, "narrow", 0, 0, tiled=True).astype(F32), axis=0)
+
         query_grad = lin_grad[:, :, :head_cols].transpose(1, 0, 2).reshape(rows, -1)
 
         def kv_join(part):

time: 904 us -> 591 us (0.65)
  local copies, waits for them, and re-layouts: 241 us -> 53.5 us
  waiting for transfers between devices: 334 us -> 235 us
  starting transfers between devices: 135 us -> 64.9 us
  blocking collectives: 0 us -> 51.9 us
  other arithmetic: 73 us -> 34.4 us
  matrix products: 81.6 us -> 102 us
  between operations: 2.58 us -> 15.3 us
    ppermute x79 -> x26, waiting for transfers between devices: 334 us -> 83 us  [exchange(): return lax.ppermute(value, axis, [(i, i ^ step) for i in range(size)])]
    all_to_all x0 -> x9, waiting for transfers between devices: none -> 152 us  [the longest x1 42.3 us: narrow_gather(): return lax.all_to_all(spread, 'narrow', 0, 0, tiled=True)]
    ppermute x79 -> x26, starting transfers between devices: 135 us -> 26.5 us  [exchange(): return lax.ppermute(value, axis, [(i, i ^ step) for i in range(size)])]
    dynamic_update_slice x79 -> x8, local copies, waits for them, and re-layouts: 106 us -> 7.25 us  [put(): lax.dynamic_update_slice(buffer, piece, tuple((jnp.asarray(i, jnp.int32)...]
    all_to_all x0 -> x1, blocking collectives: none -> 51.9 us  [narrow_gather(): return lax.all_to_all(spread, 'narrow', 0, 0, tiled=True)]
    all_to_all x0 -> x9, starting transfers between devices: none -> 38 us  [the longest x2 9.16 us: narrow_sum(): return lax.all_to_all(split, 'narrow', 0, 0, tiled=True)]
    convert_element_type x13 -> x5, other arithmetic: 26.9 us -> 4.16 us  [the longest x1 2.79 us: per_device(): down_grad = lax.psum_scatter(after(down_term, pair_sum), 'wide', scatter_...]
    dot_general x12 -> x16, matrix products: 81.6 us -> 102 us  [mm(): lax.dot_general(left, right, (dims, ((), ())), preferred_element_type=F32)]
  transfers between devices with their start and end apart: 79 -> 39, of which waited for: 33 -> 21; matrix products, arithmetic and copies ran while one was open for 37% -> 23% of each run, Pallas kernels for 3% -> 5%
where the time goes in v2:
time: 591 us; the launch traced here: 584 us
  waiting for transfers between devices  235 us (40%)
  matrix products  102 us (17%)
  starting transfers between devices  64.9 us (11%)
  local copies, waits for them, and re-layouts  53.5 us (9%)
  blocking collectives  51.9 us (9%)
  other arithmetic  34.4 us (6%)
  Pallas kernels  26.9 us (5%)
  between operations  15.3 us (3%)
    dot_general x16, matrix products, mm(): lax.dot_general(left, right, (dims, ((), ())), preferred_element_type=F32)  102 us
    ppermute x26, waiting for transfers between devices, exchange(): return lax.ppermute(value, axis, [(i, i ^ step) for i in range(size)])  83 us
    all_to_all x1, blocking collectives, narrow_gather(): return lax.all_to_all(spread, 'narrow', 0, 0, tiled=True)  51.9 us
    all_to_all x1, waiting for transfers between devices, narrow_gather(): return lax.all_to_all(spread, 'narrow', 0, 0, tiled=True)  42.3 us
    all_to_all x2, waiting for transfers between devices, narrow_sum(): return lax.all_to_all(split, 'narrow', 0, 0, tiled=True)  35.9 us
    ppermute x26, starting transfers between devices, exchange(): return lax.ppermute(value, axis, [(i, i ^ step) for i in range(size)])  26.5 us
    all_to_all x1, waiting for transfers between devices, per_device(): lax.all_to_all(lin_term, 'narrow', 0, 0, tiled=True).astype(F32)  25.1 us
    unnamed x128, local copies, waits for them, and re-layouts  21.5 us
  transfers between devices with their start and end apart: 39, of which 21 were waited for; matrix products, arithmetic and copies ran while one was open for 23% of the time, Pallas kernels for 5%

profile of v2, /device:TPU:0, one launch (start us, length us, event | category | flops | bytes accessed | tf_op | source)
XLA Modules:
  0.0 583.8 jit_solution(11615355889778643909)
XLA Ops:
  7.3 5.1 collective-permute-start.2
  17.8 4.1 all-to-all-start
  24.0 2.7 pad_maximum_fusion.8
  26.8 4.5 reshape.194
  32.9 2.1 collective-permute-done.1
  36.0 2.5 collective-permute-start.8
  40.5 3.3 collective-permute-start.5
  45.1 8.7 %collective-permute-done.8 = bf16[128,2048]{1,0:T(8,128)(2,1)S(1)} collective-permute-done((bf16[128,2048]{1,0:T(8,128)(2,1)S(1)}, bf16[128,2048]{1,0:T(8,128)(2,1)S(1)}, u32[]{:S(2)}, u32[]{:S(2)}) %collective-permute-start.8) | collective-permute-done | bytes 524320 | tf_op jit(solution)/shard_map/ppermute | solution.py:288
  55.3 9.1 %collective-permute-done.7 = bf16[128,2048]{1,0:T(8,128)(2,1)S(1)} collective-permute-done((bf16[128,2048]{1,0:T(8,128)(2,1)S(1)}, bf16[128,2048]{1,0:T(8,128)(2,1)S(1)}, u32[]{:S(2)}, u32[]{:S(2)}) %collective-permute-start.7) | collective-permute-done | bytes 524320 | tf_op jit(solution)/shard_map/ppermute | solution.py:288
  69.1 10.5 %collective-permute-done.4 = bf16[8,72,384]{2,1,0:T(8,128)(2,1)S(1)} collective-permute-done((bf16[8,72,384]{2,1,0:T(8,128)(2,1)}, bf16[8,72,384]{2,1,0:T(8,128)(2,1)S(1)}, u32[]{:S(2)}, u32[]{:S(2)}) %collective-permute-start.4) | collective-permute-done | bytes 442400 | tf_op jit(solution)/shard_map/ppermute | solution.py:288
  86.3 4.3 all-to-all-start.1
  92.8 1.9 constant_dynamic-update-slice_fusion.2
  95.6 3.4 constant_dynamic-update-slice_fusion
  98.9 3.2 fusion
  104.3 11.1 %shard_map.221 = (bf16[4,64,1024]{2,1,0:T(8,128)(2,1)S(1)}, bf16[4,64,1024]{2,1,0:T(8,128)(2,1)S(1)}, bf16[1,64,1024]{2,1,0:T(8,128)(2,1)S(1)}, bf16[1,64,1024]{2,1,0:T(8,128)(2,1)S(1)}, f32[4,1,1024]{2,1,0:T(1,128)S(1)}) custom-call(s32[1]{0:T(128)} %bitcast.1.place_ref, f32[6,64,1024]{2,1,0:T(8,128)S(1)} %fusion.3.lin_ref, ...), custom_call_target="tpu_custom_call" | custom-call | flops 1073741824 | bytes 3145728 | tf_op jit(solution)/shard_map/pallas_call | solution.py:196
  118.8 3.8 collective-permute-done.10
  122.6 2.1 add_convert_fusion.3
  124.6 14.7 %all-to-all-done.1 = bf16[8,64,2048]{2,1,0:T(8,128)(2,1)} async-done(((bf16[8,64,2048]{2,1,0:T(8,128)(2,1)}), bf16[8,64,2048]{2,1,0:T(8,128)(2,1)}, u32[]{:S(2)}, u32[]{:S(2)}) %all-to-all-start.1) | async-done | bytes 2097184 | tf_op jit(solution)/shard_map/all_to_all | solution.py:406
  140.9 4.5 all-to-all-start.2
  145.4 3.1 fusion.51
  148.5 2.6 collective-permute-start.13
  152.1 42.3 %all-to-all-done.2 = bf16[4,128,2048]{2,1,0:T(8,128)(2,1)} async-done(((bf16[4,128,2048]{2,1,0:T(8,128)(2,1)}), bf16[4,128,2048]{2,1,0:T(8,128)(2,1)}, u32[]{:S(2)}, u32[]{:S(2)}) %all-to-all-start.2) | async-done | bytes 2097184 | tf_op jit(solution)/shard_map/all_to_all | solution.py:326
  196.0 2.4 multiply_reduce_fusion.1
  198.8 51.9 %all_to_all.50 = bf16[4,128,2048]{2,1,0:T(8,128)(2,1)S(1)} all-to-all(bf16[4,128,2048]{2,1,0:T(8,128)(2,1)S(1)} %broadcast_in_dim.94), channel_id=1, replica_groups=mesh['wide'=8,'narrow'=4] {'narrow'}, dimensions={0} | all-to-all | bytes 4194304 | tf_op jit(solution)/shard_map/all_to_all | solution.py:326
  252.5 6.7 %collective-permute-done.14 = bf16[512,2048]{1,0:T(8,128)(2,1)} collective-permute-done((bf16[512,2048]{1,0:T(8,128)(2,1)S(1)}, bf16[512,2048]{1,0:T(8,128)(2,1)}, u32[]{:S(2)}, u32[]{:S(2)}) %collective-permute-start.14) | collective-permute-done | bytes 2097184 | tf_op jit(solution)/shard_map/ppermute | solution.py:288
  259.3 14.5 %fusion.7 = f32[1024,2048]{1,0:T(8,128)} fusion(bf16[2048,2048]{1,0:T(8,128)(2,1)} %all-gather.5.cloned.1.call-done, bf16[512,2048]{1,0:T(8,128)(2,1)} %collective-permute-done.14, bf16[512,2048]{1,0:T(8,128)(2,1)} %bitcast.141), kind=kOutput, calls=%fused_computation.33 | convolution fusion | flops 8598323200 | bytes 20971520 | tf_op jit(solution)/shard_map/dot_general | solution.py:47
  273.7 13.0 %multiply_convert_fusion.1 = (bf16[1024,1024]{1,0:T(8,128)(2,1)S(1)}, bf16[1024,1024]{1,0:T(8,128)(2,1)S(1)}, bf16[1024,1024]{1,0:T(8,128)(2,1)}) fusion(f32[1024,2048]{1,0:T(8,128)} %fusion.7, bf16[1024,2048]{1,0:T(8,128)(2,1)} %all-gather.3.cloned.1.call-done, bf16[512,2048]{1,0:T(8,128)(2,1)} %collective-permute-done.15, bf16[512,2048]{1,0:T(8,128)(2,1)} %bitcast.26), kind=kOutput, calls=%fused_computation.21 | convolution fusion | flops 4319084544 | bytes 23068672 | tf_op jit(solution)/shard_map/dot_general | solution.py:47
  286.8 9.3 %convolution_convert_fusion.5 = bf16[512,2048]{1,0:T(8,128)(2,1)} fusion(bf16[2048,2048]{1,0:T(8,128)(2,1)} %all-gather.5.cloned.1.call-done, bf16[1024,1024]{1,0:T(8,128)(2,1)S(1)} %get-tuple-element.61, bf16[1024,1024]{1,0:T(8,128)(2,1)S(1)} %get-tuple-element.62), kind=kOutput, calls=%fused_computation.30 | convolution fusion | flops 4300210176 | bytes 14680064 | tf_op jit(solution)/shard_map/dot_general | solution.py:47
  296.7 3.8 collective-permute-done.16
  300.4 9.5 %add_convert_fusion.2 = bf16[512,2048]{1,0:T(8,128)(2,1)} fusion(bf16[512,2048]{1,0:T(8,128)(2,1)S(1)} %collective-permute-done.16, bf16[2048,2048]{1,0:T(8,128)(2,1)} %all-gather.5.cloned.1.call-done, bf16[1024,1024]{1,0:T(8,128)(2,1)S(1)} %get-tuple-element.61, bf16[1024,1024]{1,0:T(8,128)(2,1)S(1)} %get-tuple-element.62), kind=kOutput, calls=%fused_computation.19 | convolution fusion | flops 4302307328 | bytes 16777216 | tf_op jit(solution)/shard_map/dot_general | solution.py:47
  310.0 12.9 %convolution_convert_fusion = bf16[2048,2048]{1,0:T(8,128)(2,1)} fusion(bf16[1024,2048]{1,0:T(8,128)(2,1)S(1)} %pad_maximum_fusion, bf16[512,2048]{1,0:T(8,128)(2,1)} %collective-permute-done.14, bf16[512,2048]{1,0:T(8,128)(2,1)S(1)} %bitcast.142), kind=kOutput, calls=%fused_computation.5 | convolution fusion | flops 8602517504 | bytes 16777216 | tf_op jit(solution)/shard_map/dot_general | solution.py:47
  323.0 4.5 all-to-all-start.4
  327.5 5.3 convolution_convert_fusion.2
  333.2 3.9 collective-permute-done.17
  337.0 3.7 add_convert_fusion.1
  340.7 35.6 %all-to-all-done.4 = bf16[4,128,2048]{2,1,0:T(8,128)(2,1)} async-done(((bf16[4,128,2048]{2,1,0:T(8,128)(2,1)}), bf16[4,128,2048]{2,1,0:T(8,128)(2,1)}, u32[]{:S(2)}, u32[]{:S(2)}) %all-to-all-start.4) | async-done | bytes 2097184 | tf_op jit(solution)/shard_map/all_to_all | solution.py:330
  376.3 2.1 convert_reduce_fusion.1
  383.9 4.7 all-to-all-start.5
  388.6 9.5 %convolution_convert_fusion.1 = bf16[1024,2048]{1,0:T(8,128)(2,1)} fusion(bf16[1024,1024]{1,0:T(8,128)(2,1)} %get-tuple-element.43, bf16[512,2048]{1,0:T(8,128)(2,1)} %collective-permute-done.15, bf16[512,2048]{1,0:T(8,128)(2,1)} %bitcast.26), kind=kOutput, calls=%fused_computation.26 | convolution fusion | flops 4305453056 | bytes 10485760 | tf_op jit(solution)/shard_map/dot_general | solution.py:47
  398.1 9.1 %collective-permute-done.20 = bf16[128,2048]{1,0:T(8,128)(2,1)S(1)} collective-permute-done((bf16[128,2048]{1,0:T(8,128)(2,1)}, bf16[128,2048]{1,0:T(8,128)(2,1)S(1)}, u32[]{:S(2)}, u32[]{:S(2)}) %collective-permute-start.20) | collective-permute-done | bytes 524320 | tf_op jit(solution)/shard_map/ppermute | solution.py:288
  407.2 10.3 %collective-permute-done.19 = bf16[128,2048]{1,0:T(8,128)(2,1)S(1)} collective-permute-done((bf16[128,2048]{1,0:T(8,128)(2,1)}, bf16[128,2048]{1,0:T(8,128)(2,1)S(1)}, u32[]{:S(2)}, u32[]{:S(2)}) %collective-permute-start.19) | collective-permute-done | bytes 524320 | tf_op jit(solution)/shard_map/ppermute | solution.py:288
  417.5 10.9 %collective-permute-done.18 = bf16[128,2048]{1,0:T(8,128)(2,1)S(1)} collective-permute-done((bf16[128,2048]{1,0:T(8,128)(2,1)}, bf16[128,2048]{1,0:T(8,128)(2,1)S(1)}, u32[]{:S(2)}, u32[]{:S(2)}) %collective-permute-start.18) | collective-permute-done | bytes 524320 | tf_op jit(solution)/shard_map/ppermute | solution.py:288
  435.8 3.6 all-to-all-start.6
  439.6 3.9 convolution_convert_fusion.8
  443.5 12.9 %shard_map.222 = bf16[6,64,1024]{2,1,0:T(8,128)(2,1)S(1)} custom-call(s32[1]{0:T(128)} %bitcast.1.place_ref, bf16[4,64,1024]{2,1,0:T(8,128)(2,1)S(1)} %bitcast.122, bf16[4,64,1024]{2,1,0:T(8,128)(2,1)S(1)} %copy-done.10, bf16[1,64,1024]{2,1,0:T(8,128)(2,1)S(1)} %copy-done.12, bf16[1,64,1024]{2,1,0:T(8,128)(2,1)S(1)} %copy-done.14, ...), custom_call_target="tpu_custom_call" | custom-call | flops 2684354560 | bytes 3145728 | tf_op jit(solution)/shard_map/pallas_call | solution.py:225
  456.4 2.7 convolution_convert_fusion.4
  459.6 3.9 collective-permute-done.22
  463.5 5.1 convolution_convert_fusion.6
  469.9 18.1 %all-to-all-done.6.gate_part.up_part = bf16[8,64,2048]{2,1,0:T(8,128)(2,1)S(1)} async-done(((bf16[8,64,2048]{2,1,0:T(8,128)(2,1)}), bf16[8,64,2048]{2,1,0:T(8,128)(2,1)S(1)}, u32[]{:S(2)}, u32[]{:S(2)}) %all-to-all-start.6) | async-done | bytes 2097184 | tf_op jit(solution)/shard_map/all_to_all | solution.py:532
  488.0 4.4 all-to-all-start.7
  492.3 3.4 add_convert_fusion
  497.8 2.1 collective-permute-start.25
  500.5 4.5 convolution_convert_fusion.7
  505.1 25.1 %all-to-all-done.7 = bf16[4,8,64,384]{3,2,1,0:T(8,128)(2,1)} async-done(((bf16[4,8,64,384]{3,2,1,0:T(8,128)(2,1)}), bf16[4,8,64,384]{3,2,1,0:T(8,128)(2,1)}, u32[]{:S(2)}, u32[]{:S(2)}) %all-to-all-start.7) | async-done | bytes 1572896 | tf_op jit(solution)/shard_map/all_to_all | solution.py:551
  530.1 4.5 all-to-all-start.9
  534.7 2.1 convert_reduce_fusion
  536.8 2.0 fusion.19
  538.9 4.5 fusion.31
  543.3 2.5 reduce_sum.146
  545.9 14.6 %all-to-all-done.9 = bf16[4,64,2048]{2,1,0:T(8,128)(2,1)} async-done(((bf16[4,64,2048]{2,1,0:T(8,128)(2,1)}), bf16[4,64,2048]{2,1,0:T(8,128)(2,1)}, u32[]{:S(2)}, u32[]{:S(2)}) %all-to-all-start.9) | async-done | bytes 1048608 | tf_op jit(solution)/shard_map/all_to_all | solution.py:555
  560.4 3.5 all-to-all-start.8
  563.9 2.2 convert_reduce_fusion.2
  567.3 2.9 shard_map.223
  574.0 2.8 convert_element_type.211
  (244 shorter events, 64.3 us)
Async XLA Ops:
  7.2 14.8 %copy-start.8 = (s32[1,1024]{1,0:T(1,128)S(1)}, s32[1,1024]{1,0:T(1,128)}, u32[]{:S(2)}) copy-start(s32[1,1024]{1,0:T(1,128)} %doc_ref.3) | copy-start | bytes 12292
  7.2 15.0 %copy-start.47 = (s32[1,1024]{1,0:T(1,128)S(1)}, s32[1,1024]{1,0:T(1,128)}, u32[]{:S(2)}) copy-start(s32[1,1024]{1,0:T(1,128)} %param.17) | copy-start | bytes 12292
  7.2 15.0 %copy-start = (bf16[64,8192]{1,0:T(8,128)(2,1)S(1)}, bf16[64,8192]{1,0:T(8,128)(2,1)}, u32[]{:S(2)}) copy-start(bf16[64,8192]{1,0:T(8,128)(2,1)} %up_weight.1) | copy-start | bytes 3145732
  7.2 15.3 %copy-start.2 = (bf16[64,8192]{1,0:T(8,128)(2,1)S(1)}, bf16[64,8192]{1,0:T(8,128)(2,1)}, u32[]{:S(2)}) copy-start(bf16[64,8192]{1,0:T(8,128)(2,1)} %gate_weight.1) | copy-start | bytes 3145732
  7.2 132.1 %all-gather.3.cloned.1.call-start = ((), (), s32[]{:S(2)}) async-start(), calls=%async_computation.12 | async-start | bytes 5242880 | tf_op jit(solution)/shard_map/all_gather | solution.py:409
  7.3 32.3 %collective-permute-start.2 = (bf16[64,2048]{1,0:T(8,128)(2,1)}, bf16[64,2048]{1,0:T(8,128)(2,1)}, u32[]{:S(2)}, u32[]{:S(2)}) collective-permute-start(bf16[64,2048]{1,0:T(8,128)(2,1)} %param.22), channel_id=1, source_target_pairs={{0,3},{1,2},{2,1},{3,0},{4,7},{5,6},{6,5},{7,4},{8,11},{9,10},{10,... | collective-permute-start | bytes 786440 | tf_op jit(solution)/shard_map/ppermute | solution.py:288
  12.4 22.6 %collective-permute-start.1 = (bf16[64,2048]{1,0:T(8,128)(2,1)}, bf16[64,2048]{1,0:T(8,128)(2,1)}, u32[]{:S(2)}, u32[]{:S(2)}) collective-permute-start(bf16[64,2048]{1,0:T(8,128)(2,1)} %param.22), channel_id=1, source_target_pairs={{0,2},{1,3},{2,0},{3,1},{4,6},{5,7},{6,4},{7,5},{8,10},{9,11},{10,... | collective-permute-start | bytes 786440 | tf_op jit(solution)/shard_map/ppermute | solution.py:288
  12.4 19.5 %collective-permute-start = (bf16[64,2048]{1,0:T(8,128)(2,1)}, bf16[64,2048]{1,0:T(8,128)(2,1)}, u32[]{:S(2)}, u32[]{:S(2)}) collective-permute-start(bf16[64,2048]{1,0:T(8,128)(2,1)} %param.22), channel_id=1, source_target_pairs={{0,1},{1,0},{2,3},{3,2},{4,5},{5,4},{6,7},{7,6},{8,9},{9,8},{10,11... | collective-permute-start | bytes 786440 | tf_op jit(solution)/shard_map/ppermute | solution.py:288
  17.8 18.2 %all-to-all-start = ((bf16[8,72,384]{2,1,0:T(8,128)(2,1)}), bf16[8,72,384]{2,1,0:T(8,128)(2,1)}, u32[]{:S(2)}, u32[]{:S(2)}) async-start(bf16[8,72,384]{2,1,0:T(8,128)(2,1)} %copy.79), calls=%async_computation | async-start | bytes 884736 | tf_op jit(solution)/shard_map/all_to_all | solution.py:393
  23.9 7.4 %copy-start.54 = (f32[32]{0:T(128)S(1)}, f32[32]{0:T(128)}, u32[]{:S(2)}) copy-start(f32[32]{0:T(128)} %constant.54.clone) | copy-start | bytes 388
  23.9 12.1 %copy-start.20 = (bf16[1,128,2048]{2,1,0:T(8,128)(2,1)S(1)}, bf16[1,128,2048]{2,1,0:T(8,128)(2,1)}, u32[]{:S(2)}) copy-start(bf16[1,128,2048]{2,1,0:T(8,128)(2,1)} %param.14) | copy-start | bytes 1572868
  31.8 72.5 %copy-start.6 = (f32[32,1024]{1,0:T(8,128)}, f32[32,1024]{1,0:T(8,128)S(1)}, u32[]{:S(2)}) copy-start(f32[32,1024]{1,0:T(8,128)S(1)} %get-tuple-element.83.cos_ref) | copy-start | bytes 393220
  36.0 17.8 %collective-permute-start.8 = (bf16[128,2048]{1,0:T(8,128)(2,1)S(1)}, bf16[128,2048]{1,0:T(8,128)(2,1)S(1)}, u32[]{:S(2)}, u32[]{:S(2)}) collective-permute-start(bf16[128,2048]{1,0:T(8,128)(2,1)S(1)} %bitcast.126), channel_id=1, source_target_pairs={{0,24},{4,28},{8,16},{12,20},{16,8},{20,12},{24,0},{28,4},{1,25},{... | collective-permute-start | bytes 1572872 | tf_op jit(solution)/shard_map/ppermute | solution.py:288
  38.5 25.9 %collective-permute-start.7 = (bf16[128,2048]{1,0:T(8,128)(2,1)S(1)}, bf16[128,2048]{1,0:T(8,128)(2,1)S(1)}, u32[]{:S(2)}, u32[]{:S(2)}) collective-permute-start(bf16[128,2048]{1,0:T(8,128)(2,1)S(1)} %bitcast.127), channel_id=1, source_target_pairs={{0,16},{4,20},{8,24},{12,28},{16,0},{20,4},{24,8},{28,12},{1,17},{... | collective-permute-start | bytes 1572872 | tf_op jit(solution)/shard_map/ppermute | solution.py:288
  39.0 25.6 %collective-permute-start.6 = (bf16[128,2048]{1,0:T(8,128)(2,1)S(1)}, bf16[128,2048]{1,0:T(8,128)(2,1)S(1)}, u32[]{:S(2)}, u32[]{:S(2)}) collective-permute-start(bf16[128,2048]{1,0:T(8,128)(2,1)S(1)} %bitcast.128), channel_id=1, source_target_pairs={{0,8},{4,12},{8,0},{12,4},{16,24},{20,28},{24,16},{28,20},{1,9},{5... | collective-permute-start | bytes 1572872 | tf_op jit(solution)/shard_map/ppermute | solution.py:288
  40.5 27.8 %collective-permute-start.5 = (bf16[8,72,384]{2,1,0:T(8,128)(2,1)}, bf16[8,72,384]{2,1,0:T(8,128)(2,1)S(1)}, u32[]{:S(2)}, u32[]{:S(2)}) collective-permute-start(bf16[8,72,384]{2,1,0:T(8,128)(2,1)} %all-to-all-done), channel_id=1, source_target_pairs={{0,3},{1,2},{2,1},{3,0},{4,7},{5,6},{6,5},{7,4},{8,11},{9,10},{10,... | collective-permute-start | bytes 1327112 | tf_op jit(solution)/shard_map/ppermute | solution.py:288
  43.8 35.8 %collective-permute-start.4 = (bf16[8,72,384]{2,1,0:T(8,128)(2,1)}, bf16[8,72,384]{2,1,0:T(8,128)(2,1)S(1)}, u32[]{:S(2)}, u32[]{:S(2)}) collective-permute-start(bf16[8,72,384]{2,1,0:T(8,128)(2,1)} %all-to-all-done), channel_id=1, source_target_pairs={{0,2},{1,3},{2,0},{3,1},{4,6},{5,7},{6,4},{7,5},{8,10},{9,11},{10,... | collective-permute-start | bytes 1327112 | tf_op jit(solution)/shard_map/ppermute | solution.py:288
  53.8 26.6 %collective-permute-start.3 = (bf16[8,72,384]{2,1,0:T(8,128)(2,1)}, bf16[8,72,384]{2,1,0:T(8,128)(2,1)S(1)}, u32[]{:S(2)}, u32[]{:S(2)}) collective-permute-start(bf16[8,72,384]{2,1,0:T(8,128)(2,1)} %all-to-all-done), channel_id=1, source_target_pairs={{0,1},{1,0},{2,3},{3,2},{4,5},{5,4},{6,7},{7,6},{8,9},{9,8},{10,11... | collective-permute-start | bytes 1327112 | tf_op jit(solution)/shard_map/ppermute | solution.py:288
  66.7 28.9 %collective-permute-start.9 = (bf16[512,2048]{1,0:T(8,128)(2,1)}, bf16[512,2048]{1,0:T(8,128)(2,1)}, u32[]{:S(2)}, u32[]{:S(2)}) collective-permute-start(bf16[512,2048]{1,0:T(8,128)(2,1)} %pad_maximum_fusion.7), channel_id=1, source_target_pairs={{0,4},{4,0},{8,12},{12,8},{16,20},{20,16},{24,28},{28,24},{1,5},{5... | collective-permute-start | bytes 6291464 | tf_op jit(solution)/shard_map/ppermute | solution.py:288
  81.4 20.8 %copy-start.45 = (f32[2048]{0:T(1024)}, f32[2048]{0:T(1024)S(1)}, u32[]{:S(2)}) copy-start(f32[2048]{0:T(1024)S(1)} %mul.147) | copy-start | bytes 24580
  84.6 19.7 %copy-start.18 = (bf16[8,4,64,384]{3,2,1,0:T(8,128)(2,1)}, bf16[8,4,64,384]{3,2,1,0:T(8,128)(2,1)S(1)}, u32[]{:S(2)}) copy-start(bf16[8,4,64,384]{3,2,1,0:T(8,128)(2,1)S(1)} %fusion.34) | copy-start | bytes 4718596
  86.3 52.9 %all-to-all-start.1 = ((bf16[8,64,2048]{2,1,0:T(8,128)(2,1)}), bf16[8,64,2048]{2,1,0:T(8,128)(2,1)}, u32[]{:S(2)}, u32[]{:S(2)}) async-start(bf16[8,64,2048]{2,1,0:T(8,128)(2,1)} %reshape.194), calls=%async_computation.1 | async-start | bytes 4194304 | tf_op jit(solution)/shard_map/all_to_all | solution.py:406
  90.7 168.6 %all-gather.5.cloned.1.call-start = ((), (), s32[]{:S(2)}) async-start(), calls=%async_computation.13 | async-start | bytes 10485760 | tf_op jit(solution)/shard_map/all_gather | solution.py:455
  104.3 13.3 %copy-start.24 = (bf16[4,64,2048]{2,1,0:T(8,128)(2,1)S(1)}, bf16[4,64,2048]{2,1,0:T(8,128)(2,1)}, u32[]{:S(2)}) copy-start(bf16[4,64,2048]{2,1,0:T(8,128)(2,1)} %copy-done.23) | copy-start | bytes 3145732
  117.6 7.1 %copy-start.15 = (f32[4,1,1024]{2,1,0:T(1,128)}, f32[4,1,1024]{2,1,0:T(1,128)S(1)}, u32[]{:S(2)}) copy-start(f32[4,1,1024]{2,1,0:T(1,128)S(1)} %get-tuple-element.50.lse_ref) | copy-start | bytes 49156
  118.3 21.0 %copy-start.26 = (bf16[1,128,2048]{2,1,0:T(8,128)(2,1)S(1)}, bf16[1,128,2048]{2,1,0:T(8,128)(2,1)}, u32[]{:S(2)}) copy-start(bf16[1,128,2048]{2,1,0:T(8,128)(2,1)} %param.15) | copy-start | bytes 1572868
  118.3 4.2 collective-permute-start.10
  140.9 53.5 %all-to-all-start.2 = ((bf16[4,128,2048]{2,1,0:T(8,128)(2,1)}), bf16[4,128,2048]{2,1,0:T(8,128)(2,1)}, u32[]{:S(2)}, u32[]{:S(2)}) async-start(bf16[4,128,2048]{2,1,0:T(8,128)(2,1)} %broadcast_in_dim.93), calls=%async_computation.2 | async-start | bytes 4194304 | tf_op jit(solution)/shard_map/all_to_all | solution.py:326
  145.4 290.5 %reduce-scatter.3.cloned.1.call-start = ((), (), s32[]{:S(2)}) async-start(), calls=%async_computation.14 | async-start | bytes 10485760 | tf_op jit(solution)/shard_map/reduce_scatter | solution.py:486
  148.5 45.8 %collective-permute-start.13 = (bf16[128,2048]{1,0:T(8,128)(2,1)}, bf16[128,2048]{1,0:T(8,128)(2,1)S(1)}, u32[]{:S(2)}, u32[]{:S(2)}) collective-permute-start(bf16[128,2048]{1,0:T(8,128)(2,1)} %get-tuple-element.68), channel_id=1, source_target_pairs={{0,24},{4,28},{8,16},{12,20},{16,8},{20,12},{24,0},{28,4},{1,25},{... | collective-permute-start | bytes 1572872 | tf_op jit(solution)/shard_map/ppermute | solution.py:288
  151.1 43.3 %collective-permute-start.12 = (bf16[128,2048]{1,0:T(8,128)(2,1)}, bf16[128,2048]{1,0:T(8,128)(2,1)S(1)}, u32[]{:S(2)}, u32[]{:S(2)}) collective-permute-start(bf16[128,2048]{1,0:T(8,128)(2,1)} %get-tuple-element.69), channel_id=1, source_target_pairs={{0,16},{4,20},{8,24},{12,28},{16,0},{20,4},{24,8},{28,12},{1,17},{... | collective-permute-start | bytes 1572872 | tf_op jit(solution)/shard_map/ppermute | solution.py:288
  151.6 44.3 %collective-permute-start.11 = (bf16[128,2048]{1,0:T(8,128)(2,1)}, bf16[128,2048]{1,0:T(8,128)(2,1)}, u32[]{:S(2)}, u32[]{:S(2)}) collective-permute-start(bf16[128,2048]{1,0:T(8,128)(2,1)} %get-tuple-element.70), channel_id=1, source_target_pairs={{0,8},{4,12},{8,0},{12,4},{16,24},{20,28},{24,16},{28,20},{1,9},{5... | collective-permute-start | bytes 1572872 | tf_op jit(solution)/shard_map/ppermute | solution.py:288
  198.4 180.3 %copy-start.17 = (f32[128,2048]{1,0:T(8,128)}, f32[128,2048]{1,0:T(8,128)S(1)}, u32[]{:S(2)}) copy-start(f32[128,2048]{1,0:T(8,128)S(1)} %get-tuple-element.60) | copy-start | bytes 3145732
  252.0 7.3 %collective-permute-start.14 = (bf16[512,2048]{1,0:T(8,128)(2,1)S(1)}, bf16[512,2048]{1,0:T(8,128)(2,1)}, u32[]{:S(2)}, u32[]{:S(2)}) collective-permute-start(bf16[512,2048]{1,0:T(8,128)(2,1)S(1)} %bitcast.140), channel_id=1, source_target_pairs={{0,4},{4,0},{8,12},{12,8},{16,20},{20,16},{24,28},{28,24},{1,5},{5... | collective-permute-start | bytes 6291464 | tf_op jit(solution)/shard_map/ppermute | solution.py:288
  252.0 21.7 %collective-permute-start.15 = (bf16[512,2048]{1,0:T(8,128)(2,1)}, bf16[512,2048]{1,0:T(8,128)(2,1)}, u32[]{:S(2)}, u32[]{:S(2)}) collective-permute-start(bf16[512,2048]{1,0:T(8,128)(2,1)} %bitcast.26), channel_id=1, source_target_pairs={{0,4},{4,0},{8,12},{12,8},{16,20},{20,16},{24,28},{28,24},{1,5},{5... | collective-permute-start | bytes 6291464 | tf_op jit(solution)/shard_map/ppermute | solution.py:288
  296.1 4.4 collective-permute-start.16
  296.7 13.3 %copy-start.28 = (bf16[4,128,2048]{2,1,0:T(8,128)(2,1)S(1)}, bf16[4,128,2048]{2,1,0:T(8,128)(2,1)}, u32[]{:S(2)}) copy-start(bf16[4,128,2048]{2,1,0:T(8,128)(2,1)} %copy-done.27) | copy-start | bytes 6291460
  323.0 53.3 %all-to-all-start.4 = ((bf16[4,128,2048]{2,1,0:T(8,128)(2,1)}), bf16[4,128,2048]{2,1,0:T(8,128)(2,1)}, u32[]{:S(2)}, u32[]{:S(2)}) async-start(bf16[4,128,2048]{2,1,0:T(8,128)(2,1)} %bitcast.143), calls=%async_computation.4 | async-start | bytes 4194304 | tf_op jit(solution)/shard_map/all_to_all | solution.py:330
  327.5 9.6 %copy-start.56 = (bf16[1024,2048]{1,0:T(8,128)(2,1)S(1)}, bf16[1024,2048]{1,0:T(8,128)(2,1)}, u32[]{:S(2)}) copy-start(bf16[1024,2048]{1,0:T(8,128)(2,1)} %all-gather.3.cloned.1.call-done) | copy-start | bytes 12582916
  327.5 9.6 %copy-start.57 = (bf16[1024,1024]{1,0:T(8,128)(2,1)S(1)}, bf16[1024,1024]{1,0:T(8,128)(2,1)}, u32[]{:S(2)}) copy-start(bf16[1024,1024]{1,0:T(8,128)(2,1)} %get-tuple-element.43) | copy-start | bytes 6291460
  332.8 4.2 collective-permute-start.17
  378.4 19.8 %copy-start.19 = (f32[128,2048]{1,0:T(8,128)}, f32[128,2048]{1,0:T(8,128)S(1)}, u32[]{:S(2)}) copy-start(f32[128,2048]{1,0:T(8,128)S(1)} %convert_reduce_fusion.1) | copy-start | bytes 3145732
  380.4 26.8 %collective-permute-start.20 = (bf16[128,2048]{1,0:T(8,128)(2,1)}, bf16[128,2048]{1,0:T(8,128)(2,1)S(1)}, u32[]{:S(2)}, u32[]{:S(2)}) collective-permute-start(bf16[128,2048]{1,0:T(8,128)(2,1)} %fusion.49), channel_id=1, source_target_pairs={{0,24},{4,28},{8,16},{12,20},{16,8},{20,12},{24,0},{28,4},{1,25},{... | collective-permute-start | bytes 1572872 | tf_op jit(solution)/shard_map/ppermute | solution.py:288
  382.1 35.4 %collective-permute-start.19 = (bf16[128,2048]{1,0:T(8,128)(2,1)}, bf16[128,2048]{1,0:T(8,128)(2,1)S(1)}, u32[]{:S(2)}, u32[]{:S(2)}) collective-permute-start(bf16[128,2048]{1,0:T(8,128)(2,1)} %fusion.49), channel_id=1, source_target_pairs={{0,16},{4,20},{8,24},{12,28},{16,0},{20,4},{24,8},{28,12},{1,17},{... | collective-permute-start | bytes 1572872 | tf_op jit(solution)/shard_map/ppermute | solution.py:288
  382.7 45.7 %collective-permute-start.18 = (bf16[128,2048]{1,0:T(8,128)(2,1)}, bf16[128,2048]{1,0:T(8,128)(2,1)S(1)}, u32[]{:S(2)}, u32[]{:S(2)}) collective-permute-start(bf16[128,2048]{1,0:T(8,128)(2,1)} %fusion.49), channel_id=1, source_target_pairs={{0,8},{4,12},{8,0},{12,4},{16,24},{20,28},{24,16},{28,20},{1,9},{5... | collective-permute-start | bytes 1572872 | tf_op jit(solution)/shard_map/ppermute | solution.py:288
  383.9 51.9 %all-to-all-start.5 = ((bf16[4,128,2048]{2,1,0:T(8,128)(2,1)}), bf16[4,128,2048]{2,1,0:T(8,128)(2,1)}, u32[]{:S(2)}, u32[]{:S(2)}) async-start(bf16[4,128,2048]{2,1,0:T(8,128)(2,1)} %bitcast.139), calls=%async_computation.5 | async-start | bytes 4194304 | tf_op jit(solution)/shard_map/all_to_all | solution.py:330
  429.6 4.5 collective-permute-start.21
  435.8 52.1 %all-to-all-start.6 = ((bf16[8,64,2048]{2,1,0:T(8,128)(2,1)}), bf16[8,64,2048]{2,1,0:T(8,128)(2,1)S(1)}, u32[]{:S(2)}, u32[]{:S(2)}) async-start(bf16[8,64,2048]{2,1,0:T(8,128)(2,1)} %bitcast.138), calls=%async_computation.7 | async-start | bytes 4194304 | tf_op jit(solution)/shard_map/all_to_all | solution.py:532
  439.4 134.5 %reduce-scatter.5.cloned.1.call-start = ((), (), s32[]{:S(2)}) async-start(), calls=%async_computation.15 | async-start | bytes 5242880 | tf_op jit(solution)/shard_map/reduce_scatter | solution.py:499
  456.4 7.1 %copy-start.46 = (f32[2048]{0:T(1024)S(1)}, f32[2048]{0:T(1024)}, u32[]{:S(2)}) copy-start(f32[2048]{0:T(1024)} %copy-done.45) | copy-start | bytes 24580
  456.4 7.1 %copy-start.49 = (f32[1024]{0:T(1024)S(1)}, f32[1024]{0:T(1024)}, u32[]{:S(2)}) copy-start(f32[1024]{0:T(1024)} %copy-done.48) | copy-start | bytes 12292
  459.1 4.4 collective-permute-start.22
  488.0 42.2 %all-to-all-start.7 = ((bf16[4,8,64,384]{3,2,1,0:T(8,128)(2,1)}), bf16[4,8,64,384]{3,2,1,0:T(8,128)(2,1)}, u32[]{:S(2)}, u32[]{:S(2)}) async-start(bf16[4,8,64,384]{3,2,1,0:T(8,128)(2,1)} %bitcast.134), calls=%async_computation.8 | async-start | bytes 3145728 | tf_op jit(solution)/shard_map/all_to_all | solution.py:551
  492.3 8.2 %copy-start.5 = (bf16[4,64,1024]{2,1,0:T(8,128)(2,1)S(1)}, bf16[4,64,1024]{2,1,0:T(8,128)(2,1)}, u32[]{:S(2)}) copy-start(bf16[4,64,1024]{2,1,0:T(8,128)(2,1)} %copy-done.4) | copy-start | bytes 1572868
  497.0 39.7 %collective-permute-start.23 = (bf16[128,2048]{1,0:T(8,128)(2,1)}, bf16[128,2048]{1,0:T(8,128)(2,1)S(1)}, u32[]{:S(2)}, u32[]{:S(2)}) collective-permute-start(bf16[128,2048]{1,0:T(8,128)(2,1)} %get-tuple-element.64), channel_id=1, source_target_pairs={{0,8},{4,12},{8,0},{12,4},{16,24},{20,28},{24,16},{28,20},{1,9},{5... | collective-permute-start | bytes 1572872 | tf_op jit(solution)/shard_map/ppermute | solution.py:288
  497.8 39.0 %collective-permute-start.25 = (bf16[128,2048]{1,0:T(8,128)(2,1)}, bf16[128,2048]{1,0:T(8,128)(2,1)}, u32[]{:S(2)}, u32[]{:S(2)}) collective-permute-start(bf16[128,2048]{1,0:T(8,128)(2,1)} %get-tuple-element.65), channel_id=1, source_target_pairs={{0,24},{4,28},{8,16},{12,20},{16,8},{20,12},{24,0},{28,4},{1,25},{... | collective-permute-start | bytes 1572872 | tf_op jit(solution)/shard_map/ppermute | solution.py:288
  499.9 34.7 %copy-start.53 = (f32[128]{0:T(128)S(1)}, f32[128]{0:T(128)}, u32[]{:S(2)}) copy-start(f32[128]{0:T(128)} %get-tuple-element.75) | copy-start | bytes 1540
  499.9 36.9 %collective-permute-start.24 = (bf16[128,2048]{1,0:T(8,128)(2,1)}, bf16[128,2048]{1,0:T(8,128)(2,1)}, u32[]{:S(2)}, u32[]{:S(2)}) collective-permute-start(bf16[128,2048]{1,0:T(8,128)(2,1)} %get-tuple-element.66), channel_id=1, source_target_pairs={{0,16},{4,20},{8,24},{12,28},{16,0},{20,4},{24,8},{28,12},{1,17},{... | collective-permute-start | bytes 1572872 | tf_op jit(solution)/shard_map/ppermute | solution.py:288
  505.1 31.7 %copy-start.21 = (bf16[1,128,2048]{2,1,0:T(8,128)(2,1)S(1)}, bf16[1,128,2048]{2,1,0:T(8,128)(2,1)}, u32[]{:S(2)}) copy-start(bf16[1,128,2048]{2,1,0:T(8,128)(2,1)} %param.14) | copy-start | bytes 1572868
  505.1 33.8 %copy-start.51 = (f32[128]{0:T(128)S(1)}, f32[128]{0:T(128)}, u32[]{:S(2)}) copy-start(f32[128]{0:T(128)} %copy-done.50) | copy-start | bytes 1540
  530.1 30.3 %all-to-all-start.9 = ((bf16[4,64,2048]{2,1,0:T(8,128)(2,1)}), bf16[4,64,2048]{2,1,0:T(8,128)(2,1)}, u32[]{:S(2)}, u32[]{:S(2)}) async-start(bf16[4,64,2048]{2,1,0:T(8,128)(2,1)} %bitcast.149), calls=%async_computation.10 | async-start | bytes 2097152 | tf_op jit(solution)/shard_map/all_to_all | solution.py:555
  538.9 27.3 %copy-start.1 = (bf16[64,8192]{1,0:T(8,128)(2,1)S(1)}, bf16[64,8192]{1,0:T(8,128)(2,1)}, u32[]{:S(2)}) copy-start(bf16[64,8192]{1,0:T(8,128)(2,1)} %up_weight.1) | copy-start | bytes 3145732
  545.9 24.5 %copy-start.55 = (bf16[64]{0:T(256)(128)(2,1)S(1)}, bf16[64]{0:T(256)(128)(2,1)}, u32[]{:S(2)}) copy-start(bf16[64]{0:T(256)(128)(2,1)} %param.23) | copy-start | bytes 388
  560.4 11.7 %all-to-all-start.8 = ((bf16[8,64,384]{2,1,0:T(8,128)(2,1)}), bf16[8,64,384]{2,1,0:T(8,128)(2,1)S(1)}, u32[]{:S(2)}, u32[]{:S(2)}) async-start(bf16[8,64,384]{2,1,0:T(8,128)(2,1)} %reduce_sum.146), calls=%async_computation.9 | async-start | bytes 786432 | tf_op jit(solution)/shard_map/all_to_all | solution.py:552
  (33 other events, 83.5 us)
Sparse Core Ops, SparseCore 0:
  13.2 73.0 all-gather.2
  139.4 108.7 all-gather.4
  323.1 106.7 reduce-scatter.2
  456.5 61.2 reduce-scatter.4

commit v3 on v2

--- a/solution.py
+++ b/solution.py
@@ -14,6 +14,7 @@
 EPSILON = 1e-05
 MASKED = -1e30
 INNER = 2
+HALVES = 2
 F32 = jnp.float32
 BF16 = jnp.bfloat16
 
@@ -210,9 +211,9 @@
         ],
         compiler_params=pltpu.CompilerParams(vmem_limit_bytes=40 * 2**20),
         cost_estimate=pl.CostEstimate(
-            flops=4 * heads * length * length * HEAD,
-            bytes_accessed=8 * total * HEAD * length,
-            transcendentals=heads * length * length,
+            flops=heads * length * HEAD,
+            bytes_accessed=total * HEAD * length,
+            transcendentals=0,
         ),
     )(place, lin, cosine, sine, keydoc, doc)
 
@@ -237,9 +238,9 @@
         ],
         compiler_params=pltpu.CompilerParams(vmem_limit_bytes=40 * 2**20),
         cost_estimate=pl.CostEstimate(
-            flops=10 * heads * length * length * HEAD,
-            bytes_accessed=8 * total * HEAD * length,
-            transcendentals=heads * length * length,
+            flops=heads * length * HEAD,
+            bytes_accessed=total * HEAD * length,
+            transcendentals=0,
         ),
     )(place, grad, query, key, value, lse, cosine, sine, keydoc, doc)
 
@@ -433,7 +434,6 @@
         grad_out_near = narrow_gather(after(grad_out_own, column)).reshape(-1, model)
 
         own = all_input.shape[0] // INNER
-        half = near_size * tokens // INNER
         documents = doc_ids[0]
         positions = stream_positions(documents)
         angles = jnp.asarray(inverse_rates(HEAD))[:, None] * positions.astype(F32)[None, :]
@@ -453,74 +453,112 @@
 
         attended, _ = near_total(out_product)
         gate_up = lax.all_gather(
-            after(column.reshape(near_size * rows, pair_cols), down, attended), "wide", axis=0, tiled=True,
+            after(column.reshape(near_size * rows, pair_cols), down, attended), "wide",
+            axis=0, tiled=True, axis_index_groups=chip_groups,
+        )
+        piece = tokens // HALVES
+        attended = attended.reshape(outer, HALVES, piece, model)
+        residual_half = residual.reshape(HALVES, piece, model)
+        after_half, scaled_half, factor_half, normed_half = [], [], [], []
+        attended_parts = [
+            [attended[0, h]] + [outer_swap(attended[step, h], step) for step in range(1, outer)]
+            for h in range(HALVES)
+        ]
+        attended_parts[0][0] = after(attended_parts[0][0], grad_out_near)
+        for h in range(HALVES):
+            after_half.append(residual_half[h] + add_up(attended_parts[h]))
+            scaled, factor = normalize(after_half[h])
+            scaled_half.append(scaled)
+            factor_half.append(factor)
+            normed_half.append((scaled * gain_two).astype(BF16))
+
+        half = narrow * piece
+        first = grad_out_near.reshape(narrow, HALVES, piece, model).transpose(1, 0, 2, 3)
+        grad_out = jnp.stack([first, core_swap(first)], axis=1).reshape(HALVES, -1, model)
+        normed_two, hidden, grad_pair, two_totals, two_parts, branch_totals = [], [], [], [], [], []
+        near_half = [narrow_gather(normed_half[h]).reshape(-1, model) for h in range(HALVES)]
+        for h in range(HALVES):
+            normed_near = after(near_half[h], two_totals[h - 1]) if h else near_half[h]
+            normed_two.append(with_sibling(normed_near))
+            pair = mm(normed_two[h], gate_up, ((1,), (0,)))
+            gate, upward = pair[:, :units], pair[:, units:]
+            sigmoid_gate = jax.nn.sigmoid(gate)
+            activated = gate * sigmoid_gate
+            hidden.append((activated * upward).astype(BF16))
+            grad_hidden = mm(grad_out[h], down, ((1,), (1,)))
+            slope = sigmoid_gate * (1.0 + gate * (1.0 - sigmoid_gate))
+            grad_gate = (grad_hidden * upward * slope).astype(BF16)
+            grad_up = (grad_hidden * activated).astype(BF16)
+            both_grads = jnp.concatenate([grad_gate, grad_up], axis=1)
+            grad_pair.append(both_grads)
+            if not h:
+                both_grads = after(both_grads, near_half[-1])
+
+            def two_product(near, both_grads=both_grads):
+                return mm(both_grads[near * half : (near + 1) * half], gate_up, ((1,), (1,)))
+
+            two_totals.append(near_total(two_product)[0])
+            total = two_totals[h] if not h else after(two_totals[h], two_parts[h - 1])
+            two_parts.append(
+                lax.psum_scatter(total, "narrow", scatter_dimension=0, tiled=True)
+            )
+
+        for h in range(HALVES):
+            late_hidden = after(hidden[h], two_totals[-1], two_parts[0])
+
+            def branch_product(near, late_hidden=late_hidden):
+                return mm(late_hidden[near * half : (near + 1) * half], down, ((1,), (0,)))
+
+            branch_totals.append(near_total(branch_product)[0])
+
+        pair_term = mm(
+            jnp.concatenate(normed_two, axis=0), jnp.concatenate(grad_pair, axis=0), ((0,), (0,))
+        ).astype(BF16)
+        pair_sum = lax.psum_scatter(
+            after(pair_term, two_parts[-1], branch_totals[-1]), "wide", scatter_dimension=0, tiled=True,
             axis_index_groups=chip_groups,
         )
-        attended_parts = scatter(attended, outer_swap, outer)
-        attended_parts[0] = after(attended_parts[0], grad_out_near)
-        after_attention = residual + add_up(attended_parts)
-        scaled_two, factor_two = normalize(after_attention)
-        normed_own = (scaled_two * gain_two).astype(BF16)
-
-        normed_near = narrow_gather(normed_own).reshape(-1, model)
-        normed_two = with_sibling(normed_near)
-        grad_out = with_sibling(grad_out_near)
-        pair = mm(normed_two, gate_up, ((1,), (0,)))
-        gate, upward = pair[:, :units], pair[:, units:]
-        sigmoid_gate = jax.nn.sigmoid(gate)
-        activated = gate * sigmoid_gate
-        hidden = (activated * upward).astype(BF16)
-        grad_hidden = mm(grad_out, down, ((1,), (1,)))
-        slope = sigmoid_gate * (1.0 + gate * (1.0 - sigmoid_gate))
-        grad_gate = (grad_hidden * upward * slope).astype(BF16)
-        grad_up = (grad_hidden * activated).astype(BF16)
-        grad_pair = jnp.concatenate([grad_gate, grad_up], axis=1)
-
-        def two_product(near):
-            return mm(grad_pair[near * half : (near + 1) * half], gate_up, ((1,), (1,)))
-
-        two_total, _ = near_total(two_product)
-        two_parts = narrow_sum(two_total)
-
-        pair_term = mm(normed_two, after(grad_pair, two_total), ((0,), (0,))).astype(BF16)
-        pair_sum = lax.psum_scatter(
-            pair_term, "wide", scatter_dimension=0, tiled=True, axis_index_groups=chip_groups
-        )
-        late_hidden = after(hidden, pair_term)
-
-        def branch_product(near):
-            return mm(late_hidden[near * half : (near + 1) * half], down, ((1,), (0,)))
-
-        branch_total, _ = near_total(branch_product)
-        down_term = mm(late_hidden, grad_out, ((0,), (0,))).astype(BF16)
-        grad_two = jnp.sum(after(two_parts, branch_total).astype(F32), axis=0)
-        branch_parts = narrow_sum(after(branch_total, grad_two))
-        layer_output = after_attention + jnp.sum(branch_parts.astype(F32), axis=0)
-        down_grad = lax.psum_scatter(
-            after(down_term, pair_sum), "wide", scatter_dimension=0, tiled=True,
-            axis_index_groups=chip_groups,
-        ).astype(F32)
-
+
+        grad_two = jnp.concatenate(two_parts, axis=0).astype(F32)
+        scaled_two = jnp.concatenate(scaled_half, axis=0)
+        factor_two = jnp.concatenate(factor_half, axis=0)
         grad_scaled_two = grad_two * gain_two
         grad_middle = grad_out_own.astype(F32) + factor_two * (
             grad_scaled_two
             - scaled_two * jnp.mean(grad_scaled_two * scaled_two, axis=-1, keepdims=True)
         )
         middle_parts = fan_out(grad_middle.astype(BF16), outer_swap, outer)
+        branch_total = jnp.stack(
+            [total.reshape(narrow, piece, model) for total in branch_totals], axis=1
+        ).reshape(-1, model)
+        branch_parts = narrow_sum(after(branch_total, middle_parts[0]))
+        after_attention = jnp.concatenate(after_half, axis=0)
+        layer_output = after_attention + jnp.sum(branch_parts.astype(F32), axis=0)
+        down_term = mm(
+            jnp.concatenate([after(hidden[0], middle_parts[0])] + hidden[1:], axis=0),
+            grad_out.reshape(-1, model), ((0,), (0,)),
+        ).astype(BF16)
         middle_parts[0] = after(middle_parts[0], down_term)
-        grad_attention = join_near(middle_parts)
-        grad_mixed = mm(out_own, grad_attention, ((1,), (1,)))
+        near_middle = lax.optimization_barrier(jnp.concatenate(middle_parts, axis=0))
+        grad_attention = after(with_sibling(near_middle), branch_parts)
+        out_term = mm(mixed, grad_attention, ((1,), (0,))).astype(BF16)
+        out_term = out_term.reshape(narrow, rows, model)
+        out_split = [pick(out_term, layer ^ step) for step in range(narrow)]
+        out_sent = [narrow_swap(out_split[step], step) for step in range(1, narrow)]
+        grad_mixed = mm(out_own, after(grad_attention, *out_split), ((1,), (1,)))
         grad_mixed = grad_mixed.astype(BF16)
         grad_lin = attend_back(
             place_arg, grad_mixed.reshape(heads, HEAD, -1), query, key, value, lse, cosine, sine,
             keydoc, doc, tokens, outer,
         ).reshape(cols, -1)
+        grad_lin = after(grad_lin, *out_sent)
 
         def one_product(near):
             return mm(grad_lin[:, near * own : (near + 1) * own], attention_weight, ((0,), (1,)))
 
         one_total, one_swapped = near_total(one_product)
-        grad_one = add_up(scatter(one_total, outer_swap, outer))
+        one_parts = scatter(one_total, outer_swap, outer)
+        grad_one = add_up(one_parts)
         scaled_one, factor_one = normalize(residual)
         grad_scaled_one = grad_one * gain_one
         input_grad = grad_middle + factor_one * (
@@ -528,7 +566,26 @@
             - scaled_one * jnp.mean(grad_scaled_one * scaled_one, axis=-1, keepdims=True)
         )
 
-        pair_sum = after(pair_sum, branch_parts).reshape(near_size, rows, pair_cols)
+        late_lin = after(grad_lin, one_swapped)
+        lin_term = mm(normed_one, late_lin, ((0,), (1,))).astype(BF16)
+        lin_term = lin_term.reshape(wide, narrow, rows, cols).transpose(1, 0, 2, 3)
+        out_grad = add_up([after(out_split[0], lin_term)] + out_sent)
+        lin_sum = jnp.sum(lax.all_to_all(lin_term, "narrow", 0, 0, tiled=True).astype(F32), axis=0)
+        lin_split = lin_sum.astype(BF16).reshape(outer, INNER, rows, cols)
+        mine = pick(lin_split, core, 1)
+        other = core_swap(pick(lin_split, 1 - core, 1))
+        lin_pair = jnp.stack([mine, other], axis=1)
+        lin_parts = [pick(lin_pair, chip)] + [
+            outer_swap(pick(lin_pair, chip ^ step), step) for step in range(1, outer)
+        ]
+        lin_parts = jnp.concatenate(lin_parts, axis=0)
+        lin_grad = jnp.stack([pick(lin_parts, place ^ w) for w in range(wide)]).astype(F32)
+        down_grad = lax.psum_scatter(
+            after(down_term, pair_sum, lin_term), "wide", scatter_dimension=0, tiled=True,
+            axis_index_groups=chip_groups,
+        ).astype(F32)
+
+        pair_sum = after(pair_sum, lin_sum, one_parts[0]).reshape(near_size, rows, pair_cols)
         pair_grad = lax.all_to_all(pair_sum, both, 0, 0, axis_index_groups=near_groups, tiled=True)
         if down_rows % 128 == 0:
             gate_grad, up_grad, gain_sum = join_pair(
@@ -543,16 +600,6 @@
                 up_grad * up_weight.astype(F32), axis=1
             )
         gain_two_grad = gain_sum / feedforward_gain.astype(F32)
-
-        late_lin = after(grad_lin, one_swapped)
-        lin_term = mm(normed_one, late_lin, ((0,), (1,))).astype(BF16)
-        lin_term = lin_term.reshape(wide, narrow, rows, cols).transpose(1, 0, 2, 3)
-        lin_term = after(lin_term, pair_grad)
-        lin_sum = jnp.sum(lax.all_to_all(lin_term, "narrow", 0, 0, tiled=True).astype(F32), axis=0)
-        lin_grad = lax.all_to_all(lin_sum.astype(BF16), "wide", 0, 0, tiled=True).astype(F32)
-        out_term = mm(mixed, after(grad_attention, late_lin), ((1,), (0,))).astype(BF16)
-        out_term = out_term.reshape(narrow, rows, model)
-        out_grad = jnp.sum(lax.all_to_all(out_term, "narrow", 0, 0, tiled=True).astype(F32), axis=0)
 
         query_grad = lin_grad[:, :, :head_cols].transpose(1, 0, 2).reshape(rows, -1)
 

time: 591 us -> 575 us (0.973)
  blocking collectives: 51.9 us -> 0 us
  other arithmetic: 34.4 us -> 49.3 us
  local copies, waits for them, and re-layouts: 53.5 us -> 66 us
  starting transfers between devices: 64.9 us -> 76.4 us
    all_to_all x1 -> x0, blocking collectives: 51.9 us -> none  [narrow_gather(): return lax.all_to_all(spread, 'narrow', 0, 0, tiled=True)]
    ppermute x26 -> x39, waiting for transfers between devices: 83 us -> 130 us  [exchange(): return lax.ppermute(value, axis, [(i, i ^ step) for i in range(size)])]
    all_to_all x2 -> x1, waiting for transfers between devices: 35.9 us -> 0.01 us  [narrow_sum(): return lax.all_to_all(split, 'narrow', 0, 0, tiled=True)]
    all_to_all x2 -> x0, waiting for transfers between devices: 15.8 us -> none  [the longest x1 14.6 us: per_device(): lax.all_to_all(out_term, 'narrow', 0, 0, tiled=True).astype(F32)]
    all_to_all x1 -> x3, waiting for transfers between devices: 42.3 us -> 26.7 us  [narrow_gather(): return lax.all_to_all(spread, 'narrow', 0, 0, tiled=True)]
    ppermute x26 -> x39, starting transfers between devices: 26.5 us -> 40 us  [exchange(): return lax.ppermute(value, axis, [(i, i ^ step) for i in range(size)])]
    all_to_all x1 -> x3, starting transfers between devices: 4.45 us -> 13.3 us  [narrow_gather(): return lax.all_to_all(spread, 'narrow', 0, 0, tiled=True)]
    reduce_scatter x2 -> x4, waiting for transfers between devices: 0.01 us -> 8.56 us  [the longest x2 8.56 us: per_device(): lax.psum_scatter(total, 'narrow', scatter_dimension=0, tiled=True)]
  transfers between devices with their start and end apart: 39 -> 53, of which waited for: 21 -> 33; matrix products, arithmetic and copies ran while one was open for 23% -> 34% of each run, Pallas kernels for 5% -> 5%
where the time goes in v3:
time: 575 us; the launch traced here: 567 us
  waiting for transfers between devices  231 us (40%)
  matrix products  102 us (18%)
  starting transfers between devices  76.4 us (13%)
  local copies, waits for them, and re-layouts  66 us (11%)
  other arithmetic  49.3 us (9%)
  Pallas kernels  26.8 us (5%)
  between operations  15.7 us (3%)
    ppermute x39, waiting for transfers between devices, exchange(): return lax.ppermute(value, axis, [(i, i ^ step) for i in range(size)])  130 us
    dot_general x22, matrix products, mm(): lax.dot_general(left, right, (dims, ((), ())), preferred_element_type=F32)  102 us
    ppermute x39, starting transfers between devices, exchange(): return lax.ppermute(value, axis, [(i, i ^ step) for i in range(size)])  40 us
    all_to_all x3, waiting for transfers between devices, narrow_gather(): return lax.all_to_all(spread, 'narrow', 0, 0, tiled=True)  26.7 us
    all_to_all x1, waiting for transfers between devices, per_device(): lax.all_to_all(lin_term, 'narrow', 0, 0, tiled=True).astype(F32)  23 us
    all_to_all x1, waiting for transfers between devices, per_device(): lax.all_to_all(pair_sum, both, 0, 0, axis_index_groups=near_groups, tiled...  18.6 us
    unnamed x135, local copies, waits for them, and re-layouts  17.4 us
    all_to_all x1, waiting for transfers between devices, per_device(): lax.all_to_all(pair_weight, both, 0, 0, axis_index_groups=near_groups, ti...  16.5 us
  transfers between devices with their start and end apart: 53, of which 33 were waited for; matrix products, arithmetic and copies ran while one was open for 34% of the time, Pallas kernels for 5%

profile of v3, /device:TPU:0, one launch (start us, length us, event | category | flops | bytes accessed | tf_op | source)
XLA Modules:
  0.0 567.3 jit_solution(13064506668839924408)
XLA Ops:
  7.2 5.1 collective-permute-start.2
  17.9 4.1 all-to-all-start
  25.7 2.7 pad_maximum_fusion.3
  28.6 4.5 reshape.277
  37.0 2.8 collective-permute-start.8
  42.2 3.7 collective-permute-start.5
  49.2 7.8 %collective-permute-done.8 = bf16[128,2048]{1,0:T(8,128)(2,1)S(1)} collective-permute-done((bf16[128,2048]{1,0:T(8,128)(2,1)S(1)}, bf16[128,2048]{1,0:T(8,128)(2,1)S(1)}, u32[]{:S(2)}, u32[]{:S(2)}) %collective-permute-start.8) | collective-permute-done | bytes 524320 | tf_op jit(solution)/shard_map/ppermute | solution.py:289
  58.0 17.4 %collective-permute-done.7 = bf16[128,2048]{1,0:T(8,128)(2,1)S(1)} collective-permute-done((bf16[128,2048]{1,0:T(8,128)(2,1)S(1)}, bf16[128,2048]{1,0:T(8,128)(2,1)S(1)}, u32[]{:S(2)}, u32[]{:S(2)}) %collective-permute-start.7) | collective-permute-done | bytes 524320 | tf_op jit(solution)/shard_map/ppermute | solution.py:289
  75.3 3.3 collective-permute-done.6
  90.4 2.6 copy.93
  93.0 4.6 all-to-all-start.2
  100.4 3.3 constant_dynamic-update-slice_fusion
  103.7 3.2 fusion
  109.1 11.1 %shard_map.221 = (bf16[4,64,1024]{2,1,0:T(8,128)(2,1)S(1)}, bf16[4,64,1024]{2,1,0:T(8,128)(2,1)S(1)}, bf16[1,64,1024]{2,1,0:T(8,128)(2,1)S(1)}, bf16[1,64,1024]{2,1,0:T(8,128)(2,1)S(1)}, f32[4,1,1024]{2,1,0:T(1,128)S(1)}) custom-call(s32[1]{0:T(128)} %bitcast.1.place_ref, f32[6,64,1024]{2,1,0:T(8,128)S(1)} %fusion.17.lin_ref, ...), custom_call_target="tpu_custom_call" | custom-call | flops 262144 | bytes 393216 | tf_op jit(solution)/shard_map/pallas_call | solution.py:197
  122.7 3.8 collective-permute-done.10
  126.5 3.3 add_convert_fusion.1
  129.8 16.5 %all-to-all-done.2 = bf16[8,64,2048]{2,1,0:T(8,128)(2,1)} async-done(((bf16[8,64,2048]{2,1,0:T(8,128)(2,1)}), bf16[8,64,2048]{2,1,0:T(8,128)(2,1)}, u32[]{:S(2)}, u32[]{:S(2)}) %all-to-all-start.2) | async-done | bytes 2097184 | tf_op jit(solution)/shard_map/all_to_all | solution.py:407
  147.9 4.4 all-to-all-start.3
  152.4 2.7 slice_bitcast_fusion.13
  162.5 8.3 %collective-permute-done.16 = bf16[64,2048]{1,0:T(8,128)(2,1)S(1)} collective-permute-done((bf16[64,2048]{1,0:T(8,128)(2,1)S(1)}, bf16[64,2048]{1,0:T(8,128)(2,1)S(1)}, u32[]{:S(2)}, u32[]{:S(2)}) %collective-permute-start.16) | collective-permute-done | bytes 262176 | tf_op jit(solution)/shard_map/ppermute | solution.py:289
  176.9 5.0 collective-permute-done.14
  182.0 11.4 %collective-permute-done.13 = bf16[64,2048]{1,0:T(8,128)(2,1)} collective-permute-done((bf16[64,2048]{1,0:T(8,128)(2,1)}, bf16[64,2048]{1,0:T(8,128)(2,1)}, u32[]{:S(2)}, u32[]{:S(2)}) %collective-permute-start.13) | collective-permute-done | bytes 262176 | tf_op jit(solution)/shard_map/ppermute | solution.py:289
  193.6 8.1 %collective-permute-done.11 = bf16[64,2048]{1,0:T(8,128)(2,1)} collective-permute-done((bf16[64,2048]{1,0:T(8,128)(2,1)S(1)}, bf16[64,2048]{1,0:T(8,128)(2,1)}, u32[]{:S(2)}, u32[]{:S(2)}) %collective-permute-start.11) | collective-permute-done | bytes 262176 | tf_op jit(solution)/shard_map/ppermute | solution.py:289
  208.0 4.6 all-to-all-start.1
  212.6 25.9 %all-to-all-done.1 = bf16[4,64,2048]{2,1,0:T(8,128)(2,1)} async-done(((bf16[4,64,2048]{2,1,0:T(8,128)(2,1)}), bf16[4,64,2048]{2,1,0:T(8,128)(2,1)}, u32[]{:S(2)}, u32[]{:S(2)}) %all-to-all-start.1) | async-done | bytes 1048608 | tf_op jit(solution)/shard_map/all_to_all | solution.py:327
  239.6 4.2 all-to-all-start.4
  244.1 3.7 fusion.19
  247.9 7.2 %all-gather.5.cloned.1.call-done = bf16[2048,2048]{1,0:T(8,128)(2,1)} async-done(((bf16[512,2048]{1,0:T(8,128)(2,1)}), bf16[2048,2048]{1,0:T(8,128)(2,1)}) %all-gather.5.cloned.1.call-update) | async-done | bytes 8388624 | tf_op jit(solution)/shard_map/all_gather | solution.py:455
  255.1 7.7 %fusion.21 = f32[512,2048]{1,0:T(8,128)S(1)} fusion(bf16[2048,2048]{1,0:T(8,128)(2,1)} %all-gather.5.cloned.1.call-done, bf16[256,2048]{1,0:T(8,128)(2,1)} %collective-permute-done.17, bf16[256,2048]{1,0:T(8,128)(2,1)} %bitcast.32), kind=kOutput, calls=%fused_computation.44 | convolution fusion | flops 4299161600 | bytes 14680064 | tf_op jit(solution)/shard_map/dot_general | solution.py:48
  262.8 4.1 multiply_convert_fusion.4
  270.6 6.2 %convolution_convert_fusion.9 = bf16[256,2048]{1,0:T(8,128)(2,1)S(1)} fusion(bf16[2048,2048]{1,0:T(8,128)(2,1)} %all-gather.5.cloned.1.call-done, bf16[512,2048]{1,0:T(8,128)(2,1)} %pad_maximum_fusion.4), kind=kOutput, calls=%fused_computation.40 | convolution fusion | flops 2148007936 | bytes 10485760 | tf_op jit(solution)/shard_map/dot_general | solution.py:48
  276.8 2.6 collective-permute-done.19
  279.5 6.7 %add_convert_fusion.5 = bf16[256,2048]{1,0:T(8,128)(2,1)} fusion(bf16[256,2048]{1,0:T(8,128)(2,1)S(1)} %collective-permute-done.19, bf16[2048,2048]{1,0:T(8,128)(2,1)} %all-gather.5.cloned.1.call-done, bf16[512,2048]{1,0:T(8,128)(2,1)S(1)} %copy-done.25), kind=kOutput, calls=%fused_computation.69 | convolution fusion | flops 2149056512 | bytes 11534336 | tf_op jit(solution)/shard_map/dot_general | solution.py:48
  289.2 7.8 %fusion.25 = f32[512,2048]{1,0:T(8,128)S(1)} fusion(bf16[2048,2048]{1,0:T(8,128)(2,1)} %all-gather.5.cloned.1.call-done, bf16[256,2048]{1,0:T(8,128)(2,1)} %collective-permute-done.20, bf16[256,2048]{1,0:T(8,128)(2,1)} %bitcast.45), kind=kOutput, calls=%fused_computation.50 | convolution fusion | flops 4299161600 | bytes 14680064 | tf_op jit(solution)/shard_map/dot_general | solution.py:48
  297.1 4.1 multiply_convert_fusion.2
  306.4 3.4 add_convert_fusion.4
  309.7 3.2 reduce-scatter.5.cloned.1.call-done
  313.2 4.7 convolution_convert_fusion.6
  317.9 12.7 %convolution_convert_fusion = bf16[2048,2048]{1,0:T(8,128)(2,1)} fusion(bf16[256,2048]{1,0:T(8,128)(2,1)} %collective-permute-done.20, bf16[256,2048]{1,0:T(8,128)(2,1)} %bitcast.45, bf16[256,2048]{1,0:T(8,128)(2,1)} %collective-permute-done.17, bf16[256,2048]{1,0:T(8,128)(2,1)} %bitcast.32, bf16[512,1024]{1,0:T(8,128)(2,1)S(1)} %copy-done.57, ...), kind=kOutput, calls=%fused_computation.5 | convolution fusion | flops 8627683328 | bytes 16777216 | tf_op jit(solution)/shard_map/dot_general | solution.py:48
  330.7 4.9 add_convert_fusion.2
  335.6 5.4 reduce-scatter.7.cloned.1.call-done
  341.0 3.6 convolution_convert_fusion.7
  359.3 4.5 all-to-all-start.5
  364.1 9.5 %convolution_convert_fusion.1 = bf16[1024,2048]{1,0:T(8,128)(2,1)} fusion(bf16[1024,2048]{1,0:T(8,128)(2,1)} %bitcast.207, bf16[512,1024]{1,0:T(8,128)(2,1)} %get-tuple-element.49, bf16[512,1024]{1,0:T(8,128)(2,1)} %get-tuple-element.52), kind=kOutput, calls=%fused_computation.31 | convolution fusion | flops 4301258752 | bytes 10485760 | tf_op jit(solution)/shard_map/dot_general | solution.py:48
  373.6 9.4 %collective-permute-done.26 = bf16[128,2048]{1,0:T(8,128)(2,1)} collective-permute-done((bf16[128,2048]{1,0:T(8,128)(2,1)}, bf16[128,2048]{1,0:T(8,128)(2,1)}, u32[]{:S(2)}, u32[]{:S(2)}) %collective-permute-start.26) | collective-permute-done | bytes 524320 | tf_op jit(solution)/shard_map/ppermute | solution.py:289
  383.0 11.7 %collective-permute-done.25 = bf16[128,2048]{1,0:T(8,128)(2,1)} collective-permute-done((bf16[128,2048]{1,0:T(8,128)(2,1)}, bf16[128,2048]{1,0:T(8,128)(2,1)}, u32[]{:S(2)}, u32[]{:S(2)}) %collective-permute-start.25) | collective-permute-done | bytes 524320 | tf_op jit(solution)/shard_map/ppermute | solution.py:289
  394.8 10.6 %collective-permute-done.24 = bf16[128,2048]{1,0:T(8,128)(2,1)} collective-permute-done((bf16[128,2048]{1,0:T(8,128)(2,1)}, bf16[128,2048]{1,0:T(8,128)(2,1)}, u32[]{:S(2)}, u32[]{:S(2)}) %collective-permute-start.24) | collective-permute-done | bytes 524320 | tf_op jit(solution)/shard_map/ppermute | solution.py:289
  407.5 4.1 collective-permute-done.27
  414.2 3.6 convolution_convert_fusion.5
  419.9 3.0 collective-permute-start.28
  425.5 12.8 %shard_map.222 = bf16[6,64,1024]{2,1,0:T(8,128)(2,1)S(1)} custom-call(s32[1]{0:T(128)} %bitcast.1.place_ref, bf16[4,64,1024]{2,1,0:T(8,128)(2,1)S(1)} %bitcast.189, bf16[4,64,1024]{2,1,0:T(8,128)(2,1)S(1)} %get-tuple-element.56.query_ref, bf16[1,64,1024]{2,1,0:T(8,128)(2,1)S(1)} %get-tuple-element.57.key_ref, ...), custom_call_target="tpu_custom_call" | custom-call | flops 262144 | bytes 393216 | tf_op jit(solution)/shard_map/pallas_call | solution.py:226
  438.3 5.0 collective-permute-done.29
  444.2 2.7 convolution_convert_fusion.3
  447.0 4.1 collective-permute-done.31
  451.1 2.9 convolution_convert_fusion.4
  455.4 4.4 all-to-all-start.6
  464.3 4.0 add_convert_fusion
  474.3 23.0 %all-to-all-done.6 = bf16[4,8,64,384]{3,2,1,0:T(8,128)(2,1)} async-done(((bf16[4,8,64,384]{3,2,1,0:T(8,128)(2,1)}), bf16[4,8,64,384]{3,2,1,0:T(8,128)(2,1)}, u32[]{:S(2)}, u32[]{:S(2)}) %all-to-all-start.6) | async-done | bytes 1572896 | tf_op jit(solution)/shard_map/all_to_all | solution.py:573
  499.9 4.0 all-to-all-start.7
  506.0 4.3 collective-permute-done.34
  517.6 3.2 fusion.48
  533.8 18.6 %all-to-all-done.7.gate_part.up_part = bf16[8,64,2048]{2,1,0:T(8,128)(2,1)S(1)} async-done(((bf16[8,64,2048]{2,1,0:T(8,128)(2,1)}), bf16[8,64,2048]{2,1,0:T(8,128)(2,1)S(1)}, u32[]{:S(2)}, u32[]{:S(2)}) %all-to-all-start.7) | async-done | bytes 2097184 | tf_op jit(solution)/shard_map/all_to_all | solution.py:589
  553.6 2.9 shard_map.223
  557.2 2.8 convert_element_type.298
  (300 shorter events, 137.6 us)
Async XLA Ops:
  7.2 139.2 %all-gather.3.cloned.1.call-start = ((), (), s32[]{:S(2)}) async-start(), calls=%async_computation.12 | async-start | bytes 5242880 | tf_op jit(solution)/shard_map/all_gather | solution.py:410
  7.2 33.3 %collective-permute-start.2 = (bf16[64,2048]{1,0:T(8,128)(2,1)}, bf16[64,2048]{1,0:T(8,128)(2,1)}, u32[]{:S(2)}, u32[]{:S(2)}) collective-permute-start(bf16[64,2048]{1,0:T(8,128)(2,1)} %param.22), channel_id=1, source_target_pairs={{0,3},{1,2},{2,1},{3,0},{4,7},{5,6},{6,5},{7,4},{8,11},{9,10},{10,... | collective-permute-start | bytes 786440 | tf_op jit(solution)/shard_map/ppermute | solution.py:289
  12.3 23.0 %collective-permute-start.1 = (bf16[64,2048]{1,0:T(8,128)(2,1)}, bf16[64,2048]{1,0:T(8,128)(2,1)}, u32[]{:S(2)}, u32[]{:S(2)}) collective-permute-start(bf16[64,2048]{1,0:T(8,128)(2,1)} %param.22), channel_id=1, source_target_pairs={{0,2},{1,3},{2,0},{3,1},{4,6},{5,7},{6,4},{7,5},{8,10},{9,11},{10,... | collective-permute-start | bytes 786440 | tf_op jit(solution)/shard_map/ppermute | solution.py:289
  12.3 21.3 %collective-permute-start = (bf16[64,2048]{1,0:T(8,128)(2,1)}, bf16[64,2048]{1,0:T(8,128)(2,1)}, u32[]{:S(2)}, u32[]{:S(2)}) collective-permute-start(bf16[64,2048]{1,0:T(8,128)(2,1)} %param.22), channel_id=1, source_target_pairs={{0,1},{1,0},{2,3},{3,2},{4,5},{5,4},{6,7},{7,6},{8,9},{9,8},{10,11... | collective-permute-start | bytes 786440 | tf_op jit(solution)/shard_map/ppermute | solution.py:289
  17.9 19.1 %all-to-all-start = ((bf16[8,72,384]{2,1,0:T(8,128)(2,1)}), bf16[8,72,384]{2,1,0:T(8,128)(2,1)}, u32[]{:S(2)}, u32[]{:S(2)}) async-start(bf16[8,72,384]{2,1,0:T(8,128)(2,1)} %copy.90), calls=%async_computation | async-start | bytes 884736 | tf_op jit(solution)/shard_map/all_to_all | solution.py:394
  37.0 20.0 %collective-permute-start.8 = (bf16[128,2048]{1,0:T(8,128)(2,1)S(1)}, bf16[128,2048]{1,0:T(8,128)(2,1)S(1)}, u32[]{:S(2)}, u32[]{:S(2)}) collective-permute-start(bf16[128,2048]{1,0:T(8,128)(2,1)S(1)} %bitcast.195), channel_id=1, source_target_pairs={{0,24},{4,28},{8,16},{12,20},{16,8},{20,12},{24,0},{28,4},{1,25},{... | collective-permute-start | bytes 1572872 | tf_op jit(solution)/shard_map/ppermute | solution.py:289
  39.8 35.5 %collective-permute-start.7 = (bf16[128,2048]{1,0:T(8,128)(2,1)S(1)}, bf16[128,2048]{1,0:T(8,128)(2,1)S(1)}, u32[]{:S(2)}, u32[]{:S(2)}) collective-permute-start(bf16[128,2048]{1,0:T(8,128)(2,1)S(1)} %bitcast.196), channel_id=1, source_target_pairs={{0,16},{4,20},{8,24},{12,28},{16,0},{20,4},{24,8},{28,12},{1,17},{... | collective-permute-start | bytes 1572872 | tf_op jit(solution)/shard_map/ppermute | solution.py:289
  40.3 38.3 %collective-permute-start.6 = (bf16[128,2048]{1,0:T(8,128)(2,1)S(1)}, bf16[128,2048]{1,0:T(8,128)(2,1)S(1)}, u32[]{:S(2)}, u32[]{:S(2)}) collective-permute-start(bf16[128,2048]{1,0:T(8,128)(2,1)S(1)} %bitcast.197), channel_id=1, source_target_pairs={{0,8},{4,12},{8,0},{12,4},{16,24},{20,28},{24,16},{28,20},{1,9},{5... | collective-permute-start | bytes 1572872 | tf_op jit(solution)/shard_map/ppermute | solution.py:289
  42.2 39.5 %collective-permute-start.5 = (bf16[8,72,384]{2,1,0:T(8,128)(2,1)}, bf16[8,72,384]{2,1,0:T(8,128)(2,1)S(1)}, u32[]{:S(2)}, u32[]{:S(2)}) collective-permute-start(bf16[8,72,384]{2,1,0:T(8,128)(2,1)} %all-to-all-done), channel_id=1, source_target_pairs={{0,3},{1,2},{2,1},{3,0},{4,7},{5,6},{6,5},{7,4},{8,11},{9,10},{10,... | collective-permute-start | bytes 1327112 | tf_op jit(solution)/shard_map/ppermute | solution.py:289
  45.9 37.3 %collective-permute-start.4 = (bf16[8,72,384]{2,1,0:T(8,128)(2,1)}, bf16[8,72,384]{2,1,0:T(8,128)(2,1)S(1)}, u32[]{:S(2)}, u32[]{:S(2)}) collective-permute-start(bf16[8,72,384]{2,1,0:T(8,128)(2,1)} %all-to-all-done), channel_id=1, source_target_pairs={{0,2},{1,3},{2,0},{3,1},{4,6},{5,7},{6,4},{7,5},{8,10},{9,11},{10,... | collective-permute-start | bytes 1327112 | tf_op jit(solution)/shard_map/ppermute | solution.py:289
  57.0 27.1 %collective-permute-start.3 = (bf16[8,72,384]{2,1,0:T(8,128)(2,1)}, bf16[8,72,384]{2,1,0:T(8,128)(2,1)S(1)}, u32[]{:S(2)}, u32[]{:S(2)}) collective-permute-start(bf16[8,72,384]{2,1,0:T(8,128)(2,1)} %all-to-all-done), channel_id=1, source_target_pairs={{0,1},{1,0},{2,3},{3,2},{4,5},{5,4},{6,7},{7,6},{8,9},{9,8},{10,11... | collective-permute-start | bytes 1327112 | tf_op jit(solution)/shard_map/ppermute | solution.py:289
  80.1 20.3 %collective-permute-start.9 = (bf16[512,2048]{1,0:T(8,128)(2,1)}, bf16[512,2048]{1,0:T(8,128)(2,1)}, u32[]{:S(2)}, u32[]{:S(2)}) collective-permute-start(bf16[512,2048]{1,0:T(8,128)(2,1)} %pad_maximum_fusion.2), channel_id=1, source_target_pairs={{0,4},{4,0},{8,12},{12,8},{16,20},{20,16},{24,28},{28,24},{1,5},{5... | collective-permute-start | bytes 6291464 | tf_op jit(solution)/shard_map/ppermute | solution.py:289
  93.0 53.3 %all-to-all-start.2 = ((bf16[8,64,2048]{2,1,0:T(8,128)(2,1)}), bf16[8,64,2048]{2,1,0:T(8,128)(2,1)}, u32[]{:S(2)}, u32[]{:S(2)}) async-start(bf16[8,64,2048]{2,1,0:T(8,128)(2,1)} %reshape.277), calls=%async_computation.2 | async-start | bytes 4194304 | tf_op jit(solution)/shard_map/all_to_all | solution.py:407
  97.6 157.4 %all-gather.5.cloned.1.call-start = ((), (), s32[]{:S(2)}) async-start(), calls=%async_computation.13 | async-start | bytes 10485760 | tf_op jit(solution)/shard_map/all_gather | solution.py:455
  122.1 4.3 collective-permute-start.10
  129.8 16.6 %copy-start.10 = (bf16[1,128,2048]{2,1,0:T(8,128)(2,1)S(1)}, bf16[1,128,2048]{2,1,0:T(8,128)(2,1)}, u32[]{:S(2)}) copy-start(bf16[1,128,2048]{2,1,0:T(8,128)(2,1)} %param.15) | copy-start | bytes 1572868
  147.9 58.0 %all-to-all-start.3 = ((bf16[4,128,2048]{2,1,0:T(8,128)(2,1)}), bf16[4,128,2048]{2,1,0:T(8,128)(2,1)}, u32[]{:S(2)}, u32[]{:S(2)}) async-start(bf16[4,128,2048]{2,1,0:T(8,128)(2,1)} %broadcast_in_dim.101), calls=%async_computation.3 | async-start | bytes 4194304 | tf_op jit(solution)/shard_map/all_to_all | solution.py:327
  155.1 15.6 %collective-permute-start.16 = (bf16[64,2048]{1,0:T(8,128)(2,1)S(1)}, bf16[64,2048]{1,0:T(8,128)(2,1)S(1)}, u32[]{:S(2)}, u32[]{:S(2)}) collective-permute-start(bf16[64,2048]{1,0:T(8,128)(2,1)S(1)} %get-tuple-element.89), channel_id=1, source_target_pairs={{0,24},{4,28},{8,16},{12,20},{16,8},{20,12},{24,0},{28,4},{1,25},{... | collective-permute-start | bytes 786440 | tf_op jit(solution)/shard_map/ppermute | solution.py:289
  157.3 19.6 %collective-permute-start.15 = (bf16[64,2048]{1,0:T(8,128)(2,1)}, bf16[64,2048]{1,0:T(8,128)(2,1)}, u32[]{:S(2)}, u32[]{:S(2)}) collective-permute-start(bf16[64,2048]{1,0:T(8,128)(2,1)} %get-tuple-element.90), channel_id=1, source_target_pairs={{0,16},{4,20},{8,24},{12,28},{16,0},{20,4},{24,8},{28,12},{1,17},{... | collective-permute-start | bytes 786440 | tf_op jit(solution)/shard_map/ppermute | solution.py:289
  159.0 23.0 %collective-permute-start.14 = (bf16[64,2048]{1,0:T(8,128)(2,1)}, bf16[64,2048]{1,0:T(8,128)(2,1)}, u32[]{:S(2)}, u32[]{:S(2)}) collective-permute-start(bf16[64,2048]{1,0:T(8,128)(2,1)} %get-tuple-element.91), channel_id=1, source_target_pairs={{0,8},{4,12},{8,0},{12,4},{16,24},{20,28},{24,16},{28,20},{1,9},{5... | collective-permute-start | bytes 786440 | tf_op jit(solution)/shard_map/ppermute | solution.py:289
  159.0 34.3 %collective-permute-start.13 = (bf16[64,2048]{1,0:T(8,128)(2,1)}, bf16[64,2048]{1,0:T(8,128)(2,1)}, u32[]{:S(2)}, u32[]{:S(2)}) collective-permute-start(bf16[64,2048]{1,0:T(8,128)(2,1)} %get-tuple-element.92), channel_id=1, source_target_pairs={{0,24},{4,28},{8,16},{12,20},{16,8},{20,12},{24,0},{28,4},{1,25},{... | collective-permute-start | bytes 786440 | tf_op jit(solution)/shard_map/ppermute | solution.py:289
  160.8 32.8 %collective-permute-start.12 = (bf16[64,2048]{1,0:T(8,128)(2,1)S(1)}, bf16[64,2048]{1,0:T(8,128)(2,1)}, u32[]{:S(2)}, u32[]{:S(2)}) collective-permute-start(bf16[64,2048]{1,0:T(8,128)(2,1)S(1)} %get-tuple-element.93), channel_id=1, source_target_pairs={{0,16},{4,20},{8,24},{12,28},{16,0},{20,4},{24,8},{28,12},{1,17},{... | collective-permute-start | bytes 786440 | tf_op jit(solution)/shard_map/ppermute | solution.py:289
  171.4 30.3 %collective-permute-start.11 = (bf16[64,2048]{1,0:T(8,128)(2,1)S(1)}, bf16[64,2048]{1,0:T(8,128)(2,1)}, u32[]{:S(2)}, u32[]{:S(2)}) collective-permute-start(bf16[64,2048]{1,0:T(8,128)(2,1)S(1)} %get-tuple-element.94), channel_id=1, source_target_pairs={{0,8},{4,12},{8,0},{12,4},{16,24},{20,28},{24,16},{28,20},{1,9},{5... | collective-permute-start | bytes 786440 | tf_op jit(solution)/shard_map/ppermute | solution.py:289
  208.0 30.5 %all-to-all-start.1 = ((bf16[4,64,2048]{2,1,0:T(8,128)(2,1)}), bf16[4,64,2048]{2,1,0:T(8,128)(2,1)}, u32[]{:S(2)}, u32[]{:S(2)}) async-start(bf16[4,64,2048]{2,1,0:T(8,128)(2,1)} %broadcast_in_dim.100), calls=%async_computation.1 | async-start | bytes 2097152 | tf_op jit(solution)/shard_map/all_to_all | solution.py:327
  212.6 31.5 %collective-permute-start.18 = (bf16[2,4,64,2048]{3,2,0,1:T(8,128)(2,1)}, bf16[2,4,64,2048]{3,2,0,1:T(8,128)(2,1)}, u32[]{:S(2)}, u32[]{:S(2)}) collective-permute-start(bf16[2,4,64,2048]{3,2,0,1:T(8,128)(2,1)} %bitcast.40), channel_id=1, source_target_pairs={{0,4},{4,0},{8,12},{12,8},{16,20},{20,16},{24,28},{28,24},{1,5},{5... | collective-permute-start | bytes 6291464 | tf_op jit(solution)/shard_map/ppermute | solution.py:289
  238.5 9.4 %collective-permute-start.17 = (bf16[256,2048]{1,0:T(8,128)(2,1)}, bf16[256,2048]{1,0:T(8,128)(2,1)}, u32[]{:S(2)}, u32[]{:S(2)}) collective-permute-start(bf16[256,2048]{1,0:T(8,128)(2,1)} %bitcast.32), channel_id=1, source_target_pairs={{0,4},{4,0},{8,12},{12,8},{16,20},{20,16},{24,28},{28,24},{1,5},{5... | collective-permute-start | bytes 3145736 | tf_op jit(solution)/shard_map/ppermute | solution.py:289
  239.6 31.0 %all-to-all-start.4 = ((bf16[4,64,2048]{2,1,0:T(8,128)(2,1)}), bf16[4,64,2048]{2,1,0:T(8,128)(2,1)}, u32[]{:S(2)}, u32[]{:S(2)}) async-start(bf16[4,64,2048]{2,1,0:T(8,128)(2,1)} %broadcast_in_dim.102), calls=%async_computation.4 | async-start | bytes 2097152 | tf_op jit(solution)/shard_map/all_to_all | solution.py:327
  243.8 69.1 %reduce-scatter.5.cloned.1.call-start = ((), (), s32[]{:S(2)}) async-start(), calls=%async_computation.14 | async-start | bytes 1310720 | tf_op jit(solution)/shard_map/reduce_scatter | solution.py:503
  270.5 8.9 %copy-start.25 = (bf16[512,2048]{1,0:T(8,128)(2,1)S(1)}, bf16[512,2048]{1,0:T(8,128)(2,1)}, u32[]{:S(2)}) copy-start(bf16[512,2048]{1,0:T(8,128)(2,1)} %pad_maximum_fusion.4) | copy-start | bytes 6291460
  276.8 2.7 collective-permute-start.19
  286.2 3.0 collective-permute-start.20
  286.4 54.6 %reduce-scatter.7.cloned.1.call-start = ((), (), s32[]{:S(2)}) async-start(), calls=%async_computation.15 | async-start | bytes 1310720 | tf_op jit(solution)/shard_map/reduce_scatter | solution.py:503
  286.9 10.2 %copy-start.26 = (bf16[1,2,4,64,2048]{4,3,0,2,1:T(8,128)(2,1)S(1)}, bf16[1,2,4,64,2048]{4,3,0,2,1:T(8,128)(2,1)}, u32[]{:S(2)}) copy-start(bf16[1,2,4,64,2048]{4,3,0,2,1:T(8,128)(2,1)} %get-tuple-element.83) | copy-start | bytes 6291460
  286.9 10.2 %copy-start.51 = (bf16[1024,2048]{1,0:T(8,128)(2,1)S(1)}, bf16[1024,2048]{1,0:T(8,128)(2,1)}, u32[]{:S(2)}) copy-start(bf16[1024,2048]{1,0:T(8,128)(2,1)} %all-gather.3.cloned.1.call-done) | copy-start | bytes 12582916
  289.2 12.0 %slice-start = ((s8[8388608]{0:T(1024)(128)(4,1)}), s8[4194304]{0:T(1024)(128)(4,1)S(1)}, s32[]{:S(2)}) async-start(s8[8388608]{0:T(1024)(128)(4,1)} %bitcast.224), calls=%async_computation.18 | async-start | bytes 8388608
  303.6 2.7 collective-permute-start.21
  312.9 142.4 %reduce-scatter.9.cloned.1.call-start = ((), (), s32[]{:S(2)}) async-start(), calls=%async_computation.16 | async-start | bytes 10485760 | tf_op jit(solution)/shard_map/reduce_scatter | solution.py:517
  317.9 12.8 %collective-permute-start.23 = (bf16[256,2048]{1,0:T(8,128)(2,1)}, bf16[256,2048]{1,0:T(8,128)(2,1)}, u32[]{:S(2)}, u32[]{:S(2)}) collective-permute-start(bf16[256,2048]{1,0:T(8,128)(2,1)} %convolution_convert_fusion.6), channel_id=1, source_target_pairs={{0,4},{4,0},{8,12},{12,8},{16,20},{20,16},{24,28},{28,24},{1,5},{5... | collective-permute-start | bytes 3145736 | tf_op jit(solution)/shard_map/ppermute | solution.py:289
  344.6 5.3 collective-permute-start.22
  355.8 27.2 %collective-permute-start.26 = (bf16[128,2048]{1,0:T(8,128)(2,1)}, bf16[128,2048]{1,0:T(8,128)(2,1)}, u32[]{:S(2)}, u32[]{:S(2)}) collective-permute-start(bf16[128,2048]{1,0:T(8,128)(2,1)} %fusion.88), channel_id=1, source_target_pairs={{0,24},{4,28},{8,16},{12,20},{16,8},{20,12},{24,0},{28,4},{1,25},{... | collective-permute-start | bytes 1572872 | tf_op jit(solution)/shard_map/ppermute | solution.py:289
  358.2 36.5 %collective-permute-start.25 = (bf16[128,2048]{1,0:T(8,128)(2,1)}, bf16[128,2048]{1,0:T(8,128)(2,1)}, u32[]{:S(2)}, u32[]{:S(2)}) collective-permute-start(bf16[128,2048]{1,0:T(8,128)(2,1)} %fusion.88), channel_id=1, source_target_pairs={{0,16},{4,20},{8,24},{12,28},{16,0},{20,4},{24,8},{28,12},{1,17},{... | collective-permute-start | bytes 1572872 | tf_op jit(solution)/shard_map/ppermute | solution.py:289
  358.8 46.6 %collective-permute-start.24 = (bf16[128,2048]{1,0:T(8,128)(2,1)}, bf16[128,2048]{1,0:T(8,128)(2,1)}, u32[]{:S(2)}, u32[]{:S(2)}) collective-permute-start(bf16[128,2048]{1,0:T(8,128)(2,1)} %fusion.88), channel_id=1, source_target_pairs={{0,8},{4,12},{8,0},{12,4},{16,24},{20,28},{24,16},{28,20},{1,9},{5... | collective-permute-start | bytes 1572872 | tf_op jit(solution)/shard_map/ppermute | solution.py:289
  359.3 54.8 %all-to-all-start.5 = ((bf16[4,128,2048]{2,1,0:T(8,128)(2,1)}), bf16[4,128,2048]{2,1,0:T(8,128)(2,1)}, u32[]{:S(2)}, u32[]{:S(2)}) async-start(bf16[4,128,2048]{2,1,0:T(8,128)(2,1)} %bitcast.202), calls=%async_computation.7 | async-start | bytes 4194304 | tf_op jit(solution)/shard_map/all_to_all | solution.py:331
  363.8 193.3 %reduce-scatter.11.cloned.1.call-start = ((), (), s32[]{:S(2)}) async-start(), calls=%async_computation.17 | async-start | bytes 5242880 | tf_op jit(solution)/shard_map/reduce_scatter | solution.py:583
  407.4 4.2 collective-permute-start.27
  418.6 19.7 %collective-permute-start.30 = (bf16[64,2048]{1,0:T(8,128)(2,1)S(1)}, bf16[64,2048]{1,0:T(8,128)(2,1)S(1)}, u32[]{:S(2)}, u32[]{:S(2)}) collective-permute-start(bf16[64,2048]{1,0:T(8,128)(2,1)S(1)} %get-tuple-element.95), channel_id=1, source_target_pairs={{0,3},{1,2},{2,1},{3,0},{4,7},{5,6},{6,5},{7,4},{8,11},{9,10},{10,... | collective-permute-start | bytes 786440 | tf_op jit(solution)/shard_map/ppermute | solution.py:289
  419.4 24.0 %collective-permute-start.29 = (bf16[64,2048]{1,0:T(8,128)(2,1)S(1)}, bf16[64,2048]{1,0:T(8,128)(2,1)S(1)}, u32[]{:S(2)}, u32[]{:S(2)}) collective-permute-start(bf16[64,2048]{1,0:T(8,128)(2,1)S(1)} %get-tuple-element.96), channel_id=1, source_target_pairs={{0,2},{1,3},{2,0},{3,1},{4,6},{5,7},{6,4},{7,5},{8,10},{9,11},{10,... | collective-permute-start | bytes 786440 | tf_op jit(solution)/shard_map/ppermute | solution.py:289
  419.9 23.5 %collective-permute-start.28 = (bf16[64,2048]{1,0:T(8,128)(2,1)S(1)}, bf16[64,2048]{1,0:T(8,128)(2,1)S(1)}, u32[]{:S(2)}, u32[]{:S(2)}) collective-permute-start(bf16[64,2048]{1,0:T(8,128)(2,1)S(1)} %get-tuple-element.97), channel_id=1, source_target_pairs={{0,1},{1,0},{2,3},{3,2},{4,5},{5,4},{6,7},{7,6},{8,9},{9,8},{10,11... | collective-permute-start | bytes 786440 | tf_op jit(solution)/shard_map/ppermute | solution.py:289
  425.5 25.7 %copy-start.9 = (bf16[1024,2048]{1,0:T(8,128)(2,1)S(1)}, bf16[1024,2048]{1,0:T(8,128)(2,1)}, u32[]{:S(2)}) copy-start(bf16[1024,2048]{1,0:T(8,128)(2,1)} %constant_dynamic-update-slice_fusion) | copy-start | bytes 12582916
  446.9 4.2 collective-permute-start.31
  455.4 42.0 %all-to-all-start.6 = ((bf16[4,8,64,384]{3,2,1,0:T(8,128)(2,1)}), bf16[4,8,64,384]{3,2,1,0:T(8,128)(2,1)}, u32[]{:S(2)}, u32[]{:S(2)}) async-start(bf16[4,8,64,384]{3,2,1,0:T(8,128)(2,1)} %bitcast.203), calls=%async_computation.8 | async-start | bytes 3145728 | tf_op jit(solution)/shard_map/all_to_all | solution.py:573
  470.9 35.1 %collective-permute-start.32 = (bf16[128,2048]{1,0:T(8,128)(2,1)}, bf16[128,2048]{1,0:T(8,128)(2,1)}, u32[]{:S(2)}, u32[]{:S(2)}) collective-permute-start(bf16[128,2048]{1,0:T(8,128)(2,1)} %get-tuple-element.85), channel_id=1, source_target_pairs={{0,8},{4,12},{8,0},{12,4},{16,24},{20,28},{24,16},{28,20},{1,9},{5... | collective-permute-start | bytes 1572872 | tf_op jit(solution)/shard_map/ppermute | solution.py:289
  472.0 38.3 %collective-permute-start.34 = (bf16[128,2048]{1,0:T(8,128)(2,1)}, bf16[128,2048]{1,0:T(8,128)(2,1)}, u32[]{:S(2)}, u32[]{:S(2)}) collective-permute-start(bf16[128,2048]{1,0:T(8,128)(2,1)} %get-tuple-element.86), channel_id=1, source_target_pairs={{0,24},{4,28},{8,16},{12,20},{16,8},{20,12},{24,0},{28,4},{1,25},{... | collective-permute-start | bytes 1572872 | tf_op jit(solution)/shard_map/ppermute | solution.py:289
  472.9 37.4 %collective-permute-start.33 = (bf16[128,2048]{1,0:T(8,128)(2,1)}, bf16[128,2048]{1,0:T(8,128)(2,1)}, u32[]{:S(2)}, u32[]{:S(2)}) collective-permute-start(bf16[128,2048]{1,0:T(8,128)(2,1)} %get-tuple-element.87), channel_id=1, source_target_pairs={{0,16},{4,20},{8,24},{12,28},{16,0},{20,4},{24,8},{28,12},{1,17},{... | collective-permute-start | bytes 1572872 | tf_op jit(solution)/shard_map/ppermute | solution.py:289
  499.9 52.5 %all-to-all-start.7 = ((bf16[8,64,2048]{2,1,0:T(8,128)(2,1)}), bf16[8,64,2048]{2,1,0:T(8,128)(2,1)S(1)}, u32[]{:S(2)}, u32[]{:S(2)}) async-start(bf16[8,64,2048]{2,1,0:T(8,128)(2,1)} %bitcast.210), calls=%async_computation.10 | async-start | bytes 4194304 | tf_op jit(solution)/shard_map/all_to_all | solution.py:589
  506.0 11.6 %copy-start.7 = (f32[64,2048]{1,0:T(8,128)S(1)}, f32[64,2048]{1,0:T(8,128)}, u32[]{:S(2)}) copy-start(f32[64,2048]{1,0:T(8,128)} %get-tuple-element.112) | copy-start | bytes 1572868
  506.0 11.6 %copy-start.12 = (bf16[1,128,2048]{2,1,0:T(8,128)(2,1)S(1)}, bf16[1,128,2048]{2,1,0:T(8,128)(2,1)}, u32[]{:S(2)}) copy-start(bf16[1,128,2048]{2,1,0:T(8,128)(2,1)} %param.15) | copy-start | bytes 1572868
  506.0 11.6 %copy-start.20 = (bf16[64,2048]{1,0:T(8,128)(2,1)S(1)}, bf16[64,2048]{1,0:T(8,128)(2,1)}, u32[]{:S(2)}) copy-start(bf16[64,2048]{1,0:T(8,128)(2,1)} %reduce-scatter.5.cloned.1.call-done) | copy-start | bytes 786436
  506.0 11.6 %copy-start.22 = (bf16[64,2048]{1,0:T(8,128)(2,1)S(1)}, bf16[64,2048]{1,0:T(8,128)(2,1)}, u32[]{:S(2)}) copy-start(bf16[64,2048]{1,0:T(8,128)(2,1)} %reduce-scatter.7.cloned.1.call-done) | copy-start | bytes 786436
  512.5 1.5 collective-permute-start.35
  514.0 7.8 %collective-permute-start.36 = (bf16[2,64,384]{2,1,0:T(8,128)(2,1)S(1)}, bf16[2,64,384]{2,1,0:T(8,128)(2,1)S(1)}, u32[]{:S(2)}, u32[]{:S(2)}) collective-permute-start(bf16[2,64,384]{2,1,0:T(8,128)(2,1)S(1)} %get-tuple-element.104), channel_id=1, source_target_pairs={{0,8},{4,12},{8,0},{12,4},{16,24},{20,28},{24,16},{28,20},{1,9},{5... | collective-permute-start | bytes 294920 | tf_op jit(solution)/shard_map/ppermute | solution.py:289
  514.6 8.0 %collective-permute-start.37 = (bf16[2,64,384]{2,1,0:T(8,128)(2,1)S(1)}, bf16[2,64,384]{2,1,0:T(8,128)(2,1)S(1)}, u32[]{:S(2)}, u32[]{:S(2)}) collective-permute-start(bf16[2,64,384]{2,1,0:T(8,128)(2,1)S(1)} %get-tuple-element.105), channel_id=1, source_target_pairs={{0,16},{4,20},{8,24},{12,28},{16,0},{20,4},{24,8},{28,12},{1,17},{... | collective-permute-start | bytes 294920 | tf_op jit(solution)/shard_map/ppermute | solution.py:289
  515.0 9.7 %collective-permute-start.38 = (bf16[2,64,384]{2,1,0:T(8,128)(2,1)S(1)}, bf16[2,64,384]{2,1,0:T(8,128)(2,1)S(1)}, u32[]{:S(2)}, u32[]{:S(2)}) collective-permute-start(bf16[2,64,384]{2,1,0:T(8,128)(2,1)S(1)} %get-tuple-element.106), channel_id=1, source_target_pairs={{0,24},{4,28},{8,16},{12,20},{16,8},{20,12},{24,0},{28,4},{1,25},{... | collective-permute-start | bytes 294920 | tf_op jit(solution)/shard_map/ppermute | solution.py:289
  527.0 25.3 %copy-start.1 = (bf16[64,8192]{1,0:T(8,128)(2,1)S(1)}, bf16[64,8192]{1,0:T(8,128)(2,1)}, u32[]{:S(2)}) copy-start(bf16[64,8192]{1,0:T(8,128)(2,1)} %up_weight.1) | copy-start | bytes 3145732
  (49 other events, 180.8 us)
Sparse Core Ops, SparseCore 0:
  13.1 73.7 all-gather.2
  146.5 108.5 all-gather.4
  286.5 26.3 reduce-scatter.4
  315.2 25.7 reduce-scatter.6
  343.9 107.5 reduce-scatter.8
  455.5 69.7 reduce-scatter.10

commit v4 on v3

--- a/solution.py
+++ b/solution.py
@@ -474,7 +474,8 @@
 
         half = narrow * piece
         first = grad_out_near.reshape(narrow, HALVES, piece, model).transpose(1, 0, 2, 3)
-        grad_out = jnp.stack([first, core_swap(first)], axis=1).reshape(HALVES, -1, model)
+        first_far = core_swap(first)
+        grad_out = jnp.stack([first, first_far], axis=1).reshape(HALVES, -1, model)
         normed_two, hidden, grad_pair, two_totals, two_parts, branch_totals = [], [], [], [], [], []
         near_half = [narrow_gather(normed_half[h]).reshape(-1, model) for h in range(HALVES)]
         for h in range(HALVES):
@@ -536,7 +537,8 @@
         layer_output = after_attention + jnp.sum(branch_parts.astype(F32), axis=0)
         down_term = mm(
             jnp.concatenate([after(hidden[0], middle_parts[0])] + hidden[1:], axis=0),
-            grad_out.reshape(-1, model), ((0,), (0,)),
+            jnp.stack([after(first, middle_parts[1]), first_far], axis=1).reshape(-1, model),
+            ((0,), (0,)),
         ).astype(BF16)
         middle_parts[0] = after(middle_parts[0], down_term)
         near_middle = lax.optimization_barrier(jnp.concatenate(middle_parts, axis=0))
@@ -553,10 +555,14 @@
         ).reshape(cols, -1)
         grad_lin = after(grad_lin, *out_sent)
 
+        lin_term = mm(normed_one, grad_lin, ((0,), (1,))).astype(BF16)
+        lin_term = lin_term.reshape(wide, narrow, rows, cols).transpose(1, 0, 2, 3)
+        late_lin = after(grad_lin, lin_term)
+
         def one_product(near):
-            return mm(grad_lin[:, near * own : (near + 1) * own], attention_weight, ((0,), (1,)))
-
-        one_total, one_swapped = near_total(one_product)
+            return mm(late_lin[:, near * own : (near + 1) * own], attention_weight, ((0,), (1,)))
+
+        one_total, _ = near_total(one_product)
         one_parts = scatter(one_total, outer_swap, outer)
         grad_one = add_up(one_parts)
         scaled_one, factor_one = normalize(residual)
@@ -566,11 +572,9 @@
             - scaled_one * jnp.mean(grad_scaled_one * scaled_one, axis=-1, keepdims=True)
         )
 
-        late_lin = after(grad_lin, one_swapped)
-        lin_term = mm(normed_one, late_lin, ((0,), (1,))).astype(BF16)
-        lin_term = lin_term.reshape(wide, narrow, rows, cols).transpose(1, 0, 2, 3)
         out_grad = add_up([after(out_split[0], lin_term)] + out_sent)
-        lin_sum = jnp.sum(lax.all_to_all(lin_term, "narrow", 0, 0, tiled=True).astype(F32), axis=0)
+        lin_near = after(lax.all_to_all(lin_term, "narrow", 0, 0, tiled=True), one_parts[0])
+        lin_sum = jnp.sum(lin_near.astype(F32), axis=0)
         lin_split = lin_sum.astype(BF16).reshape(outer, INNER, rows, cols)
         mine = pick(lin_split, core, 1)
         other = core_swap(pick(lin_split, 1 - core, 1))
@@ -581,15 +585,15 @@
         lin_parts = jnp.concatenate(lin_parts, axis=0)
         lin_grad = jnp.stack([pick(lin_parts, place ^ w) for w in range(wide)]).astype(F32)
         down_grad = lax.psum_scatter(
-            after(down_term, pair_sum, lin_term), "wide", scatter_dimension=0, tiled=True,
+            after(down_term, pair_sum, lin_sum, one_total), "wide", scatter_dimension=0, tiled=True,
             axis_index_groups=chip_groups,
         ).astype(F32)
 
-        pair_sum = after(pair_sum, lin_sum, one_parts[0]).reshape(near_size, rows, pair_cols)
+        pair_sum = after(pair_sum, lin_sum).reshape(near_size, rows, pair_cols)
         pair_grad = lax.all_to_all(pair_sum, both, 0, 0, axis_index_groups=near_groups, tiled=True)
         if down_rows % 128 == 0:
             gate_grad, up_grad, gain_sum = join_pair(
-                pair_grad, gate_weight, up_weight, outer, down_rows
+                pair_grad, after(gate_weight, down_grad), up_weight, outer, down_rows
             )
             gain_sum = gain_sum[:, 0]
         else:

time: 575 us -> 586 us (1.019)
  waiting for transfers between devices: 231 us -> 248 us
    all_to_all x1, waiting for transfers between devices: 18.6 us -> 0.01 us  [per_device(): lax.all_to_all(pair_sum, both, 0, 0, axis_index_groups=near_groups, tiled...]
    reduce_scatter x1, waiting for transfers between devices: 0.01 us -> 12 us  [per_device(): lax.psum_scatter(after(down_term, pair_sum, lin_sum, one_total), 'wide',...]
    ppermute x39, waiting for transfers between devices: 130 us -> 141 us  [exchange(): return lax.ppermute(value, axis, [(i, i ^ step) for i in range(size)])]
    all_to_all x1, waiting for transfers between devices: 23 us -> 33.1 us  [per_device(): lax.all_to_all(lin_term, 'narrow', 0, 0, tiled=True)]
    unnamed x135 -> x139, local copies, waits for them, and re-layouts: 17.4 us -> 14.2 us
  transfers between devices with their start and end apart: 53 -> 53, of which waited for: 33 -> 30; matrix products, arithmetic and copies ran while one was open for 34% -> 33% of each run, Pallas kernels for 5% -> 4%
where the time goes in v4:
time: 586 us; the launch traced here: 579 us
  waiting for transfers between devices  248 us (42%)
  matrix products  101 us (17%)
  starting transfers between devices  76.7 us (13%)
  local copies, waits for them, and re-layouts  60.3 us (10%)
  other arithmetic  49.7 us (8%)
  Pallas kernels  26.8 us (5%)
  between operations  15.7 us (3%)
    ppermute x39, waiting for transfers between devices, exchange(): return lax.ppermute(value, axis, [(i, i ^ step) for i in range(size)])  141 us
    dot_general x22, matrix products, mm(): lax.dot_general(left, right, (dims, ((), ())), preferred_element_type=F32)  101 us
    ppermute x39, starting transfers between devices, exchange(): return lax.ppermute(value, axis, [(i, i ^ step) for i in range(size)])  40.6 us
    all_to_all x1, waiting for transfers between devices, per_device(): lax.all_to_all(lin_term, 'narrow', 0, 0, tiled=True)  33.1 us
    all_to_all x3, waiting for transfers between devices, narrow_gather(): return lax.all_to_all(spread, 'narrow', 0, 0, tiled=True)  26.7 us
    all_to_all x1, waiting for transfers between devices, per_device(): lax.all_to_all(pair_weight, both, 0, 0, axis_index_groups=near_groups, ti...  16.6 us
    unnamed x139, local copies, waits for them, and re-layouts  14.2 us
    all_to_all x3, starting transfers between devices, narrow_gather(): return lax.all_to_all(spread, 'narrow', 0, 0, tiled=True)  13.3 us
  transfers between devices with their start and end apart: 53, of which 30 were waited for; matrix products, arithmetic and copies ran while one was open for 33% of the time, Pallas kernels for 4%

profile of v4, /device:TPU:0, one launch (start us, length us, event | category | flops | bytes accessed | tf_op | source)
XLA Modules:
  0.0 578.7 jit_solution(13371410387457169986)
XLA Ops:
  7.2 5.1 collective-permute-start.2
  17.9 4.1 all-to-all-start
  25.7 2.7 pad_maximum_fusion.4
  28.6 4.5 reshape.280
  37.0 2.8 collective-permute-start.8
  42.2 3.7 collective-permute-start.5
  49.2 7.8 %collective-permute-done.8 = bf16[128,2048]{1,0:T(8,128)(2,1)S(1)} collective-permute-done((bf16[128,2048]{1,0:T(8,128)(2,1)S(1)}, bf16[128,2048]{1,0:T(8,128)(2,1)S(1)}, u32[]{:S(2)}, u32[]{:S(2)}) %collective-permute-start.8) | collective-permute-done | bytes 524320 | tf_op jit(solution)/shard_map/ppermute | solution.py:289
  58.0 17.3 %collective-permute-done.7 = bf16[128,2048]{1,0:T(8,128)(2,1)S(1)} collective-permute-done((bf16[128,2048]{1,0:T(8,128)(2,1)S(1)}, bf16[128,2048]{1,0:T(8,128)(2,1)S(1)}, u32[]{:S(2)}, u32[]{:S(2)}) %collective-permute-start.7) | collective-permute-done | bytes 524320 | tf_op jit(solution)/shard_map/ppermute | solution.py:289
  75.4 3.3 collective-permute-done.6
  93.0 4.6 all-to-all-start.2
  100.4 3.3 constant_dynamic-update-slice_fusion
  103.7 3.2 fusion
  109.1 11.1 %shard_map.221 = (bf16[4,64,1024]{2,1,0:T(8,128)(2,1)S(1)}, bf16[4,64,1024]{2,1,0:T(8,128)(2,1)S(1)}, bf16[1,64,1024]{2,1,0:T(8,128)(2,1)S(1)}, bf16[1,64,1024]{2,1,0:T(8,128)(2,1)S(1)}, f32[4,1,1024]{2,1,0:T(1,128)S(1)}) custom-call(s32[1]{0:T(128)} %bitcast.1.place_ref, f32[6,64,1024]{2,1,0:T(8,128)S(1)} %fusion.17.lin_ref, ...), custom_call_target="tpu_custom_call" | custom-call | flops 262144 | bytes 393216 | tf_op jit(solution)/shard_map/pallas_call | solution.py:197
  122.7 3.8 collective-permute-done.10
  126.5 3.3 add_convert_fusion.1
  129.8 16.6 %all-to-all-done.2 = bf16[8,64,2048]{2,1,0:T(8,128)(2,1)} async-done(((bf16[8,64,2048]{2,1,0:T(8,128)(2,1)}), bf16[8,64,2048]{2,1,0:T(8,128)(2,1)}, u32[]{:S(2)}, u32[]{:S(2)}) %all-to-all-start.2) | async-done | bytes 2097184 | tf_op jit(solution)/shard_map/all_to_all | solution.py:407
  147.9 4.4 all-to-all-start.3
  152.4 2.7 slice_bitcast_fusion.13
  162.5 8.3 %collective-permute-done.16 = bf16[64,2048]{1,0:T(8,128)(2,1)S(1)} collective-permute-done((bf16[64,2048]{1,0:T(8,128)(2,1)S(1)}, bf16[64,2048]{1,0:T(8,128)(2,1)S(1)}, u32[]{:S(2)}, u32[]{:S(2)}) %collective-permute-start.16) | collective-permute-done | bytes 262176 | tf_op jit(solution)/shard_map/ppermute | solution.py:289
  177.0 5.0 collective-permute-done.14
  182.0 11.4 %collective-permute-done.13 = bf16[64,2048]{1,0:T(8,128)(2,1)} collective-permute-done((bf16[64,2048]{1,0:T(8,128)(2,1)}, bf16[64,2048]{1,0:T(8,128)(2,1)}, u32[]{:S(2)}, u32[]{:S(2)}) %collective-permute-start.13) | collective-permute-done | bytes 262176 | tf_op jit(solution)/shard_map/ppermute | solution.py:289
  193.7 8.1 %collective-permute-done.11 = bf16[64,2048]{1,0:T(8,128)(2,1)} collective-permute-done((bf16[64,2048]{1,0:T(8,128)(2,1)S(1)}, bf16[64,2048]{1,0:T(8,128)(2,1)}, u32[]{:S(2)}, u32[]{:S(2)}) %collective-permute-start.11) | collective-permute-done | bytes 262176 | tf_op jit(solution)/shard_map/ppermute | solution.py:289
  208.0 4.6 all-to-all-start.1
  212.6 25.9 %all-to-all-done.1 = bf16[4,64,2048]{2,1,0:T(8,128)(2,1)} async-done(((bf16[4,64,2048]{2,1,0:T(8,128)(2,1)}), bf16[4,64,2048]{2,1,0:T(8,128)(2,1)}, u32[]{:S(2)}, u32[]{:S(2)}) %all-to-all-start.1) | async-done | bytes 1048608 | tf_op jit(solution)/shard_map/all_to_all | solution.py:327
  239.6 4.2 all-to-all-start.4
  244.1 3.7 fusion.19
  247.9 7.2 %all-gather.5.cloned.1.call-done = bf16[2048,2048]{1,0:T(8,128)(2,1)} async-done(((bf16[512,2048]{1,0:T(8,128)(2,1)}), bf16[2048,2048]{1,0:T(8,128)(2,1)}) %all-gather.5.cloned.1.call-update) | async-done | bytes 8388624 | tf_op jit(solution)/shard_map/all_gather | solution.py:455
  255.1 7.7 %fusion.20 = f32[512,2048]{1,0:T(8,128)S(1)} fusion(bf16[2048,2048]{1,0:T(8,128)(2,1)} %all-gather.5.cloned.1.call-done, bf16[256,2048]{1,0:T(8,128)(2,1)} %collective-permute-done.17, bf16[256,2048]{1,0:T(8,128)(2,1)} %bitcast.32), kind=kOutput, calls=%fused_computation.42 | convolution fusion | flops 4299161600 | bytes 14680064 | tf_op jit(solution)/shard_map/dot_general | solution.py:48
  262.8 4.1 multiply_convert_fusion.4
  270.5 6.2 %convolution_convert_fusion.9 = bf16[256,2048]{1,0:T(8,128)(2,1)S(1)} fusion(bf16[2048,2048]{1,0:T(8,128)(2,1)} %all-gather.5.cloned.1.call-done, bf16[512,2048]{1,0:T(8,128)(2,1)} %pad_maximum_fusion.5), kind=kOutput, calls=%fused_computation.38 | convolution fusion | flops 2148007936 | bytes 10485760 | tf_op jit(solution)/shard_map/dot_general | solution.py:48
  276.8 2.6 collective-permute-done.19
  279.5 6.7 %add_convert_fusion.5 = bf16[256,2048]{1,0:T(8,128)(2,1)} fusion(bf16[256,2048]{1,0:T(8,128)(2,1)S(1)} %collective-permute-done.19, bf16[2048,2048]{1,0:T(8,128)(2,1)} %all-gather.5.cloned.1.call-done, bf16[512,2048]{1,0:T(8,128)(2,1)S(1)} %copy-done.24), kind=kOutput, calls=%fused_computation.67 | convolution fusion | flops 2149056512 | bytes 11534336 | tf_op jit(solution)/shard_map/dot_general | solution.py:48
  289.2 7.8 %fusion.24 = f32[512,2048]{1,0:T(8,128)S(1)} fusion(bf16[2048,2048]{1,0:T(8,128)(2,1)} %all-gather.5.cloned.1.call-done, bf16[256,2048]{1,0:T(8,128)(2,1)} %collective-permute-done.20, bf16[256,2048]{1,0:T(8,128)(2,1)} %bitcast.45), kind=kOutput, calls=%fused_computation.48 | convolution fusion | flops 4299161600 | bytes 14680064 | tf_op jit(solution)/shard_map/dot_general | solution.py:48
  297.1 4.1 multiply_convert_fusion.2
  306.4 3.4 add_convert_fusion.4
  309.7 3.2 reduce-scatter.5.cloned.1.call-done
  313.2 4.7 convolution_convert_fusion.6
  317.9 12.7 %convolution_convert_fusion = bf16[2048,2048]{1,0:T(8,128)(2,1)} fusion(bf16[256,2048]{1,0:T(8,128)(2,1)} %collective-permute-done.20, bf16[256,2048]{1,0:T(8,128)(2,1)} %bitcast.45, bf16[256,2048]{1,0:T(8,128)(2,1)} %collective-permute-done.17, bf16[256,2048]{1,0:T(8,128)(2,1)} %bitcast.32, bf16[512,1024]{1,0:T(8,128)(2,1)S(1)} %copy-done.59, ...), kind=kOutput, calls=%fused_computation.5 | convolution fusion | flops 8627683328 | bytes 16777216 | tf_op jit(solution)/shard_map/dot_general | solution.py:48
  330.7 4.9 add_convert_fusion.2
  335.6 5.4 reduce-scatter.7.cloned.1.call-done
  341.1 3.7 convolution_convert_fusion.7
  353.3 4.7 all-to-all-start.5
  358.0 13.6 %collective-permute-done.24 = bf16[128,2048]{1,0:T(8,128)(2,1)} collective-permute-done((bf16[128,2048]{1,0:T(8,128)(2,1)}, bf16[128,2048]{1,0:T(8,128)(2,1)}, u32[]{:S(2)}, u32[]{:S(2)}) %collective-permute-start.24) | collective-permute-done | bytes 524320 | tf_op jit(solution)/shard_map/ppermute | solution.py:289
  371.6 2.6 pad_maximum_fusion
  376.0 6.3 %convolution_convert_fusion.1 = bf16[1024,2048]{1,0:T(8,128)(2,1)} fusion(bf16[1024,2048]{1,0:T(8,128)(2,1)S(1)} %bitcast.208, bf16[512,1024]{1,0:T(8,128)(2,1)S(1)} %copy-done.55, bf16[512,1024]{1,0:T(8,128)(2,1)S(1)} %copy-done.54), kind=kOutput, calls=%fused_computation.29 | convolution fusion | flops 4301258752 | bytes 10485760 | tf_op jit(solution)/shard_map/dot_general | solution.py:48
  382.3 12.3 %collective-permute-done.26 = bf16[128,2048]{1,0:T(8,128)(2,1)} collective-permute-done((bf16[128,2048]{1,0:T(8,128)(2,1)}, bf16[128,2048]{1,0:T(8,128)(2,1)}, u32[]{:S(2)}, u32[]{:S(2)}) %collective-permute-start.26) | collective-permute-done | bytes 524320 | tf_op jit(solution)/shard_map/ppermute | solution.py:289
  396.4 4.1 collective-permute-done.27
  403.2 3.3 all-to-all-done.5
  406.5 3.6 convolution_convert_fusion.5
  412.6 2.7 collective-permute-start.28
  415.2 2.7 convolution_convert_fusion.10
  417.9 12.8 %shard_map.222 = bf16[6,64,1024]{2,1,0:T(8,128)(2,1)S(1)} custom-call(s32[1]{0:T(128)} %bitcast.1.place_ref, bf16[4,64,1024]{2,1,0:T(8,128)(2,1)S(1)} %bitcast.190, bf16[4,64,1024]{2,1,0:T(8,128)(2,1)S(1)} %get-tuple-element.60.query_ref, bf16[1,64,1024]{2,1,0:T(8,128)(2,1)S(1)} %get-tuple-element.61.key_ref, ...), custom_call_target="tpu_custom_call" | custom-call | flops 262144 | bytes 393216 | tf_op jit(solution)/shard_map/pallas_call | solution.py:226
  433.0 2.9 convolution_convert_fusion.4
  437.3 4.1 convolution_convert_fusion.3
  441.4 4.4 all-to-all-start.6
  445.9 4.7 add_convert_fusion
  450.6 33.1 %all-to-all-done.6 = bf16[4,8,64,384]{3,2,1,0:T(8,128)(2,1)} async-done(((bf16[4,8,64,384]{3,2,1,0:T(8,128)(2,1)}), bf16[4,8,64,384]{3,2,1,0:T(8,128)(2,1)}, u32[]{:S(2)}, u32[]{:S(2)}) %all-to-all-start.6) | async-done | bytes 1572896 | tf_op jit(solution)/shard_map/all_to_all | solution.py:576
  495.9 3.7 all-to-all-start.7
  505.2 12.8 %collective-permute-done.32 = bf16[128,2048]{1,0:T(8,128)(2,1)} collective-permute-done((bf16[128,2048]{1,0:T(8,128)(2,1)}, bf16[128,2048]{1,0:T(8,128)(2,1)}, u32[]{:S(2)}, u32[]{:S(2)}) %collective-permute-start.32) | collective-permute-done | bytes 524320 | tf_op jit(solution)/shard_map/ppermute | solution.py:289
  519.4 20.2 %collective-permute-done.34 = bf16[128,2048]{1,0:T(8,128)(2,1)} collective-permute-done((bf16[128,2048]{1,0:T(8,128)(2,1)}, bf16[128,2048]{1,0:T(8,128)(2,1)}, u32[]{:S(2)}, u32[]{:S(2)}) %collective-permute-start.34) | collective-permute-done | bytes 524320 | tf_op jit(solution)/shard_map/ppermute | solution.py:289
  541.6 3.0 fusion.47
  551.8 12.0 %reduce-scatter.11.cloned.1.call-done = bf16[256,2048]{1,0:T(8,128)(2,1)} async-done(((bf16[1024,2048]{1,0:T(8,128)(2,1)}), bf16[256,2048]{1,0:T(8,128)(2,1)}) %reduce-scatter.11.cloned.1.call-update) | async-done | bytes 1048592 | tf_op jit(solution)/shard_map/reduce_scatter | solution.py:587
  563.9 2.8 convert_element_type.297
  567.9 2.9 shard_map.223
  (304 shorter events, 127.7 us)
Async XLA Ops:
  7.2 139.1 %all-gather.3.cloned.1.call-start = ((), (), s32[]{:S(2)}) async-start(), calls=%async_computation.12 | async-start | bytes 5242880 | tf_op jit(solution)/shard_map/all_gather | solution.py:410
  7.2 33.3 %collective-permute-start.2 = (bf16[64,2048]{1,0:T(8,128)(2,1)}, bf16[64,2048]{1,0:T(8,128)(2,1)}, u32[]{:S(2)}, u32[]{:S(2)}) collective-permute-start(bf16[64,2048]{1,0:T(8,128)(2,1)} %param.22), channel_id=1, source_target_pairs={{0,3},{1,2},{2,1},{3,0},{4,7},{5,6},{6,5},{7,4},{8,11},{9,10},{10,... | collective-permute-start | bytes 786440 | tf_op jit(solution)/shard_map/ppermute | solution.py:289
  12.3 23.0 %collective-permute-start.1 = (bf16[64,2048]{1,0:T(8,128)(2,1)}, bf16[64,2048]{1,0:T(8,128)(2,1)}, u32[]{:S(2)}, u32[]{:S(2)}) collective-permute-start(bf16[64,2048]{1,0:T(8,128)(2,1)} %param.22), channel_id=1, source_target_pairs={{0,2},{1,3},{2,0},{3,1},{4,6},{5,7},{6,4},{7,5},{8,10},{9,11},{10,... | collective-permute-start | bytes 786440 | tf_op jit(solution)/shard_map/ppermute | solution.py:289
  12.3 21.3 %collective-permute-start = (bf16[64,2048]{1,0:T(8,128)(2,1)}, bf16[64,2048]{1,0:T(8,128)(2,1)}, u32[]{:S(2)}, u32[]{:S(2)}) collective-permute-start(bf16[64,2048]{1,0:T(8,128)(2,1)} %param.22), channel_id=1, source_target_pairs={{0,1},{1,0},{2,3},{3,2},{4,5},{5,4},{6,7},{7,6},{8,9},{9,8},{10,11... | collective-permute-start | bytes 786440 | tf_op jit(solution)/shard_map/ppermute | solution.py:289
  17.9 19.1 %all-to-all-start = ((bf16[8,72,384]{2,1,0:T(8,128)(2,1)}), bf16[8,72,384]{2,1,0:T(8,128)(2,1)}, u32[]{:S(2)}, u32[]{:S(2)}) async-start(bf16[8,72,384]{2,1,0:T(8,128)(2,1)} %copy.90), calls=%async_computation | async-start | bytes 884736 | tf_op jit(solution)/shard_map/all_to_all | solution.py:394
  37.0 20.0 %collective-permute-start.8 = (bf16[128,2048]{1,0:T(8,128)(2,1)S(1)}, bf16[128,2048]{1,0:T(8,128)(2,1)S(1)}, u32[]{:S(2)}, u32[]{:S(2)}) collective-permute-start(bf16[128,2048]{1,0:T(8,128)(2,1)S(1)} %bitcast.196), channel_id=1, source_target_pairs={{0,24},{4,28},{8,16},{12,20},{16,8},{20,12},{24,0},{28,4},{1,25},{... | collective-permute-start | bytes 1572872 | tf_op jit(solution)/shard_map/ppermute | solution.py:289
  39.8 35.5 %collective-permute-start.7 = (bf16[128,2048]{1,0:T(8,128)(2,1)S(1)}, bf16[128,2048]{1,0:T(8,128)(2,1)S(1)}, u32[]{:S(2)}, u32[]{:S(2)}) collective-permute-start(bf16[128,2048]{1,0:T(8,128)(2,1)S(1)} %bitcast.197), channel_id=1, source_target_pairs={{0,16},{4,20},{8,24},{12,28},{16,0},{20,4},{24,8},{28,12},{1,17},{... | collective-permute-start | bytes 1572872 | tf_op jit(solution)/shard_map/ppermute | solution.py:289
  40.4 38.3 %collective-permute-start.6 = (bf16[128,2048]{1,0:T(8,128)(2,1)S(1)}, bf16[128,2048]{1,0:T(8,128)(2,1)S(1)}, u32[]{:S(2)}, u32[]{:S(2)}) collective-permute-start(bf16[128,2048]{1,0:T(8,128)(2,1)S(1)} %bitcast.198), channel_id=1, source_target_pairs={{0,8},{4,12},{8,0},{12,4},{16,24},{20,28},{24,16},{28,20},{1,9},{5... | collective-permute-start | bytes 1572872 | tf_op jit(solution)/shard_map/ppermute | solution.py:289
  42.2 39.5 %collective-permute-start.5 = (bf16[8,72,384]{2,1,0:T(8,128)(2,1)}, bf16[8,72,384]{2,1,0:T(8,128)(2,1)S(1)}, u32[]{:S(2)}, u32[]{:S(2)}) collective-permute-start(bf16[8,72,384]{2,1,0:T(8,128)(2,1)} %all-to-all-done), channel_id=1, source_target_pairs={{0,3},{1,2},{2,1},{3,0},{4,7},{5,6},{6,5},{7,4},{8,11},{9,10},{10,... | collective-permute-start | bytes 1327112 | tf_op jit(solution)/shard_map/ppermute | solution.py:289
  45.9 37.3 %collective-permute-start.4 = (bf16[8,72,384]{2,1,0:T(8,128)(2,1)}, bf16[8,72,384]{2,1,0:T(8,128)(2,1)S(1)}, u32[]{:S(2)}, u32[]{:S(2)}) collective-permute-start(bf16[8,72,384]{2,1,0:T(8,128)(2,1)} %all-to-all-done), channel_id=1, source_target_pairs={{0,2},{1,3},{2,0},{3,1},{4,6},{5,7},{6,4},{7,5},{8,10},{9,11},{10,... | collective-permute-start | bytes 1327112 | tf_op jit(solution)/shard_map/ppermute | solution.py:289
  57.0 27.1 %collective-permute-start.3 = (bf16[8,72,384]{2,1,0:T(8,128)(2,1)}, bf16[8,72,384]{2,1,0:T(8,128)(2,1)S(1)}, u32[]{:S(2)}, u32[]{:S(2)}) collective-permute-start(bf16[8,72,384]{2,1,0:T(8,128)(2,1)} %all-to-all-done), channel_id=1, source_target_pairs={{0,1},{1,0},{2,3},{3,2},{4,5},{5,4},{6,7},{7,6},{8,9},{9,8},{10,11... | collective-permute-start | bytes 1327112 | tf_op jit(solution)/shard_map/ppermute | solution.py:289
  80.2 20.3 %collective-permute-start.9 = (bf16[512,2048]{1,0:T(8,128)(2,1)}, bf16[512,2048]{1,0:T(8,128)(2,1)}, u32[]{:S(2)}, u32[]{:S(2)}) collective-permute-start(bf16[512,2048]{1,0:T(8,128)(2,1)} %pad_maximum_fusion.3), channel_id=1, source_target_pairs={{0,4},{4,0},{8,12},{12,8},{16,20},{20,16},{24,28},{28,24},{1,5},{5... | collective-permute-start | bytes 6291464 | tf_op jit(solution)/shard_map/ppermute | solution.py:289
  93.0 53.3 %all-to-all-start.2 = ((bf16[8,64,2048]{2,1,0:T(8,128)(2,1)}), bf16[8,64,2048]{2,1,0:T(8,128)(2,1)}, u32[]{:S(2)}, u32[]{:S(2)}) async-start(bf16[8,64,2048]{2,1,0:T(8,128)(2,1)} %reshape.280), calls=%async_computation.2 | async-start | bytes 4194304 | tf_op jit(solution)/shard_map/all_to_all | solution.py:407
  97.6 157.4 %all-gather.5.cloned.1.call-start = ((), (), s32[]{:S(2)}) async-start(), calls=%async_computation.13 | async-start | bytes 10485760 | tf_op jit(solution)/shard_map/all_gather | solution.py:455
  122.1 4.4 collective-permute-start.10
  129.7 16.6 %copy-start.12 = (bf16[1,128,2048]{2,1,0:T(8,128)(2,1)S(1)}, bf16[1,128,2048]{2,1,0:T(8,128)(2,1)}, u32[]{:S(2)}) copy-start(bf16[1,128,2048]{2,1,0:T(8,128)(2,1)} %param.15) | copy-start | bytes 1572868
  147.9 58.0 %all-to-all-start.3 = ((bf16[4,128,2048]{2,1,0:T(8,128)(2,1)}), bf16[4,128,2048]{2,1,0:T(8,128)(2,1)}, u32[]{:S(2)}, u32[]{:S(2)}) async-start(bf16[4,128,2048]{2,1,0:T(8,128)(2,1)} %broadcast_in_dim.101), calls=%async_computation.3 | async-start | bytes 4194304 | tf_op jit(solution)/shard_map/all_to_all | solution.py:327
  155.1 15.6 %collective-permute-start.16 = (bf16[64,2048]{1,0:T(8,128)(2,1)S(1)}, bf16[64,2048]{1,0:T(8,128)(2,1)S(1)}, u32[]{:S(2)}, u32[]{:S(2)}) collective-permute-start(bf16[64,2048]{1,0:T(8,128)(2,1)S(1)} %get-tuple-element.95), channel_id=1, source_target_pairs={{0,24},{4,28},{8,16},{12,20},{16,8},{20,12},{24,0},{28,4},{1,25},{... | collective-permute-start | bytes 786440 | tf_op jit(solution)/shard_map/ppermute | solution.py:289
  157.3 19.6 %collective-permute-start.15 = (bf16[64,2048]{1,0:T(8,128)(2,1)}, bf16[64,2048]{1,0:T(8,128)(2,1)}, u32[]{:S(2)}, u32[]{:S(2)}) collective-permute-start(bf16[64,2048]{1,0:T(8,128)(2,1)} %get-tuple-element.96), channel_id=1, source_target_pairs={{0,16},{4,20},{8,24},{12,28},{16,0},{20,4},{24,8},{28,12},{1,17},{... | collective-permute-start | bytes 786440 | tf_op jit(solution)/shard_map/ppermute | solution.py:289
  159.0 23.0 %collective-permute-start.14 = (bf16[64,2048]{1,0:T(8,128)(2,1)}, bf16[64,2048]{1,0:T(8,128)(2,1)}, u32[]{:S(2)}, u32[]{:S(2)}) collective-permute-start(bf16[64,2048]{1,0:T(8,128)(2,1)} %get-tuple-element.97), channel_id=1, source_target_pairs={{0,8},{4,12},{8,0},{12,4},{16,24},{20,28},{24,16},{28,20},{1,9},{5... | collective-permute-start | bytes 786440 | tf_op jit(solution)/shard_map/ppermute | solution.py:289
  159.0 34.3 %collective-permute-start.13 = (bf16[64,2048]{1,0:T(8,128)(2,1)}, bf16[64,2048]{1,0:T(8,128)(2,1)}, u32[]{:S(2)}, u32[]{:S(2)}) collective-permute-start(bf16[64,2048]{1,0:T(8,128)(2,1)} %get-tuple-element.98), channel_id=1, source_target_pairs={{0,24},{4,28},{8,16},{12,20},{16,8},{20,12},{24,0},{28,4},{1,25},{... | collective-permute-start | bytes 786440 | tf_op jit(solution)/shard_map/ppermute | solution.py:289
  160.8 32.8 %collective-permute-start.12 = (bf16[64,2048]{1,0:T(8,128)(2,1)S(1)}, bf16[64,2048]{1,0:T(8,128)(2,1)}, u32[]{:S(2)}, u32[]{:S(2)}) collective-permute-start(bf16[64,2048]{1,0:T(8,128)(2,1)S(1)} %get-tuple-element.99), channel_id=1, source_target_pairs={{0,16},{4,20},{8,24},{12,28},{16,0},{20,4},{24,8},{28,12},{1,17},{... | collective-permute-start | bytes 786440 | tf_op jit(solution)/shard_map/ppermute | solution.py:289
  171.5 30.3 %collective-permute-start.11 = (bf16[64,2048]{1,0:T(8,128)(2,1)S(1)}, bf16[64,2048]{1,0:T(8,128)(2,1)}, u32[]{:S(2)}, u32[]{:S(2)}) collective-permute-start(bf16[64,2048]{1,0:T(8,128)(2,1)S(1)} %get-tuple-element.100), channel_id=1, source_target_pairs={{0,8},{4,12},{8,0},{12,4},{16,24},{20,28},{24,16},{28,20},{1,9},{5... | collective-permute-start | bytes 786440 | tf_op jit(solution)/shard_map/ppermute | solution.py:289
  208.0 30.5 %all-to-all-start.1 = ((bf16[4,64,2048]{2,1,0:T(8,128)(2,1)}), bf16[4,64,2048]{2,1,0:T(8,128)(2,1)}, u32[]{:S(2)}, u32[]{:S(2)}) async-start(bf16[4,64,2048]{2,1,0:T(8,128)(2,1)} %broadcast_in_dim.100), calls=%async_computation.1 | async-start | bytes 2097152 | tf_op jit(solution)/shard_map/all_to_all | solution.py:327
  212.6 31.5 %collective-permute-start.18 = (bf16[2,4,64,2048]{3,2,0,1:T(8,128)(2,1)}, bf16[2,4,64,2048]{3,2,0,1:T(8,128)(2,1)}, u32[]{:S(2)}, u32[]{:S(2)}) collective-permute-start(bf16[2,4,64,2048]{3,2,0,1:T(8,128)(2,1)} %bitcast.40), channel_id=1, source_target_pairs={{0,4},{4,0},{8,12},{12,8},{16,20},{20,16},{24,28},{28,24},{1,5},{5... | collective-permute-start | bytes 6291464 | tf_op jit(solution)/shard_map/ppermute | solution.py:289
  238.4 9.4 %collective-permute-start.17 = (bf16[256,2048]{1,0:T(8,128)(2,1)}, bf16[256,2048]{1,0:T(8,128)(2,1)}, u32[]{:S(2)}, u32[]{:S(2)}) collective-permute-start(bf16[256,2048]{1,0:T(8,128)(2,1)} %bitcast.32), channel_id=1, source_target_pairs={{0,4},{4,0},{8,12},{12,8},{16,20},{20,16},{24,28},{28,24},{1,5},{5... | collective-permute-start | bytes 3145736 | tf_op jit(solution)/shard_map/ppermute | solution.py:289
  239.6 31.0 %all-to-all-start.4 = ((bf16[4,64,2048]{2,1,0:T(8,128)(2,1)}), bf16[4,64,2048]{2,1,0:T(8,128)(2,1)}, u32[]{:S(2)}, u32[]{:S(2)}) async-start(bf16[4,64,2048]{2,1,0:T(8,128)(2,1)} %broadcast_in_dim.102), calls=%async_computation.4 | async-start | bytes 2097152 | tf_op jit(solution)/shard_map/all_to_all | solution.py:327
  243.8 69.1 %reduce-scatter.5.cloned.1.call-start = ((), (), s32[]{:S(2)}) async-start(), calls=%async_computation.14 | async-start | bytes 1310720 | tf_op jit(solution)/shard_map/reduce_scatter | solution.py:504
  276.8 2.7 collective-permute-start.19
  286.2 3.0 collective-permute-start.20
  286.4 54.6 %reduce-scatter.7.cloned.1.call-start = ((), (), s32[]{:S(2)}) async-start(), calls=%async_computation.15 | async-start | bytes 1310720 | tf_op jit(solution)/shard_map/reduce_scatter | solution.py:504
  286.9 10.2 %copy-start.25 = (bf16[1,2,4,64,2048]{4,3,0,2,1:T(8,128)(2,1)S(1)}, bf16[1,2,4,64,2048]{4,3,0,2,1:T(8,128)(2,1)}, u32[]{:S(2)}) copy-start(bf16[1,2,4,64,2048]{4,3,0,2,1:T(8,128)(2,1)} %get-tuple-element.89) | copy-start | bytes 6291460
  286.9 10.2 %copy-start.51 = (bf16[1024,2048]{1,0:T(8,128)(2,1)S(1)}, bf16[1024,2048]{1,0:T(8,128)(2,1)}, u32[]{:S(2)}) copy-start(bf16[1024,2048]{1,0:T(8,128)(2,1)} %all-gather.3.cloned.1.call-done) | copy-start | bytes 12582916
  289.2 12.0 %slice-start = ((s8[8388608]{0:T(1024)(128)(4,1)}), s8[4194304]{0:T(1024)(128)(4,1)S(1)}, s32[]{:S(2)}) async-start(s8[8388608]{0:T(1024)(128)(4,1)} %bitcast.224), calls=%async_computation.18 | async-start | bytes 8388608
  303.6 2.7 collective-permute-start.21
  312.9 173.3 %reduce-scatter.9.cloned.1.call-start = ((), (), s32[]{:S(2)}) async-start(), calls=%async_computation.16 | async-start | bytes 10485760 | tf_op jit(solution)/shard_map/reduce_scatter | solution.py:518
  317.9 12.8 %collective-permute-start.23 = (bf16[256,2048]{1,0:T(8,128)(2,1)}, bf16[256,2048]{1,0:T(8,128)(2,1)}, u32[]{:S(2)}, u32[]{:S(2)}) collective-permute-start(bf16[256,2048]{1,0:T(8,128)(2,1)} %convolution_convert_fusion.6), channel_id=1, source_target_pairs={{0,4},{4,0},{8,12},{12,8},{16,20},{20,16},{24,28},{28,24},{1,5},{5... | collective-permute-start | bytes 3145736 | tf_op jit(solution)/shard_map/ppermute | solution.py:289
  344.8 3.0 collective-permute-start.22
  346.4 25.2 %collective-permute-start.24 = (bf16[128,2048]{1,0:T(8,128)(2,1)}, bf16[128,2048]{1,0:T(8,128)(2,1)}, u32[]{:S(2)}, u32[]{:S(2)}) collective-permute-start(bf16[128,2048]{1,0:T(8,128)(2,1)} %fusion.87), channel_id=1, source_target_pairs={{0,8},{4,12},{8,0},{12,4},{16,24},{20,28},{24,16},{28,20},{1,9},{5... | collective-permute-start | bytes 1572872 | tf_op jit(solution)/shard_map/ppermute | solution.py:289
  350.7 43.9 %collective-permute-start.26 = (bf16[128,2048]{1,0:T(8,128)(2,1)}, bf16[128,2048]{1,0:T(8,128)(2,1)}, u32[]{:S(2)}, u32[]{:S(2)}) collective-permute-start(bf16[128,2048]{1,0:T(8,128)(2,1)} %fusion.87), channel_id=1, source_target_pairs={{0,24},{4,28},{8,16},{12,20},{16,8},{20,12},{24,0},{28,4},{1,25},{... | collective-permute-start | bytes 1572872 | tf_op jit(solution)/shard_map/ppermute | solution.py:289
  352.7 41.9 %collective-permute-start.25 = (bf16[128,2048]{1,0:T(8,128)(2,1)}, bf16[128,2048]{1,0:T(8,128)(2,1)}, u32[]{:S(2)}, u32[]{:S(2)}) collective-permute-start(bf16[128,2048]{1,0:T(8,128)(2,1)} %fusion.87), channel_id=1, source_target_pairs={{0,16},{4,20},{8,24},{12,28},{16,0},{20,4},{24,8},{28,12},{1,17},{... | collective-permute-start | bytes 1572872 | tf_op jit(solution)/shard_map/ppermute | solution.py:289
  353.3 53.2 %all-to-all-start.5 = ((bf16[4,128,2048]{2,1,0:T(8,128)(2,1)}), bf16[4,128,2048]{2,1,0:T(8,128)(2,1)}, u32[]{:S(2)}, u32[]{:S(2)}) async-start(bf16[4,128,2048]{2,1,0:T(8,128)(2,1)} %bitcast.203), calls=%async_computation.7 | async-start | bytes 4194304 | tf_op jit(solution)/shard_map/all_to_all | solution.py:331
  396.4 4.2 collective-permute-start.27
  410.9 19.9 %collective-permute-start.30 = (bf16[64,2048]{1,0:T(8,128)(2,1)S(1)}, bf16[64,2048]{1,0:T(8,128)(2,1)S(1)}, u32[]{:S(2)}, u32[]{:S(2)}) collective-permute-start(bf16[64,2048]{1,0:T(8,128)(2,1)S(1)} %get-tuple-element.101), channel_id=1, source_target_pairs={{0,3},{1,2},{2,1},{3,0},{4,7},{5,6},{6,5},{7,4},{8,11},{9,10},{10,... | collective-permute-start | bytes 786440 | tf_op jit(solution)/shard_map/ppermute | solution.py:289
  412.6 20.4 %collective-permute-start.29 = (bf16[64,2048]{1,0:T(8,128)(2,1)S(1)}, bf16[64,2048]{1,0:T(8,128)(2,1)S(1)}, u32[]{:S(2)}, u32[]{:S(2)}) collective-permute-start(bf16[64,2048]{1,0:T(8,128)(2,1)S(1)} %get-tuple-element.102), channel_id=1, source_target_pairs={{0,2},{1,3},{2,0},{3,1},{4,6},{5,7},{6,4},{7,5},{8,10},{9,11},{10,... | collective-permute-start | bytes 786440 | tf_op jit(solution)/shard_map/ppermute | solution.py:289
  412.6 20.4 %collective-permute-start.28 = (bf16[64,2048]{1,0:T(8,128)(2,1)S(1)}, bf16[64,2048]{1,0:T(8,128)(2,1)S(1)}, u32[]{:S(2)}, u32[]{:S(2)}) collective-permute-start(bf16[64,2048]{1,0:T(8,128)(2,1)S(1)} %get-tuple-element.103), channel_id=1, source_target_pairs={{0,1},{1,0},{2,3},{3,2},{4,5},{5,4},{6,7},{7,6},{8,9},{9,8},{10,11... | collective-permute-start | bytes 786440 | tf_op jit(solution)/shard_map/ppermute | solution.py:289
  415.2 17.8 %copy-start.11 = (bf16[1024,2048]{1,0:T(8,128)(2,1)S(1)}, bf16[1024,2048]{1,0:T(8,128)(2,1)}, u32[]{:S(2)}) copy-start(bf16[1024,2048]{1,0:T(8,128)(2,1)} %constant_dynamic-update-slice_fusion) | copy-start | bytes 12582916
  441.4 4.5 collective-permute-start.31
  441.4 42.3 %all-to-all-start.6 = ((bf16[4,8,64,384]{3,2,1,0:T(8,128)(2,1)}), bf16[4,8,64,384]{3,2,1,0:T(8,128)(2,1)}, u32[]{:S(2)}, u32[]{:S(2)}) async-start(bf16[4,8,64,384]{3,2,1,0:T(8,128)(2,1)} %bitcast.204), calls=%async_computation.8 | async-start | bytes 3145728 | tf_op jit(solution)/shard_map/all_to_all | solution.py:576
  445.7 118.1 %reduce-scatter.11.cloned.1.call-start = ((), (), s32[]{:S(2)}) async-start(), calls=%async_computation.17 | async-start | bytes 5242880 | tf_op jit(solution)/shard_map/reduce_scatter | solution.py:587
  491.6 26.3 %collective-permute-start.32 = (bf16[128,2048]{1,0:T(8,128)(2,1)}, bf16[128,2048]{1,0:T(8,128)(2,1)}, u32[]{:S(2)}, u32[]{:S(2)}) collective-permute-start(bf16[128,2048]{1,0:T(8,128)(2,1)} %get-tuple-element.91), channel_id=1, source_target_pairs={{0,8},{4,12},{8,0},{12,4},{16,24},{20,28},{24,16},{28,20},{1,9},{5... | collective-permute-start | bytes 1572872 | tf_op jit(solution)/shard_map/ppermute | solution.py:289
  492.6 47.0 %collective-permute-start.34 = (bf16[128,2048]{1,0:T(8,128)(2,1)}, bf16[128,2048]{1,0:T(8,128)(2,1)}, u32[]{:S(2)}, u32[]{:S(2)}) collective-permute-start(bf16[128,2048]{1,0:T(8,128)(2,1)} %get-tuple-element.92), channel_id=1, source_target_pairs={{0,24},{4,28},{8,16},{12,20},{16,8},{20,12},{24,0},{28,4},{1,25},{... | collective-permute-start | bytes 1572872 | tf_op jit(solution)/shard_map/ppermute | solution.py:289
  494.4 45.2 %collective-permute-start.33 = (bf16[128,2048]{1,0:T(8,128)(2,1)}, bf16[128,2048]{1,0:T(8,128)(2,1)}, u32[]{:S(2)}, u32[]{:S(2)}) collective-permute-start(bf16[128,2048]{1,0:T(8,128)(2,1)} %get-tuple-element.93), channel_id=1, source_target_pairs={{0,16},{4,20},{8,24},{12,28},{16,0},{20,4},{24,8},{28,12},{1,17},{... | collective-permute-start | bytes 1572872 | tf_op jit(solution)/shard_map/ppermute | solution.py:289
  495.9 6.0 %collective-permute-start.35 = (bf16[4,64,384]{2,1,0:T(8,128)(2,1)}, bf16[4,64,384]{2,1,0:T(8,128)(2,1)}, u32[]{:S(2)}, u32[]{:S(2)}) collective-permute-start(bf16[4,64,384]{2,1,0:T(8,128)(2,1)} %get-tuple-element.113), channel_id=1, source_target_pairs={{0,4},{4,0},{8,12},{12,8},{16,20},{20,16},{24,28},{28,24},{1,5},{5... | collective-permute-start | bytes 589832 | tf_op jit(solution)/shard_map/ppermute | solution.py:289
  495.9 70.8 %all-to-all-start.7 = ((bf16[8,64,2048]{2,1,0:T(8,128)(2,1)}), bf16[8,64,2048]{2,1,0:T(8,128)(2,1)S(1)}, u32[]{:S(2)}, u32[]{:S(2)}) async-start(bf16[8,64,2048]{2,1,0:T(8,128)(2,1)} %bitcast.211), calls=%async_computation.10 | async-start | bytes 4194304 | tf_op jit(solution)/shard_map/all_to_all | solution.py:593
  499.7 40.0 %copy-start.7 = (bf16[512,2048]{1,0:T(8,128)(2,1)S(1)}, bf16[512,2048]{1,0:T(8,128)(2,1)}, u32[]{:S(2)}) copy-start(bf16[512,2048]{1,0:T(8,128)(2,1)} %add_convert_fusion) | copy-start | bytes 6291460
  501.8 39.7 %copy-start.9 = (f32[64,2048]{1,0:T(8,128)S(1)}, f32[64,2048]{1,0:T(8,128)}, u32[]{:S(2)}) copy-start(f32[64,2048]{1,0:T(8,128)} %get-tuple-element.118) | copy-start | bytes 1572868
  501.8 39.7 %copy-start.14 = (bf16[1,128,2048]{2,1,0:T(8,128)(2,1)S(1)}, bf16[1,128,2048]{2,1,0:T(8,128)(2,1)}, u32[]{:S(2)}) copy-start(bf16[1,128,2048]{2,1,0:T(8,128)(2,1)} %param.15) | copy-start | bytes 1572868
  501.9 39.7 %copy-start.21 = (bf16[64,2048]{1,0:T(8,128)(2,1)S(1)}, bf16[64,2048]{1,0:T(8,128)(2,1)}, u32[]{:S(2)}) copy-start(bf16[64,2048]{1,0:T(8,128)(2,1)} %reduce-scatter.5.cloned.1.call-done) | copy-start | bytes 786436
  501.9 39.7 %copy-start.23 = (bf16[64,2048]{1,0:T(8,128)(2,1)S(1)}, bf16[64,2048]{1,0:T(8,128)(2,1)}, u32[]{:S(2)}) copy-start(bf16[64,2048]{1,0:T(8,128)(2,1)} %reduce-scatter.7.cloned.1.call-done) | copy-start | bytes 786436
  503.0 41.6 %collective-permute-start.36 = (bf16[2,64,384]{2,1,0:T(8,128)(2,1)S(1)}, bf16[2,64,384]{2,1,0:T(8,128)(2,1)S(1)}, u32[]{:S(2)}, u32[]{:S(2)}) collective-permute-start(bf16[2,64,384]{2,1,0:T(8,128)(2,1)S(1)} %get-tuple-element.110), channel_id=1, source_target_pairs={{0,8},{4,12},{8,0},{12,4},{16,24},{20,28},{24,16},{28,20},{1,9},{5... | collective-permute-start | bytes 294920 | tf_op jit(solution)/shard_map/ppermute | solution.py:289
  504.1 40.5 %collective-permute-start.37 = (bf16[2,64,384]{2,1,0:T(8,128)(2,1)S(1)}, bf16[2,64,384]{2,1,0:T(8,128)(2,1)S(1)}, u32[]{:S(2)}, u32[]{:S(2)}) collective-permute-start(bf16[2,64,384]{2,1,0:T(8,128)(2,1)S(1)} %get-tuple-element.111), channel_id=1, source_target_pairs={{0,16},{4,20},{8,24},{12,28},{16,0},{20,4},{24,8},{28,12},{1,17},{... | collective-permute-start | bytes 294920 | tf_op jit(solution)/shard_map/ppermute | solution.py:289
  517.9 26.7 %collective-permute-start.38 = (bf16[2,64,384]{2,1,0:T(8,128)(2,1)S(1)}, bf16[2,64,384]{2,1,0:T(8,128)(2,1)S(1)}, u32[]{:S(2)}, u32[]{:S(2)}) collective-permute-start(bf16[2,64,384]{2,1,0:T(8,128)(2,1)S(1)} %get-tuple-element.112), channel_id=1, source_target_pairs={{0,24},{4,28},{8,16},{12,20},{16,8},{20,12},{24,0},{28,4},{1,25},{... | collective-permute-start | bytes 294920 | tf_op jit(solution)/shard_map/ppermute | solution.py:289
  548.9 17.7 %copy-start.1 = (bf16[64,8192]{1,0:T(8,128)(2,1)S(1)}, bf16[64,8192]{1,0:T(8,128)(2,1)}, u32[]{:S(2)}) copy-start(bf16[64,8192]{1,0:T(8,128)(2,1)} %up_weight.1) | copy-start | bytes 3145732
  (51 other events, 201.2 us)
Sparse Core Ops, SparseCore 0:
  13.1 73.7 all-gather.2
  146.5 108.5 all-gather.4
  286.5 26.3 reduce-scatter.4
  315.1 25.7 reduce-scatter.6
  343.9 107.4 reduce-scatter.8
  486.4 77.4 reduce-scatter.10

commit v5 on v4

--- a/solution.py
+++ b/solution.py
@@ -585,7 +585,7 @@
         lin_parts = jnp.concatenate(lin_parts, axis=0)
         lin_grad = jnp.stack([pick(lin_parts, place ^ w) for w in range(wide)]).astype(F32)
         down_grad = lax.psum_scatter(
-            after(down_term, pair_sum, lin_sum, one_total), "wide", scatter_dimension=0, tiled=True,
+            after(down_term, pair_sum, one_parts[0]), "wide", scatter_dimension=0, tiled=True,
             axis_index_groups=chip_groups,
         ).astype(F32)
 

time: 586 us -> 560 us (0.956)
  waiting for transfers between devices: 248 us -> 238 us
  matrix products: 101 us -> 94.1 us
    ppermute x39, waiting for transfers between devices: 141 us -> 118 us  [exchange(): return lax.ppermute(value, axis, [(i, i ^ step) for i in range(size)])]
    all_to_all x1, waiting for transfers between devices: 0.01 us -> 11.3 us  [per_device(): lax.all_to_all(pair_sum, both, 0, 0, axis_index_groups=near_groups, tiled...]
    dot_general x22, matrix products: 101 us -> 94.1 us  [mm(): lax.dot_general(left, right, (dims, ((), ())), preferred_element_type=F32)]
    unnamed x139 -> x147, local copies, waits for them, and re-layouts: 14.2 us -> 14.6 us
  transfers between devices with their start and end apart: 53 -> 53, of which waited for: 30 -> 31; matrix products, arithmetic and copies ran while one was open for 33% -> 32% of each run, Pallas kernels for 4% -> 4%
where the time goes in v5:
time: 560 us; the launch traced here: 553 us
  waiting for transfers between devices  238 us (42%)
  matrix products  94.1 us (17%)
  starting transfers between devices  75.4 us (13%)
  local copies, waits for them, and re-layouts  55.7 us (10%)
  other arithmetic  47.8 us (9%)
  Pallas kernels  26.8 us (5%)
  between operations  15.7 us (3%)
    ppermute x39, waiting for transfers between devices, exchange(): return lax.ppermute(value, axis, [(i, i ^ step) for i in range(size)])  118 us
    dot_general x22, matrix products, mm(): lax.dot_general(left, right, (dims, ((), ())), preferred_element_type=F32)  94.1 us
    ppermute x39, starting transfers between devices, exchange(): return lax.ppermute(value, axis, [(i, i ^ step) for i in range(size)])  39.3 us
    all_to_all x1, waiting for transfers between devices, per_device(): lax.all_to_all(lin_term, 'narrow', 0, 0, tiled=True)  30.1 us
    all_to_all x3, waiting for transfers between devices, narrow_gather(): return lax.all_to_all(spread, 'narrow', 0, 0, tiled=True)  26.8 us
    all_to_all x1, waiting for transfers between devices, per_device(): lax.all_to_all(pair_weight, both, 0, 0, axis_index_groups=near_groups, ti...  19 us
    unnamed x147, local copies, waits for them, and re-layouts  14.6 us
    all_to_all x3, starting transfers between devices, narrow_gather(): return lax.all_to_all(spread, 'narrow', 0, 0, tiled=True)  13.3 us
  transfers between devices with their start and end apart: 53, of which 31 were waited for; matrix products, arithmetic and copies ran while one was open for 32% of the time, Pallas kernels for 4%

profile of v5, /device:TPU:0, one launch (start us, length us, event | category | flops | bytes accessed | tf_op | source)
XLA Modules:
  0.0 553.3 jit_solution(11873018175806694123)
XLA Ops:
  7.2 5.1 collective-permute-start.2
  17.9 4.1 all-to-all-start
  24.0 2.7 pad_maximum_fusion.4
  26.9 4.5 reshape.280
  39.5 3.4 collective-permute-start.5
  46.1 7.7 %collective-permute-done.8 = bf16[128,2048]{1,0:T(8,128)(2,1)S(1)} collective-permute-done((bf16[128,2048]{1,0:T(8,128)(2,1)S(1)}, bf16[128,2048]{1,0:T(8,128)(2,1)S(1)}, u32[]{:S(2)}, u32[]{:S(2)}) %collective-permute-start.8) | collective-permute-done | bytes 524320 | tf_op jit(solution)/shard_map/ppermute | solution.py:289
  55.4 9.1 %collective-permute-done.7 = bf16[128,2048]{1,0:T(8,128)(2,1)S(1)} collective-permute-done((bf16[128,2048]{1,0:T(8,128)(2,1)S(1)}, bf16[128,2048]{1,0:T(8,128)(2,1)S(1)}, u32[]{:S(2)}, u32[]{:S(2)}) %collective-permute-start.7) | collective-permute-done | bytes 524320 | tf_op jit(solution)/shard_map/ppermute | solution.py:289
  68.5 10.2 %collective-permute-done.4 = bf16[8,72,384]{2,1,0:T(8,128)(2,1)S(1)} collective-permute-done((bf16[8,72,384]{2,1,0:T(8,128)(2,1)}, bf16[8,72,384]{2,1,0:T(8,128)(2,1)S(1)}, u32[]{:S(2)}, u32[]{:S(2)}) %collective-permute-start.4) | collective-permute-done | bytes 442400 | tf_op jit(solution)/shard_map/ppermute | solution.py:289
  88.5 4.5 all-to-all-start.2
  95.8 3.3 constant_dynamic-update-slice_fusion
  99.0 3.2 fusion
  104.4 11.1 %shard_map.221 = (bf16[4,64,1024]{2,1,0:T(8,128)(2,1)S(1)}, bf16[4,64,1024]{2,1,0:T(8,128)(2,1)S(1)}, bf16[1,64,1024]{2,1,0:T(8,128)(2,1)S(1)}, bf16[1,64,1024]{2,1,0:T(8,128)(2,1)S(1)}, f32[4,1,1024]{2,1,0:T(1,128)S(1)}) custom-call(s32[1]{0:T(128)} %bitcast.1.place_ref, f32[6,64,1024]{2,1,0:T(8,128)S(1)} %fusion.17.lin_ref, ...), custom_call_target="tpu_custom_call" | custom-call | flops 262144 | bytes 393216 | tf_op jit(solution)/shard_map/pallas_call | solution.py:197
  116.7 3.8 collective-permute-done.10
  122.6 19.0 %all-to-all-done.2 = bf16[8,64,2048]{2,1,0:T(8,128)(2,1)} async-done(((bf16[8,64,2048]{2,1,0:T(8,128)(2,1)}), bf16[8,64,2048]{2,1,0:T(8,128)(2,1)}, u32[]{:S(2)}, u32[]{:S(2)}) %all-to-all-start.2) | async-done | bytes 2097184 | tf_op jit(solution)/shard_map/all_to_all | solution.py:407
  143.2 4.4 all-to-all-start.3
  147.6 2.8 slice_bitcast_fusion.13
  157.0 9.0 %collective-permute-done.16 = bf16[64,2048]{1,0:T(8,128)(2,1)S(1)} collective-permute-done((bf16[64,2048]{1,0:T(8,128)(2,1)S(1)}, bf16[64,2048]{1,0:T(8,128)(2,1)S(1)}, u32[]{:S(2)}, u32[]{:S(2)}) %collective-permute-start.16) | collective-permute-done | bytes 262176 | tf_op jit(solution)/shard_map/ppermute | solution.py:289
  169.5 2.8 collective-permute-done.15
  172.3 5.2 collective-permute-done.14
  177.5 11.0 %collective-permute-done.13 = bf16[64,2048]{1,0:T(8,128)(2,1)} collective-permute-done((bf16[64,2048]{1,0:T(8,128)(2,1)}, bf16[64,2048]{1,0:T(8,128)(2,1)}, u32[]{:S(2)}, u32[]{:S(2)}) %collective-permute-start.13) | collective-permute-done | bytes 262176 | tf_op jit(solution)/shard_map/ppermute | solution.py:289
  189.0 8.1 %collective-permute-done.11 = bf16[64,2048]{1,0:T(8,128)(2,1)} collective-permute-done((bf16[64,2048]{1,0:T(8,128)(2,1)S(1)}, bf16[64,2048]{1,0:T(8,128)(2,1)}, u32[]{:S(2)}, u32[]{:S(2)}) %collective-permute-start.11) | collective-permute-done | bytes 262176 | tf_op jit(solution)/shard_map/ppermute | solution.py:289
  203.4 4.6 all-to-all-start.1
  208.0 25.8 %all-to-all-done.1 = bf16[4,64,2048]{2,1,0:T(8,128)(2,1)} async-done(((bf16[4,64,2048]{2,1,0:T(8,128)(2,1)}), bf16[4,64,2048]{2,1,0:T(8,128)(2,1)}, u32[]{:S(2)}, u32[]{:S(2)}) %all-to-all-start.1) | async-done | bytes 1048608 | tf_op jit(solution)/shard_map/all_to_all | solution.py:327
  234.9 4.2 all-to-all-start.4
  239.5 3.7 fusion.19
  243.2 7.2 %all-gather.5.cloned.1.call-done = bf16[2048,2048]{1,0:T(8,128)(2,1)} async-done(((bf16[512,2048]{1,0:T(8,128)(2,1)}), bf16[2048,2048]{1,0:T(8,128)(2,1)}) %all-gather.5.cloned.1.call-update) | async-done | bytes 8388624 | tf_op jit(solution)/shard_map/all_gather | solution.py:455
  250.5 7.7 %fusion.20 = f32[512,2048]{1,0:T(8,128)S(1)} fusion(bf16[2048,2048]{1,0:T(8,128)(2,1)} %all-gather.5.cloned.1.call-done, bf16[256,2048]{1,0:T(8,128)(2,1)} %collective-permute-done.17, bf16[256,2048]{1,0:T(8,128)(2,1)} %bitcast.32), kind=kOutput, calls=%fused_computation.42 | convolution fusion | flops 4299161600 | bytes 14680064 | tf_op jit(solution)/shard_map/dot_general | solution.py:48
  258.1 4.1 multiply_convert_fusion.4
  265.9 6.2 %convolution_convert_fusion.9 = bf16[256,2048]{1,0:T(8,128)(2,1)S(1)} fusion(bf16[2048,2048]{1,0:T(8,128)(2,1)} %all-gather.5.cloned.1.call-done, bf16[512,2048]{1,0:T(8,128)(2,1)} %pad_maximum_fusion.5), kind=kOutput, calls=%fused_computation.38 | convolution fusion | flops 2148007936 | bytes 10485760 | tf_op jit(solution)/shard_map/dot_general | solution.py:48
  272.2 2.6 collective-permute-done.19
  274.9 6.7 %add_convert_fusion.5 = bf16[256,2048]{1,0:T(8,128)(2,1)} fusion(bf16[256,2048]{1,0:T(8,128)(2,1)S(1)} %collective-permute-done.19, bf16[2048,2048]{1,0:T(8,128)(2,1)} %all-gather.5.cloned.1.call-done, bf16[512,2048]{1,0:T(8,128)(2,1)S(1)} %copy-done.26), kind=kOutput, calls=%fused_computation.67 | convolution fusion | flops 2149056512 | bytes 11534336 | tf_op jit(solution)/shard_map/dot_general | solution.py:48
  284.6 7.8 %fusion.24 = f32[512,2048]{1,0:T(8,128)S(1)} fusion(bf16[2048,2048]{1,0:T(8,128)(2,1)} %all-gather.5.cloned.1.call-done, bf16[256,2048]{1,0:T(8,128)(2,1)} %collective-permute-done.20, bf16[256,2048]{1,0:T(8,128)(2,1)} %bitcast.45), kind=kOutput, calls=%fused_computation.48 | convolution fusion | flops 4299161600 | bytes 14680064 | tf_op jit(solution)/shard_map/dot_general | solution.py:48
  292.4 4.1 multiply_convert_fusion.2
  301.7 3.4 add_convert_fusion.4
  305.1 3.0 reduce-scatter.5.cloned.1.call-done
  308.4 4.7 convolution_convert_fusion.6
  313.2 12.7 %convolution_convert_fusion = bf16[2048,2048]{1,0:T(8,128)(2,1)} fusion(bf16[256,2048]{1,0:T(8,128)(2,1)} %collective-permute-done.20, bf16[256,2048]{1,0:T(8,128)(2,1)} %bitcast.45, bf16[256,2048]{1,0:T(8,128)(2,1)} %collective-permute-done.17, bf16[256,2048]{1,0:T(8,128)(2,1)} %bitcast.32, bf16[512,1024]{1,0:T(8,128)(2,1)S(1)} %copy-done.63, ...), kind=kOutput, calls=%fused_computation.5 | convolution fusion | flops 8627683328 | bytes 16777216 | tf_op jit(solution)/shard_map/dot_general | solution.py:48
  325.9 4.9 add_convert_fusion.2
  330.8 5.4 reduce-scatter.7.cloned.1.call-done
  336.3 3.7 convolution_convert_fusion.7
  348.5 4.5 all-to-all-start.5
  353.3 13.5 %collective-permute-done.24 = bf16[128,2048]{1,0:T(8,128)(2,1)} collective-permute-done((bf16[128,2048]{1,0:T(8,128)(2,1)}, bf16[128,2048]{1,0:T(8,128)(2,1)}, u32[]{:S(2)}, u32[]{:S(2)}) %collective-permute-start.24) | collective-permute-done | bytes 524320 | tf_op jit(solution)/shard_map/ppermute | solution.py:289
  366.8 2.6 pad_maximum_fusion
  371.2 6.3 %convolution_convert_fusion.1 = bf16[1024,2048]{1,0:T(8,128)(2,1)} fusion(bf16[1024,2048]{1,0:T(8,128)(2,1)S(1)} %bitcast.210, bf16[512,1024]{1,0:T(8,128)(2,1)S(1)} %copy-done.59, bf16[512,1024]{1,0:T(8,128)(2,1)S(1)} %copy-done.58), kind=kOutput, calls=%fused_computation.29 | convolution fusion | flops 4301258752 | bytes 10485760 | tf_op jit(solution)/shard_map/dot_general | solution.py:48
  377.5 12.3 %collective-permute-done.26 = bf16[128,2048]{1,0:T(8,128)(2,1)} collective-permute-done((bf16[128,2048]{1,0:T(8,128)(2,1)}, bf16[128,2048]{1,0:T(8,128)(2,1)}, u32[]{:S(2)}, u32[]{:S(2)}) %collective-permute-start.26) | collective-permute-done | bytes 524320 | tf_op jit(solution)/shard_map/ppermute | solution.py:289
  391.6 4.1 collective-permute-done.27
  398.4 3.1 all-to-all-done.5
  401.5 3.6 convolution_convert_fusion.5
  407.6 2.7 collective-permute-start.28
  411.6 12.8 %shard_map.222 = bf16[6,64,1024]{2,1,0:T(8,128)(2,1)S(1)} custom-call(s32[1]{0:T(128)} %bitcast.1.place_ref, bf16[4,64,1024]{2,1,0:T(8,128)(2,1)S(1)} %bitcast.190, bf16[4,64,1024]{2,1,0:T(8,128)(2,1)S(1)} %get-tuple-element.60.query_ref, bf16[1,64,1024]{2,1,0:T(8,128)(2,1)S(1)} %get-tuple-element.61.key_ref, ...), custom_call_target="tpu_custom_call" | custom-call | flops 262144 | bytes 393216 | tf_op jit(solution)/shard_map/pallas_call | solution.py:226
  424.4 3.7 collective-permute-done.29
  428.1 2.9 convolution_convert_fusion.4
  432.3 2.8 convolution_convert_fusion.3
  435.3 4.1 collective-permute-done.31
  439.4 2.7 add_convert_fusion
  446.6 4.6 all-to-all-start.6
  458.0 30.1 %all-to-all-done.6 = bf16[4,8,64,384]{3,2,1,0:T(8,128)(2,1)S(1)} async-done(((bf16[4,8,64,384]{3,2,1,0:T(8,128)(2,1)}), bf16[4,8,64,384]{3,2,1,0:T(8,128)(2,1)S(1)}, u32[]{:S(2)}, u32[]{:S(2)}) %all-to-all-start.6) | async-done | bytes 1572896 | tf_op jit(solution)/shard_map/all_to_all | solution.py:576
  489.2 3.6 all-to-all-start.7
  499.8 3.6 collective-permute-done.32
  505.3 3.0 fusion.47
  515.6 11.5 %reduce-scatter.11.cloned.1.call-done = bf16[256,2048]{1,0:T(8,128)(2,1)} async-done(((bf16[1024,2048]{1,0:T(8,128)(2,1)}), bf16[256,2048]{1,0:T(8,128)(2,1)}) %reduce-scatter.11.cloned.1.call-update) | async-done | bytes 1048592 | tf_op jit(solution)/shard_map/reduce_scatter | solution.py:587
  527.2 2.8 convert_element_type.297
  530.0 11.3 %all-to-all-done.7.gate_part.up_part = bf16[8,64,2048]{2,1,0:T(8,128)(2,1)S(1)} async-done(((bf16[8,64,2048]{2,1,0:T(8,128)(2,1)}), bf16[8,64,2048]{2,1,0:T(8,128)(2,1)S(1)}, u32[]{:S(2)}, u32[]{:S(2)}) %all-to-all-start.7) | async-done | bytes 2097184 | tf_op jit(solution)/shard_map/all_to_all | solution.py:593
  542.5 2.9 shard_map.223
  (312 shorter events, 124.6 us)
Async XLA Ops:
  7.2 134.4 %all-gather.3.cloned.1.call-start = ((), (), s32[]{:S(2)}) async-start(), calls=%async_computation.12 | async-start | bytes 5242880 | tf_op jit(solution)/shard_map/all_gather | solution.py:410
  7.2 32.3 %collective-permute-start.2 = (bf16[64,2048]{1,0:T(8,128)(2,1)}, bf16[64,2048]{1,0:T(8,128)(2,1)S(1)}, u32[]{:S(2)}, u32[]{:S(2)}) collective-permute-start(bf16[64,2048]{1,0:T(8,128)(2,1)} %param.22), channel_id=1, source_target_pairs={{0,3},{1,2},{2,1},{3,0},{4,7},{5,6},{6,5},{7,4},{8,11},{9,10},{10,... | collective-permute-start | bytes 786440 | tf_op jit(solution)/shard_map/ppermute | solution.py:289
  12.3 22.6 %collective-permute-start.1 = (bf16[64,2048]{1,0:T(8,128)(2,1)}, bf16[64,2048]{1,0:T(8,128)(2,1)}, u32[]{:S(2)}, u32[]{:S(2)}) collective-permute-start(bf16[64,2048]{1,0:T(8,128)(2,1)} %param.22), channel_id=1, source_target_pairs={{0,2},{1,3},{2,0},{3,1},{4,6},{5,7},{6,4},{7,5},{8,10},{9,11},{10,... | collective-permute-start | bytes 786440 | tf_op jit(solution)/shard_map/ppermute | solution.py:289
  12.3 19.6 %collective-permute-start = (bf16[64,2048]{1,0:T(8,128)(2,1)}, bf16[64,2048]{1,0:T(8,128)(2,1)}, u32[]{:S(2)}, u32[]{:S(2)}) collective-permute-start(bf16[64,2048]{1,0:T(8,128)(2,1)} %param.22), channel_id=1, source_target_pairs={{0,1},{1,0},{2,3},{3,2},{4,5},{5,4},{6,7},{7,6},{8,9},{9,8},{10,11... | collective-permute-start | bytes 786440 | tf_op jit(solution)/shard_map/ppermute | solution.py:289
  17.9 18.0 %all-to-all-start = ((bf16[8,72,384]{2,1,0:T(8,128)(2,1)}), bf16[8,72,384]{2,1,0:T(8,128)(2,1)}, u32[]{:S(2)}, u32[]{:S(2)}) async-start(bf16[8,72,384]{2,1,0:T(8,128)(2,1)} %copy.90), calls=%async_computation | async-start | bytes 884736 | tf_op jit(solution)/shard_map/all_to_all | solution.py:394
  36.0 17.8 %collective-permute-start.8 = (bf16[128,2048]{1,0:T(8,128)(2,1)S(1)}, bf16[128,2048]{1,0:T(8,128)(2,1)S(1)}, u32[]{:S(2)}, u32[]{:S(2)}) collective-permute-start(bf16[128,2048]{1,0:T(8,128)(2,1)S(1)} %bitcast.196), channel_id=1, source_target_pairs={{0,24},{4,28},{8,16},{12,20},{16,8},{20,12},{24,0},{28,4},{1,25},{... | collective-permute-start | bytes 1572872 | tf_op jit(solution)/shard_map/ppermute | solution.py:289
  38.5 26.0 %collective-permute-start.7 = (bf16[128,2048]{1,0:T(8,128)(2,1)S(1)}, bf16[128,2048]{1,0:T(8,128)(2,1)S(1)}, u32[]{:S(2)}, u32[]{:S(2)}) collective-permute-start(bf16[128,2048]{1,0:T(8,128)(2,1)S(1)} %bitcast.197), channel_id=1, source_target_pairs={{0,16},{4,20},{8,24},{12,28},{16,0},{20,4},{24,8},{28,12},{1,17},{... | collective-permute-start | bytes 1572872 | tf_op jit(solution)/shard_map/ppermute | solution.py:289
  39.0 25.5 %collective-permute-start.6 = (bf16[128,2048]{1,0:T(8,128)(2,1)S(1)}, bf16[128,2048]{1,0:T(8,128)(2,1)S(1)}, u32[]{:S(2)}, u32[]{:S(2)}) collective-permute-start(bf16[128,2048]{1,0:T(8,128)(2,1)S(1)} %bitcast.198), channel_id=1, source_target_pairs={{0,8},{4,12},{8,0},{12,4},{16,24},{20,28},{24,16},{28,20},{1,9},{5... | collective-permute-start | bytes 1572872 | tf_op jit(solution)/shard_map/ppermute | solution.py:289
  39.5 26.6 %copy-start.8 = (bf16[4,64,2048]{2,1,0:T(8,128)(2,1)}, bf16[4,64,2048]{2,1,0:T(8,128)(2,1)S(1)}, u32[]{:S(2)}) copy-start(bf16[4,64,2048]{2,1,0:T(8,128)(2,1)S(1)} %bitcast_dynamic-update-slice_fusion.1) | copy-start | bytes 3145732
  39.5 28.2 %collective-permute-start.5 = (bf16[8,72,384]{2,1,0:T(8,128)(2,1)}, bf16[8,72,384]{2,1,0:T(8,128)(2,1)S(1)}, u32[]{:S(2)}, u32[]{:S(2)}) collective-permute-start(bf16[8,72,384]{2,1,0:T(8,128)(2,1)} %all-to-all-done), channel_id=1, source_target_pairs={{0,3},{1,2},{2,1},{3,0},{4,7},{5,6},{6,5},{7,4},{8,11},{9,10},{10,... | collective-permute-start | bytes 1327112 | tf_op jit(solution)/shard_map/ppermute | solution.py:289
  42.9 35.8 %collective-permute-start.4 = (bf16[8,72,384]{2,1,0:T(8,128)(2,1)}, bf16[8,72,384]{2,1,0:T(8,128)(2,1)S(1)}, u32[]{:S(2)}, u32[]{:S(2)}) collective-permute-start(bf16[8,72,384]{2,1,0:T(8,128)(2,1)} %all-to-all-done), channel_id=1, source_target_pairs={{0,2},{1,3},{2,0},{3,1},{4,6},{5,7},{6,4},{7,5},{8,10},{9,11},{10,... | collective-permute-start | bytes 1327112 | tf_op jit(solution)/shard_map/ppermute | solution.py:289
  53.8 25.8 %collective-permute-start.3 = (bf16[8,72,384]{2,1,0:T(8,128)(2,1)}, bf16[8,72,384]{2,1,0:T(8,128)(2,1)S(1)}, u32[]{:S(2)}, u32[]{:S(2)}) collective-permute-start(bf16[8,72,384]{2,1,0:T(8,128)(2,1)} %all-to-all-done), channel_id=1, source_target_pairs={{0,1},{1,0},{2,3},{3,2},{4,5},{5,4},{6,7},{7,6},{8,9},{9,8},{10,11... | collective-permute-start | bytes 1327112 | tf_op jit(solution)/shard_map/ppermute | solution.py:289
  66.1 29.6 %collective-permute-start.9 = (bf16[512,2048]{1,0:T(8,128)(2,1)}, bf16[512,2048]{1,0:T(8,128)(2,1)}, u32[]{:S(2)}, u32[]{:S(2)}) collective-permute-start(bf16[512,2048]{1,0:T(8,128)(2,1)} %pad_maximum_fusion.3), channel_id=1, source_target_pairs={{0,4},{4,0},{8,12},{12,8},{16,20},{20,16},{24,28},{28,24},{1,5},{5... | collective-permute-start | bytes 6291464 | tf_op jit(solution)/shard_map/ppermute | solution.py:289
  88.5 53.1 %all-to-all-start.2 = ((bf16[8,64,2048]{2,1,0:T(8,128)(2,1)}), bf16[8,64,2048]{2,1,0:T(8,128)(2,1)}, u32[]{:S(2)}, u32[]{:S(2)}) async-start(bf16[8,64,2048]{2,1,0:T(8,128)(2,1)} %reshape.280), calls=%async_computation.2 | async-start | bytes 4194304 | tf_op jit(solution)/shard_map/all_to_all | solution.py:407
  93.0 157.5 %all-gather.5.cloned.1.call-start = ((), (), s32[]{:S(2)}) async-start(), calls=%async_computation.13 | async-start | bytes 10485760 | tf_op jit(solution)/shard_map/all_gather | solution.py:455
  104.4 11.1 %copy-start.9 = (bf16[4,64,2048]{2,1,0:T(8,128)(2,1)S(1)}, bf16[4,64,2048]{2,1,0:T(8,128)(2,1)}, u32[]{:S(2)}) copy-start(bf16[4,64,2048]{2,1,0:T(8,128)(2,1)} %copy-done.8) | copy-start | bytes 3145732
  116.3 4.2 collective-permute-start.10
  122.6 19.0 %copy-start.15 = (bf16[1,128,2048]{2,1,0:T(8,128)(2,1)S(1)}, bf16[1,128,2048]{2,1,0:T(8,128)(2,1)}, u32[]{:S(2)}) copy-start(bf16[1,128,2048]{2,1,0:T(8,128)(2,1)} %param.15) | copy-start | bytes 1572868
  143.2 58.2 %all-to-all-start.3 = ((bf16[4,128,2048]{2,1,0:T(8,128)(2,1)}), bf16[4,128,2048]{2,1,0:T(8,128)(2,1)}, u32[]{:S(2)}, u32[]{:S(2)}) async-start(bf16[4,128,2048]{2,1,0:T(8,128)(2,1)} %broadcast_in_dim.101), calls=%async_computation.3 | async-start | bytes 4194304 | tf_op jit(solution)/shard_map/all_to_all | solution.py:327
  150.4 15.6 %collective-permute-start.16 = (bf16[64,2048]{1,0:T(8,128)(2,1)S(1)}, bf16[64,2048]{1,0:T(8,128)(2,1)S(1)}, u32[]{:S(2)}, u32[]{:S(2)}) collective-permute-start(bf16[64,2048]{1,0:T(8,128)(2,1)S(1)} %get-tuple-element.96), channel_id=1, source_target_pairs={{0,24},{4,28},{8,16},{12,20},{16,8},{20,12},{24,0},{28,4},{1,25},{... | collective-permute-start | bytes 786440 | tf_op jit(solution)/shard_map/ppermute | solution.py:289
  152.9 19.4 %collective-permute-start.15 = (bf16[64,2048]{1,0:T(8,128)(2,1)}, bf16[64,2048]{1,0:T(8,128)(2,1)}, u32[]{:S(2)}, u32[]{:S(2)}) collective-permute-start(bf16[64,2048]{1,0:T(8,128)(2,1)} %get-tuple-element.97), channel_id=1, source_target_pairs={{0,16},{4,20},{8,24},{12,28},{16,0},{20,4},{24,8},{28,12},{1,17},{... | collective-permute-start | bytes 786440 | tf_op jit(solution)/shard_map/ppermute | solution.py:289
  153.5 24.1 %collective-permute-start.14 = (bf16[64,2048]{1,0:T(8,128)(2,1)}, bf16[64,2048]{1,0:T(8,128)(2,1)}, u32[]{:S(2)}, u32[]{:S(2)}) collective-permute-start(bf16[64,2048]{1,0:T(8,128)(2,1)} %get-tuple-element.98), channel_id=1, source_target_pairs={{0,8},{4,12},{8,0},{12,4},{16,24},{20,28},{24,16},{28,20},{1,9},{5... | collective-permute-start | bytes 786440 | tf_op jit(solution)/shard_map/ppermute | solution.py:289
  153.9 34.7 %collective-permute-start.13 = (bf16[64,2048]{1,0:T(8,128)(2,1)}, bf16[64,2048]{1,0:T(8,128)(2,1)}, u32[]{:S(2)}, u32[]{:S(2)}) collective-permute-start(bf16[64,2048]{1,0:T(8,128)(2,1)} %get-tuple-element.99), channel_id=1, source_target_pairs={{0,24},{4,28},{8,16},{12,20},{16,8},{20,12},{24,0},{28,4},{1,25},{... | collective-permute-start | bytes 786440 | tf_op jit(solution)/shard_map/ppermute | solution.py:289
  156.4 32.6 %collective-permute-start.12 = (bf16[64,2048]{1,0:T(8,128)(2,1)S(1)}, bf16[64,2048]{1,0:T(8,128)(2,1)}, u32[]{:S(2)}, u32[]{:S(2)}) collective-permute-start(bf16[64,2048]{1,0:T(8,128)(2,1)S(1)} %get-tuple-element.100), channel_id=1, source_target_pairs={{0,16},{4,20},{8,24},{12,28},{16,0},{20,4},{24,8},{28,12},{1,17},{... | collective-permute-start | bytes 786440 | tf_op jit(solution)/shard_map/ppermute | solution.py:289
  166.6 30.5 %collective-permute-start.11 = (bf16[64,2048]{1,0:T(8,128)(2,1)S(1)}, bf16[64,2048]{1,0:T(8,128)(2,1)}, u32[]{:S(2)}, u32[]{:S(2)}) collective-permute-start(bf16[64,2048]{1,0:T(8,128)(2,1)S(1)} %get-tuple-element.101), channel_id=1, source_target_pairs={{0,8},{4,12},{8,0},{12,4},{16,24},{20,28},{24,16},{28,20},{1,9},{5... | collective-permute-start | bytes 786440 | tf_op jit(solution)/shard_map/ppermute | solution.py:289
  203.4 30.4 %all-to-all-start.1 = ((bf16[4,64,2048]{2,1,0:T(8,128)(2,1)}), bf16[4,64,2048]{2,1,0:T(8,128)(2,1)}, u32[]{:S(2)}, u32[]{:S(2)}) async-start(bf16[4,64,2048]{2,1,0:T(8,128)(2,1)} %broadcast_in_dim.100), calls=%async_computation.1 | async-start | bytes 2097152 | tf_op jit(solution)/shard_map/all_to_all | solution.py:327
  208.0 31.5 %collective-permute-start.18 = (bf16[2,4,64,2048]{3,2,0,1:T(8,128)(2,1)}, bf16[2,4,64,2048]{3,2,0,1:T(8,128)(2,1)}, u32[]{:S(2)}, u32[]{:S(2)}) collective-permute-start(bf16[2,4,64,2048]{3,2,0,1:T(8,128)(2,1)} %bitcast.40), channel_id=1, source_target_pairs={{0,4},{4,0},{8,12},{12,8},{16,20},{20,16},{24,28},{28,24},{1,5},{5... | collective-permute-start | bytes 6291464 | tf_op jit(solution)/shard_map/ppermute | solution.py:289
  233.8 9.4 %collective-permute-start.17 = (bf16[256,2048]{1,0:T(8,128)(2,1)}, bf16[256,2048]{1,0:T(8,128)(2,1)}, u32[]{:S(2)}, u32[]{:S(2)}) collective-permute-start(bf16[256,2048]{1,0:T(8,128)(2,1)} %bitcast.32), channel_id=1, source_target_pairs={{0,4},{4,0},{8,12},{12,8},{16,20},{20,16},{24,28},{28,24},{1,5},{5... | collective-permute-start | bytes 3145736 | tf_op jit(solution)/shard_map/ppermute | solution.py:289
  234.9 31.0 %all-to-all-start.4 = ((bf16[4,64,2048]{2,1,0:T(8,128)(2,1)}), bf16[4,64,2048]{2,1,0:T(8,128)(2,1)}, u32[]{:S(2)}, u32[]{:S(2)}) async-start(bf16[4,64,2048]{2,1,0:T(8,128)(2,1)} %broadcast_in_dim.102), calls=%async_computation.4 | async-start | bytes 2097152 | tf_op jit(solution)/shard_map/all_to_all | solution.py:327
  239.2 69.0 %reduce-scatter.5.cloned.1.call-start = ((), (), s32[]{:S(2)}) async-start(), calls=%async_computation.14 | async-start | bytes 1310720 | tf_op jit(solution)/shard_map/reduce_scatter | solution.py:504
  272.1 2.7 collective-permute-start.19
  281.6 3.0 collective-permute-start.20
  281.7 54.5 %reduce-scatter.7.cloned.1.call-start = ((), (), s32[]{:S(2)}) async-start(), calls=%async_computation.15 | async-start | bytes 1310720 | tf_op jit(solution)/shard_map/reduce_scatter | solution.py:504
  282.2 10.2 %copy-start.27 = (bf16[1,2,4,64,2048]{4,3,0,2,1:T(8,128)(2,1)S(1)}, bf16[1,2,4,64,2048]{4,3,0,2,1:T(8,128)(2,1)}, u32[]{:S(2)}) copy-start(bf16[1,2,4,64,2048]{4,3,0,2,1:T(8,128)(2,1)} %get-tuple-element.89) | copy-start | bytes 6291460
  284.6 12.0 %slice-start = ((s8[8388608]{0:T(1024)(128)(4,1)}), s8[4194304]{0:T(1024)(128)(4,1)S(1)}, s32[]{:S(2)}) async-start(s8[8388608]{0:T(1024)(128)(4,1)} %bitcast.226), calls=%async_computation.18 | async-start | bytes 8388608
  299.0 2.7 collective-permute-start.21
  308.2 138.4 %reduce-scatter.9.cloned.1.call-start = ((), (), s32[]{:S(2)}) async-start(), calls=%async_computation.16 | async-start | bytes 10485760 | tf_op jit(solution)/shard_map/reduce_scatter | solution.py:518
  313.1 12.7 %collective-permute-start.23 = (bf16[256,2048]{1,0:T(8,128)(2,1)}, bf16[256,2048]{1,0:T(8,128)(2,1)}, u32[]{:S(2)}, u32[]{:S(2)}) collective-permute-start(bf16[256,2048]{1,0:T(8,128)(2,1)} %convolution_convert_fusion.6), channel_id=1, source_target_pairs={{0,4},{4,0},{8,12},{12,8},{16,20},{20,16},{24,28},{28,24},{1,5},{5... | collective-permute-start | bytes 3145736 | tf_op jit(solution)/shard_map/ppermute | solution.py:289
  340.0 3.0 collective-permute-start.22
  341.6 25.2 %collective-permute-start.24 = (bf16[128,2048]{1,0:T(8,128)(2,1)}, bf16[128,2048]{1,0:T(8,128)(2,1)}, u32[]{:S(2)}, u32[]{:S(2)}) collective-permute-start(bf16[128,2048]{1,0:T(8,128)(2,1)} %fusion.87), channel_id=1, source_target_pairs={{0,8},{4,12},{8,0},{12,4},{16,24},{20,28},{24,16},{28,20},{1,9},{5... | collective-permute-start | bytes 1572872 | tf_op jit(solution)/shard_map/ppermute | solution.py:289
  345.9 43.9 %collective-permute-start.26 = (bf16[128,2048]{1,0:T(8,128)(2,1)}, bf16[128,2048]{1,0:T(8,128)(2,1)}, u32[]{:S(2)}, u32[]{:S(2)}) collective-permute-start(bf16[128,2048]{1,0:T(8,128)(2,1)} %fusion.87), channel_id=1, source_target_pairs={{0,24},{4,28},{8,16},{12,20},{16,8},{20,12},{24,0},{28,4},{1,25},{... | collective-permute-start | bytes 1572872 | tf_op jit(solution)/shard_map/ppermute | solution.py:289
  347.9 41.8 %collective-permute-start.25 = (bf16[128,2048]{1,0:T(8,128)(2,1)}, bf16[128,2048]{1,0:T(8,128)(2,1)}, u32[]{:S(2)}, u32[]{:S(2)}) collective-permute-start(bf16[128,2048]{1,0:T(8,128)(2,1)} %fusion.87), channel_id=1, source_target_pairs={{0,16},{4,20},{8,24},{12,28},{16,0},{20,4},{24,8},{28,12},{1,17},{... | collective-permute-start | bytes 1572872 | tf_op jit(solution)/shard_map/ppermute | solution.py:289
  348.5 53.0 %all-to-all-start.5 = ((bf16[4,128,2048]{2,1,0:T(8,128)(2,1)}), bf16[4,128,2048]{2,1,0:T(8,128)(2,1)}, u32[]{:S(2)}, u32[]{:S(2)}) async-start(bf16[4,128,2048]{2,1,0:T(8,128)(2,1)} %bitcast.206), calls=%async_computation.7 | async-start | bytes 4194304 | tf_op jit(solution)/shard_map/all_to_all | solution.py:331
  353.0 174.1 %reduce-scatter.11.cloned.1.call-start = ((), (), s32[]{:S(2)}) async-start(), calls=%async_computation.17 | async-start | bytes 5242880 | tf_op jit(solution)/shard_map/reduce_scatter | solution.py:587
  391.6 4.2 collective-permute-start.27
  405.9 18.5 %collective-permute-start.30 = (bf16[64,2048]{1,0:T(8,128)(2,1)S(1)}, bf16[64,2048]{1,0:T(8,128)(2,1)S(1)}, u32[]{:S(2)}, u32[]{:S(2)}) collective-permute-start(bf16[64,2048]{1,0:T(8,128)(2,1)S(1)} %get-tuple-element.102), channel_id=1, source_target_pairs={{0,3},{1,2},{2,1},{3,0},{4,7},{5,6},{6,5},{7,4},{8,11},{9,10},{10,... | collective-permute-start | bytes 786440 | tf_op jit(solution)/shard_map/ppermute | solution.py:289
  407.6 20.5 %collective-permute-start.29 = (bf16[64,2048]{1,0:T(8,128)(2,1)S(1)}, bf16[64,2048]{1,0:T(8,128)(2,1)S(1)}, u32[]{:S(2)}, u32[]{:S(2)}) collective-permute-start(bf16[64,2048]{1,0:T(8,128)(2,1)S(1)} %get-tuple-element.103), channel_id=1, source_target_pairs={{0,2},{1,3},{2,0},{3,1},{4,6},{5,7},{6,4},{7,5},{8,10},{9,11},{10,... | collective-permute-start | bytes 786440 | tf_op jit(solution)/shard_map/ppermute | solution.py:289
  407.6 20.5 %collective-permute-start.28 = (bf16[64,2048]{1,0:T(8,128)(2,1)S(1)}, bf16[64,2048]{1,0:T(8,128)(2,1)S(1)}, u32[]{:S(2)}, u32[]{:S(2)}) collective-permute-start(bf16[64,2048]{1,0:T(8,128)(2,1)S(1)} %get-tuple-element.104), channel_id=1, source_target_pairs={{0,1},{1,0},{2,3},{3,2},{4,5},{5,4},{6,7},{7,6},{8,9},{9,8},{10,11... | collective-permute-start | bytes 786440 | tf_op jit(solution)/shard_map/ppermute | solution.py:289
  410.3 17.8 %copy-start.14 = (bf16[1024,2048]{1,0:T(8,128)(2,1)S(1)}, bf16[1024,2048]{1,0:T(8,128)(2,1)}, u32[]{:S(2)}) copy-start(bf16[1024,2048]{1,0:T(8,128)(2,1)} %constant_dynamic-update-slice_fusion) | copy-start | bytes 12582916
  435.2 4.2 collective-permute-start.31
  446.6 41.5 %all-to-all-start.6 = ((bf16[4,8,64,384]{3,2,1,0:T(8,128)(2,1)}), bf16[4,8,64,384]{3,2,1,0:T(8,128)(2,1)S(1)}, u32[]{:S(2)}, u32[]{:S(2)}) async-start(bf16[4,8,64,384]{3,2,1,0:T(8,128)(2,1)} %bitcast.184), calls=%async_computation.8 | async-start | bytes 3145728 | tf_op jit(solution)/shard_map/all_to_all | solution.py:576
  454.5 43.8 %collective-permute-start.34 = (bf16[128,2048]{1,0:T(8,128)(2,1)}, bf16[128,2048]{1,0:T(8,128)(2,1)}, u32[]{:S(2)}, u32[]{:S(2)}) collective-permute-start(bf16[128,2048]{1,0:T(8,128)(2,1)} %get-tuple-element.92), channel_id=1, source_target_pairs={{0,24},{4,28},{8,16},{12,20},{16,8},{20,12},{24,0},{28,4},{1,25},{... | collective-permute-start | bytes 1572872 | tf_op jit(solution)/shard_map/ppermute | solution.py:289
  456.0 43.8 %collective-permute-start.33 = (bf16[128,2048]{1,0:T(8,128)(2,1)}, bf16[128,2048]{1,0:T(8,128)(2,1)}, u32[]{:S(2)}, u32[]{:S(2)}) collective-permute-start(bf16[128,2048]{1,0:T(8,128)(2,1)} %get-tuple-element.93), channel_id=1, source_target_pairs={{0,16},{4,20},{8,24},{12,28},{16,0},{20,4},{24,8},{28,12},{1,17},{... | collective-permute-start | bytes 1572872 | tf_op jit(solution)/shard_map/ppermute | solution.py:289
  457.4 46.0 %collective-permute-start.32 = (bf16[128,2048]{1,0:T(8,128)(2,1)}, bf16[128,2048]{1,0:T(8,128)(2,1)}, u32[]{:S(2)}, u32[]{:S(2)}) collective-permute-start(bf16[128,2048]{1,0:T(8,128)(2,1)} %get-tuple-element.94), channel_id=1, source_target_pairs={{0,8},{4,12},{8,0},{12,4},{16,24},{20,28},{24,16},{28,20},{1,9},{5... | collective-permute-start | bytes 1572872 | tf_op jit(solution)/shard_map/ppermute | solution.py:289
  489.1 5.9 %collective-permute-start.35 = (bf16[4,64,384]{2,1,0:T(8,128)(2,1)}, bf16[4,64,384]{2,1,0:T(8,128)(2,1)}, u32[]{:S(2)}, u32[]{:S(2)}) collective-permute-start(bf16[4,64,384]{2,1,0:T(8,128)(2,1)} %get-tuple-element.114), channel_id=1, source_target_pairs={{0,4},{4,0},{8,12},{12,8},{16,20},{20,16},{24,28},{28,24},{1,5},{5... | collective-permute-start | bytes 589832 | tf_op jit(solution)/shard_map/ppermute | solution.py:289
  489.2 52.1 %all-to-all-start.7 = ((bf16[8,64,2048]{2,1,0:T(8,128)(2,1)}), bf16[8,64,2048]{2,1,0:T(8,128)(2,1)S(1)}, u32[]{:S(2)}, u32[]{:S(2)}) async-start(bf16[8,64,2048]{2,1,0:T(8,128)(2,1)} %bitcast.213), calls=%async_computation.10 | async-start | bytes 4194304 | tf_op jit(solution)/shard_map/all_to_all | solution.py:593
  492.8 10.6 %copy-start.7 = (bf16[512,2048]{1,0:T(8,128)(2,1)S(1)}, bf16[512,2048]{1,0:T(8,128)(2,1)}, u32[]{:S(2)}) copy-start(bf16[512,2048]{1,0:T(8,128)(2,1)} %copy-done.6) | copy-start | bytes 6291460
  495.0 10.3 %copy-start.12 = (f32[64,2048]{1,0:T(8,128)S(1)}, f32[64,2048]{1,0:T(8,128)}, u32[]{:S(2)}) copy-start(f32[64,2048]{1,0:T(8,128)} %get-tuple-element.119) | copy-start | bytes 1572868
  495.0 10.3 %copy-start.17 = (bf16[1,128,2048]{2,1,0:T(8,128)(2,1)S(1)}, bf16[1,128,2048]{2,1,0:T(8,128)(2,1)}, u32[]{:S(2)}) copy-start(bf16[1,128,2048]{2,1,0:T(8,128)(2,1)} %param.15) | copy-start | bytes 1572868
  495.0 10.3 %copy-start.25 = (bf16[64,2048]{1,0:T(8,128)(2,1)S(1)}, bf16[64,2048]{1,0:T(8,128)(2,1)}, u32[]{:S(2)}) copy-start(bf16[64,2048]{1,0:T(8,128)(2,1)} %reduce-scatter.7.cloned.1.call-done) | copy-start | bytes 786436
  496.2 12.1 %collective-permute-start.36 = (bf16[2,64,384]{2,1,0:T(8,128)(2,1)S(1)}, bf16[2,64,384]{2,1,0:T(8,128)(2,1)S(1)}, u32[]{:S(2)}, u32[]{:S(2)}) collective-permute-start(bf16[2,64,384]{2,1,0:T(8,128)(2,1)S(1)} %get-tuple-element.111), channel_id=1, source_target_pairs={{0,8},{4,12},{8,0},{12,4},{16,24},{20,28},{24,16},{28,20},{1,9},{5... | collective-permute-start | bytes 294920 | tf_op jit(solution)/shard_map/ppermute | solution.py:289
  497.6 10.7 %collective-permute-start.37 = (bf16[2,64,384]{2,1,0:T(8,128)(2,1)S(1)}, bf16[2,64,384]{2,1,0:T(8,128)(2,1)S(1)}, u32[]{:S(2)}, u32[]{:S(2)}) collective-permute-start(bf16[2,64,384]{2,1,0:T(8,128)(2,1)S(1)} %get-tuple-element.112), channel_id=1, source_target_pairs={{0,16},{4,20},{8,24},{12,28},{16,0},{20,4},{24,8},{28,12},{1,17},{... | collective-permute-start | bytes 294920 | tf_op jit(solution)/shard_map/ppermute | solution.py:289
  498.3 10.1 %collective-permute-start.38 = (bf16[2,64,384]{2,1,0:T(8,128)(2,1)S(1)}, bf16[2,64,384]{2,1,0:T(8,128)(2,1)S(1)}, u32[]{:S(2)}, u32[]{:S(2)}) collective-permute-start(bf16[2,64,384]{2,1,0:T(8,128)(2,1)S(1)} %get-tuple-element.113), channel_id=1, source_target_pairs={{0,24},{4,28},{8,16},{12,20},{16,8},{20,12},{24,0},{28,4},{1,25},{... | collective-permute-start | bytes 294920 | tf_op jit(solution)/shard_map/ppermute | solution.py:289
  512.7 28.5 %copy-start.1 = (bf16[64,8192]{1,0:T(8,128)(2,1)S(1)}, bf16[64,8192]{1,0:T(8,128)(2,1)}, u32[]{:S(2)}) copy-start(bf16[64,8192]{1,0:T(8,128)(2,1)} %up_weight.1) | copy-start | bytes 3145732
  (55 other events, 222.3 us)
Sparse Core Ops, SparseCore 0:
  13.1 73.2 all-gather.2
  141.7 108.7 all-gather.4
  281.8 26.2 reduce-scatter.4
  310.4 25.7 reduce-scatter.6
  339.1 107.4 reduce-scatter.8
  449.7 77.4 reduce-scatter.10
